TPU v7x, 128 devices: a whole 4x4x4 slice. The times are simulated.
128 devices in a mesh: dom: 32 (over y, x, z_lo), feat: 4 (over z_hi, core).
Axes of the slice: x: 4, y: 4, z: 4 (z_hi: 2, z_lo: 2; z = z_hi * 2 + z_lo), core: 2. Of those that a mesh axis runs over, the one named last changes fastest.
Arguments:
- features: bfloat16 [65536, 256], P('dom', 'feat'), may hold values from -6 to 6
- hub_feats: bfloat16 [4096, 256], P('dom', 'feat'), may hold values from -6 to 6
- hub_coef: bfloat16 [65536, 4096], P('dom'), may hold values from 0 to 0.024291992
- tile_coef: bfloat16 [3072, 128, 128], P('dom'), may hold values from 0 to 0.024291992
- tile_index: int32 [3072, 2], P('dom'), may hold values from 0 to 79, as said below
- boundary_rows: int32 [32, 32, 256], P('dom'), may hold values from -1 to 2047, as said below
- self_weight: bfloat16 [256, 256], P('feat'), may hold values from -0.375 to 0.375
- neigh_weight: bfloat16 [256, 256], P('feat'), may hold values from -0.375 to 0.375
- out_grad: bfloat16 [65536, 256], P('dom', 'feat'), may hold values from -6 to 6
Outputs:
- output_rows: bfloat16 [65536, 256], P('dom', 'feat')
- grad_feats: float32 [65536, 256], P('dom', 'feat')
- grad_hubs: float32 [4096, 256], P('dom', 'feat')
Inputs may be any that keep to these rules, and one draw needn't show every extreme that they name: `tile_index`: column 0 names a destination among the partition's 16 node tiles. Column 1 names a source tile: below 16 one of the partition's own tiles, else tile 16 + q * 2 + j is tile j of the rows received from partition q. Within each partition's 96 rows every received tile is a source exactly once. `boundary_rows`: entry [q, r, k] is a row among partition q's 2048 non-hub nodes whose features reader r needs, or -1 for an empty slot; the live entries of [q, r] come first and are distinct.
All inputs are finite; a program needn't handle non-finite values.
Results may differ from a plain program's by a relative error of at most 0.0037.
Values may be sent and summed in bfloat16 or wider, within the bound.
No kernel may reach another device: no remote copies, remote signals or barrier semaphores. Data moves between devices by JAX's collectives and lax.ppermute only.
A program may use at most 128 MiB of HBM per device.

v0:
```python
import jax
import jax.numpy as jnp
from jax import lax
from jax.sharding import PartitionSpec as P


def body(
    features,
    hub_feats,
    hub_coef,
    tile_coef,
    tile_index,
    boundary_rows,
    self_weight,
    neigh_weight,
    out_grad,
):
    node_count = features.shape[0]
    feat_width = features.shape[1]
    tile_rows = tile_coef.shape[1]
    node_tiles = node_count // tile_rows
    slot_table = boundary_rows[0]
    domain_count = slot_table.shape[0]
    slot_count = slot_table.shape[1]
    source_tiles = node_tiles + domain_count * slot_count // tile_rows
    outgoing = jnp.where(
        slot_table[..., None] >= 0,
        jnp.take(features, jnp.maximum(slot_table, 0), axis=0),
        jnp.zeros((), features.dtype),
    )
    incoming = lax.all_to_all(outgoing, "dom", split_axis=0, concat_axis=0, tiled=True)
    sources = jnp.concatenate([features, incoming.reshape(-1, feat_width)], 0).reshape(
        source_tiles, tile_rows, feat_width
    )
    picked = jnp.take(sources, tile_index[:, 1], axis=0)
    partial_products = jnp.einsum(
        "tab,tbd->tad", tile_coef, picked, preferred_element_type=jnp.float32
    )
    target_onehot = (
        tile_index[:, 0][None, :] == jnp.arange(node_tiles, dtype=jnp.int32)[:, None]
    ).astype(jnp.float32)
    tile_sum = jnp.einsum(
        "wk,kef->wef", target_onehot, partial_products, precision=lax.Precision.HIGHEST
    ).reshape(node_count, feat_width)
    hub_total_sum = jnp.dot(
        hub_coef,
        lax.all_gather(hub_feats, "dom", axis=0, tiled=True),
        preferred_element_type=jnp.float32,
    )
    aggregate = (tile_sum + hub_total_sum).astype(jnp.bfloat16)
    partial_sum = jnp.dot(features, self_weight, preferred_element_type=jnp.float32) + jnp.dot(
        aggregate, neigh_weight, preferred_element_type=jnp.float32
    )
    pre_act = lax.psum_scatter(partial_sum, "feat", scatter_dimension=1, tiled=True)
    output_rows = jax.nn.elu(pre_act).astype(jnp.bfloat16)
    slope = jnp.where(
        pre_act > 0, jnp.ones_like(pre_act), jnp.exp(jnp.minimum(pre_act, jnp.zeros_like(pre_act)))
    )
    grad_pre = (out_grad.astype(jnp.float32) * slope).astype(jnp.bfloat16)
    grad_full = lax.all_gather(grad_pre, "feat", axis=1, tiled=True)
    contract_last = (((1,), (1,)), ((), ()))
    self_back = lax.dot_general(
        grad_full, self_weight, contract_last, preferred_element_type=jnp.float32
    )
    grad_agg = lax.dot_general(
        grad_full, neigh_weight, contract_last, preferred_element_type=jnp.float32
    ).astype(jnp.bfloat16)
    target_rows = jnp.take(
        grad_agg.reshape(node_tiles, tile_rows, feat_width), tile_index[:, 0], axis=0
    )
    tile_terms = jnp.einsum(
        "tab,tad->tbd", tile_coef, target_rows, preferred_element_type=jnp.float32
    )
    source_hot = (
        tile_index[:, 1][None, :] == jnp.arange(source_tiles, dtype=jnp.int32)[:, None]
    ).astype(jnp.float32)
    source_grad = jnp.einsum("st,tbd->sbd", source_hot, tile_terms, precision=lax.Precision.HIGHEST)
    halo_back = source_grad[node_tiles:].reshape(domain_count, slot_count, feat_width)
    contract_first = (((0,), (0,)), ((), ()))
    hub_terms = lax.dot_general(
        hub_coef, grad_agg, contract_first, preferred_element_type=jnp.float32
    )
    hub_terms = hub_terms.reshape(domain_count, -1, feat_width)
    hub_arrived, returned_rows = (
        lax.all_to_all(hub_terms, "dom", split_axis=0, concat_axis=0, tiled=True),
        lax.all_to_all(halo_back, "dom", split_axis=0, concat_axis=0, tiled=True),
    )
    grad_hubs = jnp.sum(hub_arrived, 0)
    flat_index = jnp.where(slot_table >= 0, slot_table, node_count).reshape(-1)
    returned = (
        jnp.zeros((node_count + 1, feat_width), jnp.float32)
        .at[flat_index]
        .add(returned_rows.reshape(-1, feat_width))[:node_count]
    )
    grad_feats = self_back + source_grad[:node_tiles].reshape(node_count, feat_width) + returned
    return (output_rows, grad_feats, grad_hubs)


def solution(mesh):
    return jax.shard_map(
        body,
        mesh=mesh,
        in_specs=(
            P("dom", "feat"),
            P("dom", "feat"),
            P("dom", None),
            P("dom", None, None),
            P("dom", None),
            P("dom", None, None),
            P("feat", None),
            P("feat", None),
            P("dom", "feat"),
        ),
        out_specs=(P("dom", "feat"), P("dom", "feat"), P("dom", "feat")),
        check_vma=False,
    )
```

profile of v0, /device:TPU:0, one launch (start us, length us, event | category | flops | bytes accessed | tf_op | source)
XLA Modules:
  0.0 374.7 jit_solution(16052553559183952036)
XLA Ops:
  10.9 29.3 %gather_fusion = bf16[8192,64]{1,0:T(8,128)(2,1)} fusion(bf16[2048,64]{1,0:T(8,128)(2,1)} %copy.36, s32[8192]{0:T(1024)S(1)} %broadcast_clamp_fusion), kind=kCustom, calls=%fused_computation | custom fusion | bytes 2129920 | tf_op jit(solution)/shard_map/jit(_take)/gather | solution.py:28
  40.2 2.7 copy.37
  42.9 2.4 select_select_fusion
  45.3 8.9 %all-to-all-start = ((bf16[32,256,64]{1,2,0:T(8,128)(2,1)}), bf16[32,256,64]{1,2,0:T(8,128)(2,1)}, u32[]{:S(2)}, u32[]{:S(2)}) async-start(bf16[32,256,64]{1,2,0:T(8,128)(2,1)} %select_select_fusion), calls=%async_computation | async-start | bytes 2097152 | tf_op jit(solution)/shard_map/all_to_all | solution.py:31
  54.3 91.5 %all_gather.6 = bf16[4096,64]{0,1:T(8,128)(2,1)} all-gather(bf16[128,64]{0,1:T(8,128)(2,1)S(1)} %copy-done.8), channel_id=1, replica_groups=mesh['dom'=32,'feat'=4] {'dom'}, dimensions={0}, use_global_device_ids=true | all-gather | bytes 540672 | tf_op jit(solution)/shard_map/all_gather | solution.py:47
  150.4 3.3 gather_fusion.1
  153.6 3.6 convolution_bitcast_fusion.1
  157.3 3.7 fusion.2
  161.0 13.6 %convolution_add_fusion = f32[2048,256]{0,1:T(8,128)} fusion(f32[2048,256]{0,1:T(8,128)} %fusion.30, bf16[64,256]{1,0:T(8,128)(2,1)S(1)} %copy-done.6, bf16[2048,4096]{1,0:T(8,128)(2,1)} %param.11, bf16[4096,64]{0,1:T(8,128)(2,1)} %all_gather.6, f32[8,8,16,128]{3,2,1,0:T(8,128)} %bitcast.85), kind=kOutput, calls=%fused_computation.8 | convolution fusion | flops 1141637120 | bytes 22052864 | tf_op jit(solution)/shard_map/dot_general | solution.py:51
  174.8 36.2 %reduce-scatter.2.cloned.1.call-done = f32[2048,64]{0,1:T(8,128)} async-done(((f32[2048,256]{0,1:T(8,128)}), f32[2048,64]{0,1:T(8,128)}) %reduce-scatter.2.cloned.1.call-update) | async-done | bytes 524304 | tf_op jit(solution)/shard_map/reduce_scatter | solution.py:54
  213.1 20.3 %all-gather.2.cloned.1.call-done = bf16[2048,256]{0,1:T(8,128)(2,1)} async-done(((bf16[2048,64]{0,1:T(8,128)(2,1)}), bf16[2048,256]{0,1:T(8,128)(2,1)}) %all-gather.2.cloned.1.call-update) | async-done | bytes 1048592 | tf_op jit(solution)/shard_map/all_gather | solution.py:60
  235.0 8.9 %convolution_bitcast_fusion.2 = f32[8,32,8,128]{3,2,1,0:T(8,128)S(1)} fusion(bf16[2048,64]{0,1:T(8,128)(2,1)S(1)} %convolution_convert_fusion, bf16[2048,4096]{1,0:T(8,128)(2,1)} %param.11), kind=kOutput, calls=%fused_computation.20 | convolution fusion | flops 1073741824 | bytes 18087936 | tf_op jit(solution)/shard_map/dot_general | solution.py:80
  245.0 7.3 %all-to-all-start.2 = ((f32[32,128,64]{1,2,0:T(8,128)}), f32[32,128,64]{1,2,0:T(8,128)}, u32[]{:S(2)}, u32[]{:S(2)}) async-start(f32[32,128,64]{1,2,0:T(8,128)} %bitcast.83), calls=%async_computation.3 | async-start | bytes 2097152 | tf_op jit(solution)/shard_map/all_to_all | solution.py:85
  255.3 2.4 convolution_bitcast_fusion
  257.7 3.5 fusion
  264.3 2.9 reshape.106
  267.2 4.1 %copy.43 = f32[32,256,64]{1,2,0:T(8,128)} copy(f32[32,256,64]{1,0,2:T(8,128)} %reshape.106) | data formatting | bytes 4194304 | tf_op jit(solution)/shard_map/reshape | solution.py:78
  271.3 8.7 %all-to-all-start.1 = ((f32[32,256,64]{1,2,0:T(8,128)}), f32[32,256,64]{1,2,0:T(8,128)}, u32[]{:S(2)}, u32[]{:S(2)}) async-start(f32[32,256,64]{1,2,0:T(8,128)} %copy.43), calls=%async_computation.2 | async-start | bytes 4194304 | tf_op jit(solution)/shard_map/all_to_all | solution.py:86
  284.0 24.8 %all-to-all-done.1 = f32[32,256,64]{1,2,0:T(8,128)} async-done(((f32[32,256,64]{1,2,0:T(8,128)}), f32[32,256,64]{1,2,0:T(8,128)}, u32[]{:S(2)}, u32[]{:S(2)}) %all-to-all-start.1) | async-done | bytes 2097184 | tf_op jit(solution)/shard_map/all_to_all | solution.py:86
  308.8 3.8 %copy.48 = f32[32,256,64]{2,1,0:T(8,128)} copy(f32[32,256,64]{1,2,0:T(8,128)} %all-to-all-done.1) | data formatting | bytes 4194304 | tf_op jit(solution)/shard_map/reshape | solution.py:93
  312.6 48.0 %scatter_custom_fusion = f32[2049,64]{1,0:T(8,128)} fusion(s32[8192]{0:T(1024)S(1)} %bitcast.90, f32[8192,64]{1,0:T(8,128)} %bitcast.82, f32[]{:T(128)} %constant.42.clone.1), kind=kCustom, calls=%fused_computation.30 | custom fusion | flops 524288 | bytes 525056 | tf_op jit(solution)/shard_map/scatter-add | solution.py:93
  360.6 2.3 slice.30
  362.9 2.3 copy.50
  365.2 2.6 fusion.4
  (47 shorter events, 23.3 us)
Async XLA Ops:
  7.2 146.5 %copy-start = (bf16[96,128,128]{2,1,0:T(8,128)(2,1)S(1)}, bf16[96,128,128]{2,1,0:T(8,128)(2,1)}, u32[]{:S(2)}) copy-start(bf16[96,128,128]{2,1,0:T(8,128)(2,1)} %param.12) | copy-start | bytes 9437188
  42.9 11.4 %copy-start.9 = (s32[96,2]{0,1:T(2,128)S(1)}, s32[96,2]{0,1:T(2,128)}, u32[]{:S(2)}) copy-start(s32[96,2]{0,1:T(2,128)} %param.13) | copy-start | bytes 2308
  42.9 11.4 %copy-start.8 = (bf16[128,64]{0,1:T(8,128)(2,1)S(1)}, bf16[128,64]{0,1:T(8,128)(2,1)}, u32[]{:S(2)}) copy-start(bf16[128,64]{0,1:T(8,128)(2,1)} %param.10) | copy-start | bytes 49156
  42.9 103.0 %copy-start.3 = (bf16[2048,64]{0,1:T(8,128)(2,1)S(1)}, bf16[2048,64]{0,1:T(8,128)(2,1)}, u32[]{:S(2)}) copy-start(bf16[2048,64]{0,1:T(8,128)(2,1)} %param.9) | copy-start | bytes 786436
  42.9 103.0 %copy-start.7 = (bf16[64,256]{1,0:T(8,128)(2,1)S(1)}, bf16[64,256]{1,0:T(8,128)(2,1)}, u32[]{:S(2)}) copy-start(bf16[64,256]{1,0:T(8,128)(2,1)} %param.15) | copy-start | bytes 98308
  45.3 102.4 %all-to-all-start = ((bf16[32,256,64]{1,2,0:T(8,128)(2,1)}), bf16[32,256,64]{1,2,0:T(8,128)(2,1)}, u32[]{:S(2)}, u32[]{:S(2)}) async-start(bf16[32,256,64]{1,2,0:T(8,128)(2,1)} %select_select_fusion), calls=%async_computation | async-start | bytes 2097152 | tf_op jit(solution)/shard_map/all_to_all | solution.py:31
  54.2 156.8 %reduce-scatter.2.cloned.1.call-start = ((), (), s32[]{:S(2)}) async-start(), calls=%async_computation.4 | async-start | bytes 2621440 | tf_op jit(solution)/shard_map/reduce_scatter | solution.py:54
  157.3 3.7 copy-start.6
  161.0 50.0 %copy-start.5 = (bf16[2048,64]{0,1:T(8,128)(2,1)S(1)}, bf16[2048,64]{0,1:T(8,128)(2,1)}, u32[]{:S(2)}) copy-start(bf16[2048,64]{0,1:T(8,128)(2,1)} %param.17) | copy-start | bytes 786436
  174.6 58.9 %all-gather.2.cloned.1.call-start = ((), (), s32[]{:S(2)}) async-start(), calls=%async_computation.5 | async-start | bytes 1310720 | tf_op jit(solution)/shard_map/all_gather | solution.py:60
  235.0 8.9 %copy-start.2 = (bf16[2048,64]{0,1:T(8,128)(2,1)}, bf16[2048,64]{0,1:T(8,128)(2,1)S(1)}, u32[]{:S(2)}) copy-start(bf16[2048,64]{0,1:T(8,128)(2,1)S(1)} %convolution_convert_fusion) | copy-start | bytes 786436
  245.0 26.3 %all-to-all-start.2 = ((f32[32,128,64]{1,2,0:T(8,128)}), f32[32,128,64]{1,2,0:T(8,128)}, u32[]{:S(2)}, u32[]{:S(2)}) async-start(f32[32,128,64]{1,2,0:T(8,128)} %bitcast.83), calls=%async_computation.3 | async-start | bytes 2097152 | tf_op jit(solution)/shard_map/all_to_all | solution.py:85
  261.2 1.5 copy-start.1
  271.3 8.7 %copy-start.4 = (s32[1,32,256]{2,1,0:T(8,128)S(1)}, s32[1,32,256]{2,1,0:T(8,128)}, u32[]{:S(2)}) copy-start(s32[1,32,256]{2,1,0:T(8,128)} %param.14) | copy-start | bytes 98308
  271.3 37.4 %all-to-all-start.1 = ((f32[32,256,64]{1,2,0:T(8,128)}), f32[32,256,64]{1,2,0:T(8,128)}, u32[]{:S(2)}, u32[]{:S(2)}) async-start(f32[32,256,64]{1,2,0:T(8,128)} %copy.43), calls=%async_computation.2 | async-start | bytes 4194304 | tf_op jit(solution)/shard_map/all_to_all | solution.py:86
Sparse Core Ops, SparseCore 0:
  174.7 36.2 reduce-scatter.1
  213.3 20.1 all-gather.1
where the time goes:
time: 376 us; the launch traced here: 375 us
  blocking collectives  91.5 us (24%)
  waiting for transfers between devices  81.3 us (22%)
  local copies, waits for them, and re-layouts  63.1 us (17%)
  other arithmetic  57.7 us (15%)
  matrix products  41.6 us (11%)
  starting transfers between devices  25.2 us (7%)
  between operations  14.2 us (4%)
    all_gather x1, blocking collectives, body(): lax.all_gather(hub_feats, 'dom', axis=0, tiled=True)  91.5 us
    scatter-add x1, other arithmetic, body(): returned = jnp.zeros((node_count + 1, feat_width), jnp.float32).at[flat_i...  48 us
    reduce_scatter x1, waiting for transfers between devices, body(): lax.psum_scatter(partial_sum, 'feat', scatter_dimension=1, tiled=True)  36.2 us
    gather x2, local copies, waits for them, and re-layouts, body(): jnp.take(features, jnp.maximum(slot_table, 0), axis=0)  32 us
    all_to_all x1, waiting for transfers between devices, body(): lax.all_to_all(halo_back, 'dom', split_axis=0, concat_axis=0, tiled=True)  24.8 us
    all_gather x1, waiting for transfers between devices, body(): grad_full = lax.all_gather(grad_pre, 'feat', axis=1, tiled=True)  20.3 us
    dot_general x1, matrix products, body(): jnp.dot(aggregate, neigh_weight, preferred_element_type=jnp.float32)  13.6 us
    all_to_all x1, starting transfers between devices, body(): lax.all_to_all(outgoing, 'dom', split_axis=0, concat_axis=0, tiled=True)  8.89 us
  transfers between devices with their start and end apart: 5, of which 3 were waited for; matrix products, arithmetic and copies ran while one was open for 6% of the time, Pallas kernels for 0%

commit v1 on v0

v1 whole, which is shorter than its diff:
```python
import functools

import jax
import jax.numpy as jnp
from jax import lax
from jax.experimental import pallas as pl
from jax.experimental.pallas import tpu as pltpu
from jax.sharding import PartitionSpec as P

BF = jnp.bfloat16
F32 = jnp.float32
NT = (((1,), (1,)), ((), ()))
NN = (((1,), (0,)), ((), ()))
TN = (((0,), (0,)), ((), ()))

COLS = 64
NODES = 2048
DOM = 32
FEAT = 4
SLOTS = 256
TILE = 128
TILES = 96
OWN_TILES = NODES // TILE
RECV_TILES = DOM * SLOTS // TILE
QUARTER = NODES // FEAT
LOW = 256
HIGH = NODES // LOW
HUBS = 4096

VMEM = pl.BlockSpec(memory_space=pltpu.VMEM)
SMEM = pl.BlockSpec(memory_space=pltpu.SMEM)


def dot(a, b, dims):
    return lax.dot_general(a, b, dims, preferred_element_type=F32)


def params(mib=40):
    return pltpu.CompilerParams(vmem_limit_bytes=mib * 1024 * 1024)


def one_hot(low):
    rows = lax.broadcasted_iota(jnp.int32, (LOW, low.shape[1]), 0)
    return jnp.where(rows == low, 1.0, 0.0).astype(BF)


def gather_kernel(x_ref, slot_ref, out_ref, stacked):
    for b in range(HIGH):
        stacked[b * COLS : (b + 1) * COLS, :] = x_ref[:, b * LOW : (b + 1) * LOW]

    @pl.loop(0, DOM, unroll=2)
    def _(r):
        index = slot_ref[pl.ds(r, 1), :]
        high = index >> 8
        found = dot(stacked[...], one_hot(index & (LOW - 1)), NN)
        out = jnp.zeros((COLS, SLOTS), F32)
        for b in range(HIGH):
            out = jnp.where(high == b, found[b * COLS : (b + 1) * COLS], out)
        out = out.astype(BF)
        out_ref[2 * r] = out[:, :TILE]
        out_ref[2 * r + 1] = out[:, TILE:]


def gather_rows(x, slots):
    return pl.pallas_call(
        gather_kernel,
        out_shape=jax.ShapeDtypeStruct((RECV_TILES, COLS, TILE), BF),
        in_specs=[VMEM, VMEM],
        out_specs=VMEM,
        scratch_shapes=[pltpu.VMEM((HIGH * COLS, LOW), BF)],
        compiler_params=params(),
        cost_estimate=pl.CostEstimate(flops=4 * 10**9, bytes_accessed=2**21, transcendentals=0),
        name="gather_rows",
    )(x, slots)


def hub_forward_kernel(h_ref, coef_ref, out_ref, hubs):
    @pl.when(pl.program_id(0) == 0)
    def _():
        for q in range(DOM):
            hubs[:, q * TILE : (q + 1) * TILE] = h_ref[q]

    out_ref[...] = dot(hubs[...], coef_ref[...], NT)


def hub_forward(hubs, coef):
    step = 256
    return pl.pallas_call(
        hub_forward_kernel,
        grid=(NODES // step,),
        out_shape=jax.ShapeDtypeStruct((COLS, NODES), F32),
        in_specs=[
            pl.BlockSpec((DOM, COLS, TILE), lambda i: (0, 0, 0)),
            pl.BlockSpec((step, HUBS), lambda i: (i, 0)),
        ],
        out_specs=pl.BlockSpec((COLS, step), lambda i: (0, i)),
        scratch_shapes=[pltpu.VMEM((COLS, HUBS), BF)],
        compiler_params=params(),
        cost_estimate=pl.CostEstimate(flops=2 * 10**9, bytes_accessed=2**24, transcendentals=0),
        name="hub_forward",
    )(hubs, coef)


def tile_forward_kernel(index_ref, x_ref, recv_ref, coef_ref, hub_ref, out_ref, source, total):
    for t in range(OWN_TILES):
        source[t] = x_ref[:, t * TILE : (t + 1) * TILE]
        total[t] = hub_ref[:, t * TILE : (t + 1) * TILE]
    source[OWN_TILES:] = recv_ref[...]
    group = 8

    @pl.loop(0, TILES // group)
    def _(g):
        products = []
        for k in range(group):
            c = g * group + k
            products.append(dot(source[index_ref[1, c]], coef_ref[c], NT))
        for k in range(group):
            d = index_ref[0, g * group + k]
            total[d] = total[d] + products[k]

    for t in range(OWN_TILES):
        n = t * TILE % QUARTER
        out_ref[t * TILE // QUARTER, :, n : n + TILE] = total[t].astype(BF)


def tile_forward(index, x, recv, coef, hub):
    return pl.pallas_call(
        tile_forward_kernel,
        out_shape=jax.ShapeDtypeStruct((FEAT, COLS, QUARTER), BF),
        in_specs=[SMEM, VMEM, VMEM, VMEM, VMEM],
        out_specs=VMEM,
        scratch_shapes=[
            pltpu.VMEM((OWN_TILES + RECV_TILES, COLS, TILE), BF),
            pltpu.VMEM((OWN_TILES, COLS, TILE), F32),
        ],
        compiler_params=params(),
        cost_estimate=pl.CostEstimate(flops=10**9, bytes_accessed=2**22, transcendentals=0),
        name="tile_forward",
    )(index, x, recv, coef, hub)


def dense_kernel(agg_ref, early_ref, grad_agg_ref, late_ref):
    def whole(ref, first, lanes=slice(None)):
        return jnp.concatenate([ref[f, first : first + COLS, lanes] for f in range(FEAT)], 0)

    hid = FEAT * COLS
    self_weight = whole(early_ref, 2 * COLS, slice(0, hid))
    neigh_weight = whole(early_ref, 2 * COLS, slice(hid, 2 * hid))
    pre_act = dot(self_weight, whole(early_ref, 0), TN) + dot(neigh_weight, whole(agg_ref, 0), TN)
    down = jnp.exp(jnp.minimum(pre_act, 0.0))
    output = jnp.where(pre_act > 0, pre_act, down - 1.0).astype(BF)
    slope = jnp.where(pre_act > 0, 1.0, down)
    grad_pre = (whole(early_ref, COLS).astype(F32) * slope).astype(BF)
    grad_agg = dot(neigh_weight, grad_pre, NN).astype(BF)
    self_back = dot(self_weight, grad_pre, NN).astype(BF)
    for f in range(FEAT):
        grad_agg_ref[f] = grad_agg[f * COLS : (f + 1) * COLS]
        late_ref[f, :COLS] = output[f * COLS : (f + 1) * COLS]
        late_ref[f, COLS:] = self_back[f * COLS : (f + 1) * COLS]


def dense(agg, early):
    return pl.pallas_call(
        dense_kernel,
        out_shape=(
            jax.ShapeDtypeStruct((FEAT, COLS, QUARTER), BF),
            jax.ShapeDtypeStruct((FEAT, 2 * COLS, QUARTER), BF),
        ),
        in_specs=[VMEM, VMEM],
        out_specs=(VMEM, VMEM),
        compiler_params=params(),
        cost_estimate=pl.CostEstimate(flops=10**9, bytes_accessed=2**21, transcendentals=2**17),
        name="dense",
    )(agg, early)


def tile_backward_kernel(index_ref, grad_ref, coef_ref, recv_ref, own_ref, grads, total):
    for t in range(OWN_TILES):
        n = t * TILE % QUARTER
        grads[t] = grad_ref[t * TILE // QUARTER, :, n : n + TILE]
    total[:OWN_TILES] = jnp.zeros((OWN_TILES, COLS, TILE), F32)
    total[OWN_TILES:] = jnp.zeros((RECV_TILES, COLS, TILE), F32)
    group = 8

    @pl.loop(0, TILES // group)
    def _(g):
        products = []
        for k in range(group):
            c = g * group + k
            products.append(dot(grads[index_ref[0, c]], coef_ref[c], NN))
        for k in range(group):
            s = index_ref[1, g * group + k]
            total[s] = total[s] + products[k]

    recv_ref[...] = total[OWN_TILES:].astype(BF)
    for t in range(OWN_TILES):
        own_ref[:, t * TILE : (t + 1) * TILE] = total[t]


def tile_backward(index, grad, coef):
    return pl.pallas_call(
        tile_backward_kernel,
        out_shape=(
            jax.ShapeDtypeStruct((RECV_TILES, COLS, TILE), BF),
            jax.ShapeDtypeStruct((COLS, NODES), F32),
        ),
        in_specs=[SMEM, VMEM, VMEM],
        out_specs=(VMEM, VMEM),
        scratch_shapes=[
            pltpu.VMEM((OWN_TILES, COLS, TILE), BF),
            pltpu.VMEM((OWN_TILES + RECV_TILES, COLS, TILE), F32),
        ],
        compiler_params=params(),
        cost_estimate=pl.CostEstimate(flops=10**9, bytes_accessed=2**22, transcendentals=0),
        name="tile_backward",
    )(index, grad, coef)


def hub_backward_kernel(grad_ref, coef_ref, out_ref, grads):
    @pl.when(pl.program_id(0) == 0)
    def _():
        for f in range(FEAT):
            grads[:, f * QUARTER : (f + 1) * QUARTER] = grad_ref[f]

    terms = dot(grads[...], coef_ref[...], NN).astype(BF)
    for k in range(out_ref.shape[0]):
        out_ref[k] = terms[:, k * TILE : (k + 1) * TILE]


def hub_backward(grad, coef):
    step = 512
    return pl.pallas_call(
        hub_backward_kernel,
        grid=(HUBS // step,),
        out_shape=jax.ShapeDtypeStruct((DOM, COLS, TILE), BF),
        in_specs=[
            pl.BlockSpec((FEAT, COLS, QUARTER), lambda i: (0, 0, 0)),
            pl.BlockSpec((NODES, step), lambda i: (0, i)),
        ],
        out_specs=pl.BlockSpec((step // TILE, COLS, TILE), lambda i: (i, 0, 0)),
        scratch_shapes=[pltpu.VMEM((COLS, NODES), BF)],
        compiler_params=params(),
        cost_estimate=pl.CostEstimate(flops=2 * 10**9, bytes_accessed=2**24, transcendentals=0),
        name="hub_backward",
    )(grad, coef)


def scatter_kernel(slot_ref, recv_ref, own_ref, late_ref, out_ref, total):
    total[...] = jnp.zeros_like(total)
    group = 4

    @pl.loop(0, DOM // group)
    def _(g):
        spread, hots = [], []
        for k in range(group):
            r = g * group + k
            index = slot_ref[pl.ds(r, 1), :]
            high = index >> 8
            rows = jnp.concatenate([recv_ref[2 * r], recv_ref[2 * r + 1]], 1)
            spread.append(
                jnp.concatenate([jnp.where(high == b, rows, jnp.zeros_like(rows)) for b in range(HIGH)], 0)
            )
            hots.append(one_hot(index & (LOW - 1)))
        total[...] += dot(jnp.concatenate(spread, 1), jnp.concatenate(hots, 1), NT)

    for b in range(HIGH):
        lanes = slice(b * LOW, (b + 1) * LOW)
        n = b * LOW % QUARTER
        back = late_ref[b * LOW // QUARTER, COLS:, n : n + LOW].astype(F32)
        out_ref[:, lanes] = total[b * COLS : (b + 1) * COLS] + own_ref[:, lanes] + back


def scatter_rows(slots, recv, own, late):
    return pl.pallas_call(
        scatter_kernel,
        out_shape=jax.ShapeDtypeStruct((COLS, NODES), F32),
        in_specs=[VMEM, VMEM, VMEM, VMEM],
        out_specs=VMEM,
        scratch_shapes=[pltpu.VMEM((HIGH * COLS, LOW), F32)],
        compiler_params=params(),
        cost_estimate=pl.CostEstimate(flops=4 * 10**9, bytes_accessed=2**21, transcendentals=0),
        name="scatter_rows",
    )(slots, recv, own, late)


def quarters(x):
    return jnp.swapaxes(x.reshape(COLS, FEAT, QUARTER), 0, 1)


def body(
    features,
    hub_feats,
    hub_coef,
    tile_coef,
    tile_index,
    boundary_rows,
    self_weight,
    neigh_weight,
    out_grad,
):
    x = features.T
    slots = boundary_rows[0]
    index = tile_index.T
    to_dom = functools.partial(lax.all_to_all, axis_name="dom", split_axis=0, concat_axis=0, tiled=True)
    to_feat = functools.partial(lax.all_to_all, axis_name="feat", split_axis=0, concat_axis=0, tiled=True)

    hubs = to_dom(jnp.broadcast_to(hub_feats.T[None], (DOM, COLS, TILE)))
    outgoing = gather_rows(x, slots)
    incoming = to_dom(outgoing)

    weights = jnp.concatenate([self_weight, neigh_weight], 1)
    early = to_feat(
        jnp.concatenate(
            [quarters(x), quarters(out_grad.T), jnp.broadcast_to(weights[None], (FEAT, COLS, QUARTER))], 1
        )
    )
    hub_part = hub_forward(hubs, hub_coef)
    aggregate = tile_forward(index, x, incoming, tile_coef, hub_part)
    grad_quarter, late_quarter = dense(to_feat(aggregate), early)
    grad_agg = to_feat(grad_quarter)
    halo_back, own_grad = tile_backward(index, grad_agg, tile_coef)
    returned = to_dom(halo_back)
    hub_terms = hub_backward(grad_agg, hub_coef)
    late = to_feat(late_quarter)
    hub_arrived = to_dom(hub_terms)
    grad_feats = scatter_rows(slots, returned, own_grad, late)
    grad_hubs = jnp.sum(hub_arrived.astype(F32), 0)
    output_rows = jnp.swapaxes(late[:, :COLS], 0, 1).reshape(COLS, NODES)
    return (output_rows.T, grad_feats.T, grad_hubs.T)


def solution(mesh):
    return jax.shard_map(
        body,
        mesh=mesh,
        in_specs=(
            P("dom", "feat"),
            P("dom", "feat"),
            P("dom", None),
            P("dom", None, None),
            P("dom", None),
            P("dom", None, None),
            P("feat", None),
            P("feat", None),
            P("dom", "feat"),
        ),
        out_specs=(P("dom", "feat"), P("dom", "feat"), P("dom", "feat")),
        check_vma=False,
    )
```

time: 376 us -> 148 us (0.39)
  blocking collectives: 91.5 us -> 22.1 us
  local copies, waits for them, and re-layouts: 63.1 us -> 6.02 us
  other arithmetic: 57.7 us -> 2.71 us
  matrix products: 41.6 us -> 0 us
  Pallas kernels: 0 us -> 41.3 us
  waiting for transfers between devices: 81.3 us -> 43.9 us
  between operations: 14.2 us -> 0.86 us
  starting transfers between devices: 25.2 us -> 30.4 us
    all_gather x1 -> x0, blocking collectives: 91.5 us -> none  [body(): lax.all_gather(hub_feats, 'dom', axis=0, tiled=True)]
    scatter-add x1 -> x0, other arithmetic: 48 us -> none  [body(): returned = jnp.zeros((node_count + 1, feat_width), jnp.float32).at[flat_i...]
    dot_general x9 -> x0, matrix products: 41.6 us -> none  [the longest x1 13.6 us: body(): jnp.dot(aggregate, neigh_weight, preferred_element_type=jnp.float32)]
    pallas_call x0 -> x7, Pallas kernels: none -> 41.3 us  [the longest x1 10.9 us: hub_forward(): pl.pallas_call(hub_forward_kernel, grid=(NODES // step,), out_shape=jax.S...]
    gather x4 -> x0, local copies, waits for them, and re-layouts: 37.2 us -> none  [the longest x2 32 us: body(): jnp.take(features, jnp.maximum(slot_table, 0), axis=0)]
    reduce_scatter x1 -> x0, waiting for transfers between devices: 36.2 us -> none  [body(): lax.psum_scatter(partial_sum, 'feat', scatter_dimension=1, tiled=True)]
    all_to_all x0 -> x2, blocking collectives: none -> 22.1 us  [the longest x1 12.1 us: body(): grad_quarter, late_quarter = dense(to_feat(aggregate), early)]
    all_gather x1 -> x0, waiting for transfers between devices: 20.3 us -> none  [body(): grad_full = lax.all_gather(grad_pre, 'feat', axis=1, tiled=True)]
  transfers between devices with their start and end apart: 5 -> 6, of which waited for: 3 -> 4; matrix products, arithmetic and copies ran while one was open for 6% -> 3% of each run, Pallas kernels for 0% -> 23%
where the time goes in v1:
time: 148 us; the launch traced here: 147 us
  waiting for transfers between devices  43.9 us (30%)
  Pallas kernels  41.3 us (28%)
  starting transfers between devices  30.4 us (21%)
  blocking collectives  22.1 us (15%)
  local copies, waits for them, and re-layouts  6.02 us (4%)
  other arithmetic  2.71 us (2%)
    all_to_all x1, waiting for transfers between devices, body(): incoming = to_dom(outgoing)  15.6 us
    all_to_all x1, waiting for transfers between devices, body(): returned = to_dom(halo_back)  14.2 us
    all_to_all x1, blocking collectives, body(): grad_quarter, late_quarter = dense(to_feat(aggregate), early)  12.1 us
    pallas_call x1, Pallas kernels, hub_forward(): pl.pallas_call(hub_forward_kernel, grid=(NODES // step,), out_shape=jax.S...  10.9 us
    all_to_all x1, blocking collectives, body(): grad_agg = to_feat(grad_quarter)  9.92 us
    pallas_call x1, Pallas kernels, hub_backward(): pl.pallas_call(hub_backward_kernel, grid=(HUBS // step,), out_shape=jax.S...  9.59 us
    all_to_all x1, starting transfers between devices, body(): hubs = to_dom(jnp.broadcast_to(hub_feats.T[None], (DOM, COLS, TILE)))  8.76 us
    all_to_all x1, waiting for transfers between devices, body(): hub_arrived = to_dom(hub_terms)  7.88 us
  transfers between devices with their start and end apart: 6, of which 4 were waited for; matrix products, arithmetic and copies ran while one was open for 3% of the time, Pallas kernels for 23%

profile of v1, /device:TPU:0, one launch (start us, length us, event | category | flops | bytes accessed | tf_op | source)
XLA Modules:
  0.0 147.3 jit_solution(8692545420963644510)
XLA Ops:
  0.7 1.7 %broadcast_in_dim.4 = bf16[32,64,128]{2,1,0:T(8,128)(2,1)} broadcast(bf16[64,128]{1,0:T(8,128)(2,1)} %bitcast.39), dimensions={1,2} | broadcast | bytes 540672 | tf_op jit(solution)/shard_map/broadcast_in_dim | solution.py:307
  2.3 8.8 %all-to-all-start.1 = ((bf16[32,64,128]{2,1,0:T(8,128)(2,1)}), bf16[32,64,128]{2,1,0:T(8,128)(2,1)S(1)}, u32[]{:S(2)}, u32[]{:S(2)}) async-start(bf16[32,64,128]{2,1,0:T(8,128)(2,1)} %broadcast_in_dim.4), calls=%async_computation.1 | async-start | bytes 1048576 | tf_op jit(solution)/shard_map/all_to_all | solution.py:307
  11.1 6.0 %gather_rows.1 = bf16[64,64,128]{2,1,0:T(8,128)(2,1)} custom-call(bf16[64,2048]{1,0:T(8,128)(2,1)S(1)} %bitcast.27, s32[32,256]{1,0:T(8,128)S(1)} %bitcast.32), custom_call_target="tpu_custom_call" | custom-call | flops 4000000000 | bytes 2097152 | tf_op jit(solution)/shard_map/gather_rows/pallas_call | solution.py:65
  17.1 6.2 %all-to-all-done.1.h_ref = bf16[32,64,128]{2,1,0:T(8,128)(2,1)S(1)} async-done(((bf16[32,64,128]{2,1,0:T(8,128)(2,1)}), bf16[32,64,128]{2,1,0:T(8,128)(2,1)S(1)}, u32[]{:S(2)}, u32[]{:S(2)}) %all-to-all-start.1) | async-done | bytes 524320 | tf_op jit(solution)/shard_map/all_to_all | solution.py:307
  23.3 3.9 %all-to-all-start = ((bf16[64,64,128]{2,1,0:T(8,128)(2,1)}), bf16[64,64,128]{2,1,0:T(8,128)(2,1)S(1)}, u32[]{:S(2)}, u32[]{:S(2)}) async-start(bf16[64,64,128]{2,1,0:T(8,128)(2,1)} %gather_rows.1), calls=%async_computation | async-start | bytes 2097152 | tf_op jit(solution)/shard_map/all_to_all | solution.py:309
  27.4 1.0 pad_maximum_fusion
  28.3 15.6 %all-to-all-done.recv_ref = bf16[64,64,128]{2,1,0:T(8,128)(2,1)S(1)} async-done(((bf16[64,64,128]{2,1,0:T(8,128)(2,1)}), bf16[64,64,128]{2,1,0:T(8,128)(2,1)S(1)}, u32[]{:S(2)}, u32[]{:S(2)}) %all-to-all-start) | async-done | bytes 1048608 | tf_op jit(solution)/shard_map/all_to_all | solution.py:309
  43.9 4.9 %all-to-all-start.3 = ((bf16[4,192,512]{2,1,0:T(8,128)(2,1)}), bf16[4,192,512]{2,1,0:T(8,128)(2,1)S(1)}, u32[]{:S(2)}, u32[]{:S(2)}) async-start(bf16[4,192,512]{2,1,0:T(8,128)(2,1)} %pad_maximum_fusion), calls=%async_computation.3 | async-start | bytes 1572864 | tf_op jit(solution)/shard_map/all_to_all | solution.py:312
  48.8 10.9 %hub_forward.1.hub_ref = f32[64,2048]{1,0:T(8,128)S(1)} custom-call(bf16[32,64,128]{2,1,0:T(8,128)(2,1)S(1)} %all-to-all-done.1.h_ref, bf16[2048,4096]{1,0:T(8,128)(2,1)} %coef_ref.7), custom_call_target="tpu_custom_call" | custom-call | flops 2000000000 | bytes 16777216 | tf_op jit(solution)/shard_map/hub_forward/pallas_call | solution.py:88
  59.8 4.1 %tile_forward.1 = bf16[4,64,512]{2,1,0:T(8,128)(2,1)S(1)} custom-call(s32[2,96]{1,0:T(2,128)S(1)} %bitcast.30, bf16[64,2048]{1,0:T(8,128)(2,1)S(1)} %bitcast.29, bf16[64,64,128]{2,1,0:T(8,128)(2,1)S(1)} %all-to-all-done.recv_ref, bf16[96,128,128]{2,1,0:T(8,128)(2,1)S(1)} %copy-done, f32[64,2048]{1,0:T(8,128)S(1)} %hub_forward.1.hub_ref), custom_call_target="tpu_custom_call" | custom-call | flops 1000000000 | bytes 4194304 | tf_op jit(solution)/shard_map/tile_forward/pallas_call | solution.py:127
  63.9 12.1 %all_to_all.40.agg_ref = bf16[4,64,512]{2,1,0:T(8,128)(2,1)S(1)} all-to-all(bf16[4,64,512]{2,1,0:T(8,128)(2,1)S(1)} %tile_forward.1), channel_id=1, replica_groups=mesh['dom'=32,'feat'=4] {'feat'}, dimensions={0} | all-to-all | bytes 524288 | tf_op jit(solution)/shard_map/all_to_all | solution.py:319
  76.0 1.5 %dense.1 = (bf16[4,64,512]{2,1,0:T(8,128)(2,1)S(1)}, bf16[4,128,512]{2,1,0:T(8,128)(2,1)}) custom-call(bf16[4,64,512]{2,1,0:T(8,128)(2,1)S(1)} %all_to_all.40.agg_ref, bf16[4,192,512]{2,1,0:T(8,128)(2,1)S(1)} %all-to-all-done.3.early_ref), custom_call_target="tpu_custom_call" | custom-call | flops 1000000000 | bytes 2097152 | tf_op jit(solution)/shard_map/dense/pallas_call | solution.py:163
  77.5 9.9 %all_to_all.41.grad_ref = bf16[4,64,512]{2,1,0:T(8,128)(2,1)S(1)} all-to-all(bf16[4,64,512]{2,1,0:T(8,128)(2,1)S(1)} %get-tuple-element.8), channel_id=1, replica_groups=mesh['dom'=32,'feat'=4] {'feat'}, dimensions={0} | all-to-all | bytes 524288 | tf_op jit(solution)/shard_map/all_to_all | solution.py:320
  87.5 4.1 %all-to-all-start.4 = ((bf16[4,128,512]{2,1,0:T(8,128)(2,1)}), bf16[4,128,512]{2,1,0:T(8,128)(2,1)}, u32[]{:S(2)}, u32[]{:S(2)}) async-start(bf16[4,128,512]{2,1,0:T(8,128)(2,1)} %get-tuple-element.7), calls=%async_computation.4 | async-start | bytes 1048576 | tf_op jit(solution)/shard_map/all_to_all | solution.py:324
  91.6 9.6 %hub_backward.1 = bf16[32,64,128]{2,1,0:T(8,128)(2,1)S(1)} custom-call(bf16[4,64,512]{2,1,0:T(8,128)(2,1)S(1)} %all_to_all.41.grad_ref, bf16[2048,4096]{1,0:T(8,128)(2,1)} %coef_ref.7), custom_call_target="tpu_custom_call" | custom-call | flops 2000000000 | bytes 16777216 | tf_op jit(solution)/shard_map/hub_backward/pallas_call | solution.py:232
  102.0 4.6 %all-to-all-start.7 = ((bf16[32,64,128]{2,1,0:T(8,128)(2,1)}), bf16[32,64,128]{2,1,0:T(8,128)(2,1)}, u32[]{:S(2)}, u32[]{:S(2)}) async-start(bf16[32,64,128]{2,1,0:T(8,128)(2,1)} %copy-done.2), calls=%async_computation.7 | async-start | bytes 1048576 | tf_op jit(solution)/shard_map/all_to_all | solution.py:325
  106.7 3.4 %tile_backward.1 = (bf16[64,64,128]{2,1,0:T(8,128)(2,1)S(1)}, f32[64,2048]{1,0:T(8,128)S(1)}) custom-call(s32[2,96]{1,0:T(2,128)S(1)} %bitcast.31, bf16[4,64,512]{2,1,0:T(8,128)(2,1)S(1)} %all_to_all.41.grad_ref, bf16[96,128,128]{2,1,0:T(8,128)(2,1)S(1)} %copy-done.1), custom_call_target="tpu_custom_call" | custom-call | flops 1000000000 | bytes 4194304 | tf_op jit(solution)/shard_map/tile_backward/pallas_call | solution.py:201
  110.1 1.0 copy-done.4
  111.8 7.9 %all-to-all-done.7 = bf16[32,64,128]{2,1,0:T(8,128)(2,1)} async-done(((bf16[32,64,128]{2,1,0:T(8,128)(2,1)}), bf16[32,64,128]{2,1,0:T(8,128)(2,1)}, u32[]{:S(2)}, u32[]{:S(2)}) %all-to-all-start.7) | async-done | bytes 524320 | tf_op jit(solution)/shard_map/all_to_all | solution.py:325
  119.7 4.1 %all-to-all-start.6 = ((bf16[64,64,128]{2,1,0:T(8,128)(2,1)}), bf16[64,64,128]{2,1,0:T(8,128)(2,1)S(1)}, u32[]{:S(2)}, u32[]{:S(2)}) async-start(bf16[64,64,128]{2,1,0:T(8,128)(2,1)} %copy-done.4), calls=%async_computation.6 | async-start | bytes 2097152 | tf_op jit(solution)/shard_map/all_to_all | solution.py:322
  123.8 1.0 slice_bitcast_fusion
  125.5 1.7 %convert_reduce_fusion = f32[64,128]{1,0:T(8,128)} fusion(bf16[32,64,128]{2,1,0:T(8,128)(2,1)} %all-to-all-done.7), kind=kLoop, calls=%fused_computation | loop fusion | flops 516096 | bytes 557056 | tf_op jit(solution)/shard_map/reduce_sum | solution.py:327
  127.2 14.2 %all-to-all-done.6.recv_ref = bf16[64,64,128]{2,1,0:T(8,128)(2,1)S(1)} async-done(((bf16[64,64,128]{2,1,0:T(8,128)(2,1)}), bf16[64,64,128]{2,1,0:T(8,128)(2,1)S(1)}, u32[]{:S(2)}, u32[]{:S(2)}) %all-to-all-start.6) | async-done | bytes 1048608 | tf_op jit(solution)/shard_map/all_to_all | solution.py:322
  141.4 5.8 %scatter_rows.1 = f32[64,2048]{1,0:T(8,128)} custom-call(s32[32,256]{1,0:T(8,128)S(1)} %bitcast.33, bf16[64,64,128]{2,1,0:T(8,128)(2,1)S(1)} %all-to-all-done.6.recv_ref, f32[64,2048]{1,0:T(8,128)S(1)} %copy-done.8, bf16[4,128,512]{2,1,0:T(8,128)(2,1)} %all-to-all-done.4.late_ref), custom_call_target="tpu_custom_call" | custom-call | flops 4000000000 | bytes 2097152 | tf_op jit(solution)/shard_map/scatter_rows/pallas_call | solution.py:274
  (30 shorter events, 2.4 us)
Async XLA Ops:
  0.6 10.5 %copy-start.3 = (bf16[2048,64]{0,1:T(8,128)(2,1)S(1)}, bf16[2048,64]{0,1:T(8,128)(2,1)}, u32[]{:S(2)}) copy-start(bf16[2048,64]{0,1:T(8,128)(2,1)} %param.9) | copy-start | bytes 786436
  0.6 10.5 %copy-start.6 = (s32[1,32,256]{2,1,0:T(8,128)S(1)}, s32[1,32,256]{2,1,0:T(8,128)}, u32[]{:S(2)}) copy-start(s32[1,32,256]{2,1,0:T(8,128)} %param.14) | copy-start | bytes 98308
  2.3 21.0 %all-to-all-start.1 = ((bf16[32,64,128]{2,1,0:T(8,128)(2,1)}), bf16[32,64,128]{2,1,0:T(8,128)(2,1)S(1)}, u32[]{:S(2)}, u32[]{:S(2)}) async-start(bf16[32,64,128]{2,1,0:T(8,128)(2,1)} %broadcast_in_dim.4), calls=%async_computation.1 | async-start | bytes 1048576 | tf_op jit(solution)/shard_map/all_to_all | solution.py:307
  17.1 10.2 %copy-start.9 = (bf16[2048,64]{0,1:T(8,128)(2,1)S(1)}, bf16[2048,64]{0,1:T(8,128)(2,1)}, u32[]{:S(2)}) copy-start(bf16[2048,64]{0,1:T(8,128)(2,1)} %param.17) | copy-start | bytes 786436
  17.1 10.2 %copy-start.10 = (bf16[64,256]{1,0:T(8,128)(2,1)S(1)}, bf16[64,256]{1,0:T(8,128)(2,1)}, u32[]{:S(2)}) copy-start(bf16[64,256]{1,0:T(8,128)(2,1)} %param.16) | copy-start | bytes 98308
  17.1 10.3 %copy-start.11 = (bf16[64,256]{1,0:T(8,128)(2,1)S(1)}, bf16[64,256]{1,0:T(8,128)(2,1)}, u32[]{:S(2)}) copy-start(bf16[64,256]{1,0:T(8,128)(2,1)} %param.15) | copy-start | bytes 98308
  23.3 20.6 %all-to-all-start = ((bf16[64,64,128]{2,1,0:T(8,128)(2,1)}), bf16[64,64,128]{2,1,0:T(8,128)(2,1)S(1)}, u32[]{:S(2)}, u32[]{:S(2)}) async-start(bf16[64,64,128]{2,1,0:T(8,128)(2,1)} %gather_rows.1), calls=%async_computation | async-start | bytes 2097152 | tf_op jit(solution)/shard_map/all_to_all | solution.py:309
  43.9 20.0 %all-to-all-start.3 = ((bf16[4,192,512]{2,1,0:T(8,128)(2,1)}), bf16[4,192,512]{2,1,0:T(8,128)(2,1)S(1)}, u32[]{:S(2)}, u32[]{:S(2)}) async-start(bf16[4,192,512]{2,1,0:T(8,128)(2,1)} %pad_maximum_fusion), calls=%async_computation.3 | async-start | bytes 1572864 | tf_op jit(solution)/shard_map/all_to_all | solution.py:312
  48.8 10.9 %copy-start = (bf16[96,128,128]{2,1,0:T(8,128)(2,1)S(1)}, bf16[96,128,128]{2,1,0:T(8,128)(2,1)}, u32[]{:S(2)}) copy-start(bf16[96,128,128]{2,1,0:T(8,128)(2,1)} %coef_ref.6) | copy-start | bytes 9437188
  48.8 10.9 %copy-start.5 = (s32[96,2]{0,1:T(2,128)S(1)}, s32[96,2]{0,1:T(2,128)}, u32[]{:S(2)}) copy-start(s32[96,2]{0,1:T(2,128)} %param.13) | copy-start | bytes 2308
  87.5 14.6 %all-to-all-start.4 = ((bf16[4,128,512]{2,1,0:T(8,128)(2,1)}), bf16[4,128,512]{2,1,0:T(8,128)(2,1)}, u32[]{:S(2)}, u32[]{:S(2)}) async-start(bf16[4,128,512]{2,1,0:T(8,128)(2,1)} %get-tuple-element.7), calls=%async_computation.4 | async-start | bytes 1048576 | tf_op jit(solution)/shard_map/all_to_all | solution.py:324
  91.6 15.0 %copy-start.1 = (bf16[96,128,128]{2,1,0:T(8,128)(2,1)S(1)}, bf16[96,128,128]{2,1,0:T(8,128)(2,1)}, u32[]{:S(2)}) copy-start(bf16[96,128,128]{2,1,0:T(8,128)(2,1)} %coef_ref.6) | copy-start | bytes 9437188
  101.2 0.8 copy-start.2
  102.0 17.7 %all-to-all-start.7 = ((bf16[32,64,128]{2,1,0:T(8,128)(2,1)}), bf16[32,64,128]{2,1,0:T(8,128)(2,1)}, u32[]{:S(2)}, u32[]{:S(2)}) async-start(bf16[32,64,128]{2,1,0:T(8,128)(2,1)} %copy-done.2), calls=%async_computation.7 | async-start | bytes 1048576 | tf_op jit(solution)/shard_map/all_to_all | solution.py:325
  110.1 1.0 copy-start.4
  111.1 0.8 copy-start.7
  119.7 21.7 %copy-start.8 = (f32[64,2048]{1,0:T(8,128)S(1)}, f32[64,2048]{1,0:T(8,128)}, u32[]{:S(2)}) copy-start(f32[64,2048]{1,0:T(8,128)} %copy-done.7) | copy-start | bytes 1572868
  119.7 21.7 %all-to-all-start.6 = ((bf16[64,64,128]{2,1,0:T(8,128)(2,1)}), bf16[64,64,128]{2,1,0:T(8,128)(2,1)S(1)}, u32[]{:S(2)}, u32[]{:S(2)}) async-start(bf16[64,64,128]{2,1,0:T(8,128)(2,1)} %copy-done.4), calls=%async_computation.6 | async-start | bytes 2097152 | tf_op jit(solution)/shard_map/all_to_all | solution.py:322

commit v2 on v1

v2 whole, which is shorter than its diff:
```python
import jax
import jax.numpy as jnp
from jax import lax
from jax.experimental import pallas as pl
from jax.experimental.pallas import tpu as pltpu
from jax.sharding import PartitionSpec as P

BF = jnp.bfloat16
F32 = jnp.float32
NT = (((1,), (1,)), ((), ()))
NN = (((1,), (0,)), ((), ()))
TN = (((0,), (0,)), ((), ()))

COLS = 64
NODES = 2048
DOM = 32
FEAT = 4
SLOTS = 256
TILE = 128
TILES = 96
OWN_TILES = NODES // TILE
RECV_TILES = DOM * SLOTS // TILE
QUARTER = NODES // FEAT
LOW = 256
HIGH = NODES // LOW
HUBS = 4096

VMEM = pl.BlockSpec(memory_space=pltpu.VMEM)
SMEM = pl.BlockSpec(memory_space=pltpu.SMEM)


def dot(a, b, dims):
    return lax.dot_general(a, b, dims, preferred_element_type=F32)


def params(mib=40):
    return pltpu.CompilerParams(vmem_limit_bytes=mib * 1024 * 1024)


def one_hot(low):
    rows = lax.broadcasted_iota(jnp.int32, (LOW, low.shape[1]), 0)
    return jnp.where(rows == low, 1.0, 0.0).astype(BF)


def gather_kernel(x_ref, slot_ref, hub_ref, out_ref, stacked):
    for b in range(HIGH):
        stacked[b * COLS : (b + 1) * COLS, :] = x_ref[:, b * LOW : (b + 1) * LOW]

    @pl.loop(0, DOM, unroll=4)
    def _(r):
        index = slot_ref[pl.ds(r, 1), :]
        high = index >> 8
        found = dot(stacked[...], one_hot(index & (LOW - 1)), NN)
        out = jnp.zeros((COLS, SLOTS), F32)
        for b in range(HIGH):
            out = jnp.where(high == b, found[b * COLS : (b + 1) * COLS], out)
        out = out.astype(BF)
        out_ref[r, 0] = out[:, :TILE]
        out_ref[r, 1] = out[:, TILE:]
        out_ref[r, 2] = hub_ref[...]


def gather_rows(x, slots, hubs):
    return pl.pallas_call(
        gather_kernel,
        out_shape=jax.ShapeDtypeStruct((DOM, 3, COLS, TILE), BF),
        in_specs=[VMEM, VMEM, VMEM],
        out_specs=VMEM,
        scratch_shapes=[pltpu.VMEM((HIGH * COLS, LOW), BF)],
        compiler_params=params(),
        cost_estimate=pl.CostEstimate(flops=4 * 10**9, bytes_accessed=2**21, transcendentals=0),
        name="gather_rows",
    )(x, slots, hubs)


def forward_kernel(feat_ref, index_ref, x_ref, recv_ref, tile_ref, hub_ref, *rest):
    outs, (source, hubs, total) = rest[:FEAT], rest[FEAT:]
    step = pl.program_id(0)
    steps = pl.num_programs(0)
    step_tiles = OWN_TILES // 8
    group = TILES // 8

    @pl.when(step == 0)
    def _():
        for t in range(OWN_TILES):
            source[t] = x_ref[:, t * TILE : (t + 1) * TILE]
        for q in range(DOM):
            source[OWN_TILES + 2 * q] = recv_ref[q, 0]
            source[OWN_TILES + 2 * q + 1] = recv_ref[q, 1]
            hubs[:, q * TILE : (q + 1) * TILE] = recv_ref[q, 2]
        total[...] = jnp.zeros_like(total)

    products = []
    for k in range(group):
        c = step * group + k
        products.append(dot(tile_ref[c], source[index_ref[1, c]], NT))
    hub_part = dot(hub_ref[...], hubs[...], NT)
    for k in range(group):
        d = index_ref[0, step * group + k]
        total[d] = total[d] + products[k]
    for k in range(step_tiles):
        t = step * step_tiles + k
        total[t] = total[t] + hub_part[k * TILE : (k + 1) * TILE]

    @pl.when(step == steps - 1)
    def _():
        for k in range(FEAT):
            first = (feat_ref[0] ^ k) * (QUARTER // TILE)
            for j in range(QUARTER // TILE):
                outs[k][:, j * TILE : (j + 1) * TILE] = total[first + j].T.astype(BF)


def forward(feat, index, x, recv, tiles, hub_coef):
    whole = lambda shape: pl.BlockSpec(shape, lambda i: (0,) * len(shape))
    step = NODES // 8
    return pl.pallas_call(
        forward_kernel,
        grid=(8,),
        out_shape=[jax.ShapeDtypeStruct((COLS, QUARTER), BF)] * FEAT,
        in_specs=[
            SMEM,
            SMEM,
            whole((COLS, NODES)),
            whole((DOM, 3, COLS, TILE)),
            whole((TILES, TILE, TILE)),
            pl.BlockSpec((step, HUBS), lambda i: (i, 0)),
        ],
        out_specs=[whole((COLS, QUARTER))] * FEAT,
        scratch_shapes=[
            pltpu.VMEM((OWN_TILES + RECV_TILES, COLS, TILE), BF),
            pltpu.VMEM((COLS, HUBS), BF),
            pltpu.VMEM((OWN_TILES, TILE, COLS), F32),
        ],
        compiler_params=params(),
        cost_estimate=pl.CostEstimate(flops=3 * 10**9, bytes_accessed=2**24, transcendentals=0),
        name="forward",
    )(feat, index, x, recv, tiles, hub_coef)


def dense_kernel(feat_ref, *rest):
    aggs, earlies, grad_outs, lates, scratch = rest[:4], rest[4:8], rest[8:12], rest[12:16], rest[16:]
    agg, x, up, weights, down_grad, output, back = scratch
    feat = feat_ref[0]
    hid = FEAT * COLS

    def rows(k):
        return pl.ds(pl.multiple_of((feat ^ k) * COLS, COLS), COLS)

    for k in range(FEAT):
        agg[rows(k)] = aggs[k][...]
        x[rows(k)] = earlies[k][:COLS]
        up[rows(k)] = earlies[k][COLS : 2 * COLS]
        weights[rows(k)] = earlies[k][2 * COLS :]
    self_weight = weights[:, :hid]
    neigh_weight = weights[:, hid:]
    pre_act = dot(self_weight, x[...], TN) + dot(neigh_weight, agg[...], TN)
    fall = jnp.exp(jnp.minimum(pre_act, 0.0))
    output[...] = jnp.where(pre_act > 0, pre_act, fall - 1.0).astype(BF)
    slope = jnp.where(pre_act > 0, 1.0, fall)
    grad_pre = (up[...].astype(F32) * slope).astype(BF)
    down_grad[...] = dot(neigh_weight, grad_pre, NN).astype(BF)
    back[...] = dot(self_weight, grad_pre, NN).astype(BF)
    for k in range(FEAT):
        grad_outs[k][...] = down_grad[rows(k)]
        lates[k][:COLS] = output[rows(k)]
        lates[k][COLS:] = back[rows(k)]


def dense(feat, aggs, earlies):
    block = pltpu.VMEM((FEAT * COLS, QUARTER), BF)
    outs = pl.pallas_call(
        dense_kernel,
        out_shape=[jax.ShapeDtypeStruct((COLS, QUARTER), BF)] * FEAT
        + [jax.ShapeDtypeStruct((2 * COLS, QUARTER), BF)] * FEAT,
        in_specs=[SMEM] + [VMEM] * 8,
        out_specs=[VMEM] * 8,
        scratch_shapes=[block] * 7,
        compiler_params=params(),
        cost_estimate=pl.CostEstimate(flops=10**9, bytes_accessed=2**21, transcendentals=2**17),
        name="dense",
    )(feat, *aggs, *earlies)
    return outs[:4], outs[4:]


def tile_backward_kernel(feat_ref, index_ref, *rest):
    grad_refs, (coef_ref, recv_ref, own_ref, grads, total) = rest[:4], rest[4:]
    for k in range(FEAT):
        first = (feat_ref[0] ^ k) * (QUARTER // TILE)
        for j in range(QUARTER // TILE):
            grads[first + j] = grad_refs[k][:, j * TILE : (j + 1) * TILE]
    total[:OWN_TILES] = jnp.zeros((OWN_TILES, COLS, TILE), F32)
    total[OWN_TILES:] = jnp.zeros((RECV_TILES, COLS, TILE), F32)
    group = 8

    @pl.loop(0, TILES // group)
    def _(g):
        products = []
        for k in range(group):
            c = g * group + k
            products.append(dot(grads[index_ref[0, c]], coef_ref[c], NN))
        for k in range(group):
            s = index_ref[1, g * group + k]
            total[s] = total[s] + products[k]

    recv_ref[...] = total[OWN_TILES:].astype(BF)
    for t in range(OWN_TILES):
        own_ref[:, t * TILE : (t + 1) * TILE] = total[t]


def tile_backward(feat, index, grad, coef):
    return pl.pallas_call(
        tile_backward_kernel,
        out_shape=(
            jax.ShapeDtypeStruct((RECV_TILES, COLS, TILE), BF),
            jax.ShapeDtypeStruct((COLS, NODES), F32),
        ),
        in_specs=[SMEM, SMEM] + [VMEM] * 5,
        out_specs=(VMEM, VMEM),
        scratch_shapes=[
            pltpu.VMEM((OWN_TILES, COLS, TILE), BF),
            pltpu.VMEM((OWN_TILES + RECV_TILES, COLS, TILE), F32),
        ],
        compiler_params=params(),
        cost_estimate=pl.CostEstimate(flops=10**9, bytes_accessed=2**22, transcendentals=0),
        name="tile_backward",
    )(feat, index, *grad, coef)


def hub_backward_kernel(feat_ref, *rest):
    grad_refs, (coef_ref, recv_ref, out_ref, grads) = rest[:4], rest[4:]

    @pl.when(pl.program_id(0) == 0)
    def _():
        for k in range(FEAT):
            grads[:, pl.ds(pl.multiple_of((feat_ref[0] ^ k) * QUARTER, QUARTER), QUARTER)] = grad_refs[k][...]

    terms = dot(grads[...], coef_ref[...], NN).astype(BF)
    for k in range(out_ref.shape[0]):
        out_ref[k, 0] = recv_ref[2 * k]
        out_ref[k, 1] = recv_ref[2 * k + 1]
        out_ref[k, 2] = terms[:, k * TILE : (k + 1) * TILE]


def hub_backward(feat, grad, coef, recv):
    step = 512
    doms = step // TILE
    piece = pl.BlockSpec((COLS, QUARTER), lambda i: (0, 0))
    return pl.pallas_call(
        hub_backward_kernel,
        grid=(HUBS // step,),
        out_shape=jax.ShapeDtypeStruct((DOM, 3, COLS, TILE), BF),
        in_specs=[SMEM]
        + [piece] * 4
        + [pl.BlockSpec((NODES, step), lambda i: (0, i)), pl.BlockSpec((2 * doms, COLS, TILE), lambda i: (i, 0, 0))],
        out_specs=pl.BlockSpec((doms, 3, COLS, TILE), lambda i: (i, 0, 0, 0)),
        scratch_shapes=[pltpu.VMEM((COLS, NODES), BF)],
        compiler_params=params(),
        cost_estimate=pl.CostEstimate(flops=2 * 10**9, bytes_accessed=2**24, transcendentals=0),
        name="hub_backward",
    )(feat, *grad, coef, recv)


def scatter_kernel(feat_ref, slot_ref, recv_ref, own_ref, *rest):
    lates, (grad_ref, hub_ref, output_ref, total) = rest[:4], rest[4:]
    total[...] = jnp.zeros_like(total)
    group = 4

    @pl.loop(0, DOM // group)
    def _(g):
        spread, hots = [], []
        for k in range(group):
            r = g * group + k
            index = slot_ref[pl.ds(r, 1), :]
            high = index >> 8
            rows = jnp.concatenate([recv_ref[r, 0], recv_ref[r, 1]], 1)
            spread.append(
                jnp.concatenate([jnp.where(high == b, rows, jnp.zeros_like(rows)) for b in range(HIGH)], 0)
            )
            hots.append(one_hot(index & (LOW - 1)))
        total[...] += dot(jnp.concatenate(spread, 1), jnp.concatenate(hots, 1), NT)

    hub = jnp.zeros((COLS, TILE), F32)
    for r in range(DOM):
        hub = hub + recv_ref[r, 2].astype(F32)
    hub_ref[...] = hub
    for b in range(HIGH):
        lanes = slice(b * LOW, (b + 1) * LOW)
        grad_ref[:, lanes] = total[b * COLS : (b + 1) * COLS] + own_ref[:, lanes]
    for k in range(FEAT):
        lanes = pl.ds(pl.multiple_of((feat_ref[0] ^ k) * QUARTER, QUARTER), QUARTER)
        grad_ref[:, lanes] = grad_ref[:, lanes] + lates[k][COLS:].astype(F32)
        output_ref[:, lanes] = lates[k][:COLS]


def scatter_rows(feat, slots, recv, own, late):
    return pl.pallas_call(
        scatter_kernel,
        out_shape=(
            jax.ShapeDtypeStruct((COLS, NODES), F32),
            jax.ShapeDtypeStruct((COLS, TILE), F32),
            jax.ShapeDtypeStruct((COLS, NODES), BF),
        ),
        in_specs=[SMEM] + [VMEM] * 7,
        out_specs=(VMEM, VMEM, VMEM),
        scratch_shapes=[pltpu.VMEM((HIGH * COLS, LOW), F32)],
        compiler_params=params(),
        cost_estimate=pl.CostEstimate(flops=4 * 10**9, bytes_accessed=2**21, transcendentals=0),
        name="scatter_rows",
    )(feat, slots, recv, own, *late)


def to_dom(x):
    return lax.all_to_all(x, "dom", split_axis=0, concat_axis=0, tiled=True)


def to_feat(parts):
    return [parts[0]] + [
        lax.ppermute(parts[k], "feat", [(f, f ^ k) for f in range(FEAT)]) for k in range(1, FEAT)
    ]


def body(
    features,
    hub_feats,
    hub_coef,
    tile_coef,
    tile_index,
    boundary_rows,
    self_weight,
    neigh_weight,
    out_grad,
):
    x = features.T
    up = out_grad.T
    slots = boundary_rows[0]
    index = tile_index.T
    feat = lax.axis_index("feat")
    feat_ref = feat.reshape(1)
    weights = jnp.concatenate([self_weight, neigh_weight], 1)

    def early_part(k):
        first = (feat ^ k) * QUARTER
        return jnp.concatenate(
            [
                lax.dynamic_slice_in_dim(x, first, QUARTER, 1),
                lax.dynamic_slice_in_dim(up, first, QUARTER, 1),
                weights,
            ],
            0,
        )

    incoming = to_dom(gather_rows(x, slots, hub_feats.T))
    early = to_feat([early_part(k) for k in range(FEAT)])
    aggregate = forward(feat_ref, index, x, incoming, tile_coef, hub_coef)
    grad_parts, late_parts = dense(feat_ref, to_feat(aggregate), early)
    grad_agg = to_feat(grad_parts)
    halo_back, own_grad = tile_backward(feat_ref, index, grad_agg, tile_coef)
    returned = to_dom(hub_backward(feat_ref, grad_agg, hub_coef, halo_back))
    late = to_feat(late_parts)
    grad_feats, grad_hubs, output_rows = scatter_rows(feat_ref, slots, returned, own_grad, late)
    return (output_rows.T, grad_feats.T, grad_hubs.T)


def solution(mesh):
    return jax.shard_map(
        body,
        mesh=mesh,
        in_specs=(
            P("dom", "feat"),
            P("dom", "feat"),
            P("dom", None),
            P("dom", None, None),
            P("dom", None),
            P("dom", None, None),
            P("feat", None),
            P("feat", None),
            P("dom", "feat"),
        ),
        out_specs=(P("dom", "feat"), P("dom", "feat"), P("dom", "feat")),
        check_vma=False,
    )
```

time: 148 us -> 122 us (0.82)
  blocking collectives: 22.1 us -> 0 us
  waiting for transfers between devices: 43.9 us -> 51.4 us
  Pallas kernels: 41.3 us -> 35.9 us
  starting transfers between devices: 30.4 us -> 27.6 us
  other arithmetic: 2.71 us -> 0.06 us
  local copies, waits for them, and re-layouts: 6.02 us -> 4.41 us
    ppermute x0 -> x12, waiting for transfers between devices: none -> 31.8 us  [to_feat(): lax.ppermute(parts[k], 'feat', [(f, f ^ k) for f in range(FEAT)])]
    all_to_all x6 -> x2, waiting for transfers between devices: 43.9 us -> 19.5 us  [to_dom(): return lax.all_to_all(x, 'dom', split_axis=0, concat_axis=0, tiled=True)]
    all_to_all x2 -> x0, blocking collectives: 22.1 us -> none  [the longest x1 12.1 us: body(): grad_quarter, late_quarter = dense(to_feat(aggregate), early)]
    all_to_all x6 -> x2, starting transfers between devices: 30.4 us -> 13 us  [to_dom(): return lax.all_to_all(x, 'dom', split_axis=0, concat_axis=0, tiled=True)]
    ppermute x0 -> x12, starting transfers between devices: none -> 14.6 us  [to_feat(): lax.ppermute(parts[k], 'feat', [(f, f ^ k) for f in range(FEAT)])]
    pallas_call x5 -> x4, Pallas kernels: 28.3 us -> 22 us  [the longest x1 11.5 us: forward(): pl.pallas_call(forward_kernel, grid=(8,), out_shape=[jax.ShapeDtypeStruct...]
    reduce_sum x1 -> x0, other arithmetic: 1.74 us -> none  [body(): grad_hubs = jnp.sum(hub_arrived.astype(F32), 0)]
    broadcast_in_dim x2 -> x0, local copies, waits for them, and re-layouts: 1.69 us -> none  [the longest x1 1.67 us: body(): hubs = to_dom(jnp.broadcast_to(hub_feats.T[None], (DOM, COLS, TILE)))]
  transfers between devices with their start and end apart: 6 -> 14, of which waited for: 4 -> 7; matrix products, arithmetic and copies ran while one was open for 3% -> 0% of each run, Pallas kernels for 23% -> 10%
where the time goes in v2:
time: 122 us; the launch traced here: 120 us
  waiting for transfers between devices  51.4 us (42%)
  Pallas kernels  35.9 us (29%)
  starting transfers between devices  27.6 us (23%)
  local copies, waits for them, and re-layouts  4.41 us (4%)
    ppermute x12, waiting for transfers between devices, to_feat(): lax.ppermute(parts[k], 'feat', [(f, f ^ k) for f in range(FEAT)])  31.8 us
    all_to_all x2, waiting for transfers between devices, to_dom(): return lax.all_to_all(x, 'dom', split_axis=0, concat_axis=0, tiled=True)  19.5 us
    ppermute x12, starting transfers between devices, to_feat(): lax.ppermute(parts[k], 'feat', [(f, f ^ k) for f in range(FEAT)])  14.6 us
    all_to_all x2, starting transfers between devices, to_dom(): return lax.all_to_all(x, 'dom', split_axis=0, concat_axis=0, tiled=True)  13 us
    pallas_call x1, Pallas kernels, forward(): pl.pallas_call(forward_kernel, grid=(8,), out_shape=[jax.ShapeDtypeStruct...  11.5 us
    pallas_call x1, Pallas kernels, hub_backward(): pl.pallas_call(hub_backward_kernel, grid=(HUBS // step,), out_shape=jax.S...  10.4 us
    pallas_call x1, Pallas kernels, scatter_rows(): pl.pallas_call(scatter_kernel, out_shape=(jax.ShapeDtypeStruct((COLS, NOD...  4.97 us
    pallas_call x1, Pallas kernels, gather_rows(): pl.pallas_call(gather_kernel, out_shape=jax.ShapeDtypeStruct((DOM, 3, COL...  4.85 us
  transfers between devices with their start and end apart: 14, of which 7 were waited for; matrix products, arithmetic and copies ran while one was open for 0% of the time, Pallas kernels for 10%

profile of v2, /device:TPU:0, one launch (start us, length us, event | category | flops | bytes accessed | tf_op | source)
XLA Modules:
  0.0 120.1 jit_solution(10817713673674845340)
XLA Ops:
  0.6 0.9 copy-done.2
  3.1 4.8 %gather_rows.1 = bf16[32,3,64,128]{3,2,1,0:T(8,128)(2,1)} custom-call(bf16[64,2048]{1,0:T(8,128)(2,1)S(1)} %bitcast.24, s32[32,256]{1,0:T(8,128)S(1)} %bitcast.28, bf16[64,128]{1,0:T(8,128)(2,1)S(1)} %bitcast.30), custom_call_target="tpu_custom_call" | custom-call | flops 4000000000 | bytes 2097152 | tf_op jit(solution)/shard_map/gather_rows/pallas_call | solution.py:64
  7.9 8.9 %all-to-all-start = ((bf16[32,3,64,128]{3,2,1,0:T(8,128)(2,1)}), bf16[32,3,64,128]{3,2,1,0:T(8,128)(2,1)S(1)}, u32[]{:S(2)}, u32[]{:S(2)}) async-start(bf16[32,3,64,128]{3,2,1,0:T(8,128)(2,1)} %gather_rows.1), calls=%async_computation | async-start | bytes 3145728 | tf_op jit(solution)/shard_map/all_to_all | solution.py:313
  17.1 2.8 %collective-permute-start.5 = (bf16[192,512]{1,0:T(8,128)(2,1)S(1)}, bf16[192,512]{1,0:T(8,128)(2,1)S(1)}, u32[]{:S(2)}, u32[]{:S(2)}) collective-permute-start(bf16[192,512]{1,0:T(8,128)(2,1)S(1)} %get-tuple-element.45), channel_id=1, source_target_pairs={{0,3},{1,2},{2,1},{3,0},{4,7},{5,6},{6,5},{7,4},{8,11},{9,10},{10,... | collective-permute-start | bytes 589832 | tf_op jit(solution)/shard_map/ppermute | solution.py:318
  19.9 1.0 collective-permute-start.3
  20.9 19.5 %all-to-all-done.recv_ref = bf16[32,3,64,128]{3,2,1,0:T(8,128)(2,1)S(1)} async-done(((bf16[32,3,64,128]{3,2,1,0:T(8,128)(2,1)}), bf16[32,3,64,128]{3,2,1,0:T(8,128)(2,1)S(1)}, u32[]{:S(2)}, u32[]{:S(2)}) %all-to-all-start) | async-done | bytes 1572896 | tf_op jit(solution)/shard_map/all_to_all | solution.py:313
  40.4 1.9 %copy-done = bf16[96,128,128]{2,1,0:T(8,128)(2,1)S(1)} copy-done((bf16[96,128,128]{2,1,0:T(8,128)(2,1)S(1)}, bf16[96,128,128]{2,1,0:T(8,128)(2,1)}, u32[]{:S(2)}) %copy-start) | copy-done | bytes 3145752
  42.3 11.5 %forward.1 = (bf16[64,512]{1,0:T(8,128)(2,1)S(1)}, bf16[64,512]{1,0:T(8,128)(2,1)S(1)}, bf16[64,512]{1,0:T(8,128)(2,1)S(1)}, bf16[64,512]{1,0:T(8,128)(2,1)S(1)}) custom-call(s32[1]{0:T(128)} %bitcast.feat_ref, s32[2,96]{1,0:T(2,128)S(1)} %bitcast.26, bf16[64,2048]{1,0:T(8,128)(2,1)S(1)} %bitcast.25, bf16[32,3,64,128]{3,2,1,0:T(8,128)(2,1)S(1)} %all-to-all-done.recv_ref, ...), custom_call_target="tpu_custom_call" | custom-call | flops 3000000000 | bytes 16777216 | tf_op jit(solution)/shard_map/forward/pallas_call | solution.py:116
  53.9 3.7 %collective-permute-start.1 = (bf16[64,512]{1,0:T(8,128)(2,1)S(1)}, bf16[64,512]{1,0:T(8,128)(2,1)S(1)}, u32[]{:S(2)}, u32[]{:S(2)}) collective-permute-start(bf16[64,512]{1,0:T(8,128)(2,1)S(1)} %get-tuple-element.22), channel_id=1, source_target_pairs={{0,2},{1,3},{2,0},{3,1},{4,6},{5,7},{6,4},{7,5},{8,10},{9,11},{10,... | collective-permute-start | bytes 196616 | tf_op jit(solution)/shard_map/ppermute | solution.py:318
  57.6 2.6 %collective-permute-done.1.rest_2_ = bf16[64,512]{1,0:T(8,128)(2,1)S(1)} collective-permute-done((bf16[64,512]{1,0:T(8,128)(2,1)S(1)}, bf16[64,512]{1,0:T(8,128)(2,1)S(1)}, u32[]{:S(2)}, u32[]{:S(2)}) %collective-permute-start.1) | collective-permute-done | bytes 65568 | tf_op jit(solution)/shard_map/ppermute | solution.py:318
  60.2 2.9 %collective-permute-done.2.rest_3_ = bf16[64,512]{1,0:T(8,128)(2,1)S(1)} collective-permute-done((bf16[64,512]{1,0:T(8,128)(2,1)S(1)}, bf16[64,512]{1,0:T(8,128)(2,1)S(1)}, u32[]{:S(2)}, u32[]{:S(2)}) %collective-permute-start.2) | collective-permute-done | bytes 65568 | tf_op jit(solution)/shard_map/ppermute | solution.py:318
  63.1 0.8 dense.1
  64.1 1.4 %collective-permute-start.7 = (bf16[64,512]{1,0:T(8,128)(2,1)S(1)}, bf16[64,512]{1,0:T(8,128)(2,1)S(1)}, u32[]{:S(2)}, u32[]{:S(2)}) collective-permute-start(bf16[64,512]{1,0:T(8,128)(2,1)S(1)} %get-tuple-element.26), channel_id=1, source_target_pairs={{0,2},{1,3},{2,0},{3,1},{4,6},{5,7},{6,4},{7,5},{8,10},{9,11},{10,... | collective-permute-start | bytes 196616 | tf_op jit(solution)/shard_map/ppermute | solution.py:318
  65.6 1.8 %collective-permute-start.8 = (bf16[64,512]{1,0:T(8,128)(2,1)S(1)}, bf16[64,512]{1,0:T(8,128)(2,1)S(1)}, u32[]{:S(2)}, u32[]{:S(2)}) collective-permute-start(bf16[64,512]{1,0:T(8,128)(2,1)S(1)} %get-tuple-element.27), channel_id=1, source_target_pairs={{0,3},{1,2},{2,1},{3,0},{4,7},{5,6},{6,5},{7,4},{8,11},{9,10},{10,... | collective-permute-start | bytes 196616 | tf_op jit(solution)/shard_map/ppermute | solution.py:318
  67.3 2.6 %collective-permute-done.7.rest_2_ = bf16[64,512]{1,0:T(8,128)(2,1)S(1)} collective-permute-done((bf16[64,512]{1,0:T(8,128)(2,1)S(1)}, bf16[64,512]{1,0:T(8,128)(2,1)S(1)}, u32[]{:S(2)}, u32[]{:S(2)}) %collective-permute-start.7) | collective-permute-done | bytes 65568 | tf_op jit(solution)/shard_map/ppermute | solution.py:318
  70.0 1.4 %collective-permute-done.8.rest_3_ = bf16[64,512]{1,0:T(8,128)(2,1)S(1)} collective-permute-done((bf16[64,512]{1,0:T(8,128)(2,1)S(1)}, bf16[64,512]{1,0:T(8,128)(2,1)S(1)}, u32[]{:S(2)}, u32[]{:S(2)}) %collective-permute-start.8) | collective-permute-done | bytes 65568 | tf_op jit(solution)/shard_map/ppermute | solution.py:318
  71.4 3.5 %tile_backward.1 = (bf16[64,64,128]{2,1,0:T(8,128)(2,1)S(1)}, f32[64,2048]{1,0:T(8,128)S(1)}) custom-call(s32[1]{0:T(128)} %bitcast.feat_ref, s32[2,96]{1,0:T(2,128)S(1)} %bitcast.27, bf16[64,512]{1,0:T(8,128)(2,1)S(1)} %get-tuple-element.24.rest_0_, bf16[64,512]{1,0:T(8,128)(2,1)S(1)} %collective-permute-done.6.rest_1_, ...), custom_call_target="tpu_custom_call" | custom-call | flops 1000000000 | bytes 4194304 | tf_op jit(solution)/shard_map/tile_backward/pallas_call | solution.py:211
  74.8 10.4 %hub_backward.1 = bf16[32,3,64,128]{3,2,1,0:T(8,128)(2,1)} custom-call(s32[1]{0:T(128)} %bitcast.feat_ref, bf16[64,512]{1,0:T(8,128)(2,1)S(1)} %get-tuple-element.24.rest_0_, bf16[64,512]{1,0:T(8,128)(2,1)S(1)} %collective-permute-done.6.rest_1_, bf16[64,512]{1,0:T(8,128)(2,1)S(1)} %collective-permute-done.7.rest_2_, ...), custom_call_target="tpu_custom_call" | custom-call | flops 2000000000 | bytes 16777216 | tf_op jit(solution)/shard_map/hub_backward/pallas_call | solution.py:248
  85.2 4.1 %all-to-all-start.1 = ((bf16[32,3,64,128]{3,2,1,0:T(8,128)(2,1)}), bf16[32,3,64,128]{3,2,1,0:T(8,128)(2,1)S(1)}, u32[]{:S(2)}, u32[]{:S(2)}) async-start(bf16[32,3,64,128]{3,2,1,0:T(8,128)(2,1)} %hub_backward.1), calls=%async_computation.1 | async-start | bytes 3145728 | tf_op jit(solution)/shard_map/all_to_all | solution.py:313
  89.5 2.1 %collective-permute-start.10 = (bf16[128,512]{1,0:T(8,128)(2,1)S(1)}, bf16[128,512]{1,0:T(8,128)(2,1)S(1)}, u32[]{:S(2)}, u32[]{:S(2)}) collective-permute-start(bf16[128,512]{1,0:T(8,128)(2,1)S(1)} %get-tuple-element.32), channel_id=1, source_target_pairs={{0,2},{1,3},{2,0},{3,1},{4,6},{5,7},{6,4},{7,5},{8,10},{9,11},{10,... | collective-permute-start | bytes 393224 | tf_op jit(solution)/shard_map/ppermute | solution.py:318
  91.6 1.2 %collective-permute-start.11 = (bf16[128,512]{1,0:T(8,128)(2,1)S(1)}, bf16[128,512]{1,0:T(8,128)(2,1)S(1)}, u32[]{:S(2)}, u32[]{:S(2)}) collective-permute-start(bf16[128,512]{1,0:T(8,128)(2,1)S(1)} %get-tuple-element.33), channel_id=1, source_target_pairs={{0,3},{1,2},{2,1},{3,0},{4,7},{5,6},{6,5},{7,4},{8,11},{9,10},{10,... | collective-permute-start | bytes 393224 | tf_op jit(solution)/shard_map/ppermute | solution.py:318
  92.8 18.3 %collective-permute-done.10.rest_2_ = bf16[128,512]{1,0:T(8,128)(2,1)S(1)} collective-permute-done((bf16[128,512]{1,0:T(8,128)(2,1)S(1)}, bf16[128,512]{1,0:T(8,128)(2,1)S(1)}, u32[]{:S(2)}, u32[]{:S(2)}) %collective-permute-start.10) | collective-permute-done | bytes 131104 | tf_op jit(solution)/shard_map/ppermute | solution.py:318
  111.1 4.0 %collective-permute-done.11.rest_3_ = bf16[128,512]{1,0:T(8,128)(2,1)S(1)} collective-permute-done((bf16[128,512]{1,0:T(8,128)(2,1)S(1)}, bf16[128,512]{1,0:T(8,128)(2,1)S(1)}, u32[]{:S(2)}, u32[]{:S(2)}) %collective-permute-start.11) | collective-permute-done | bytes 131104 | tf_op jit(solution)/shard_map/ppermute | solution.py:318
  115.1 5.0 %scatter_rows.1 = (f32[64,2048]{1,0:T(8,128)}, f32[64,128]{1,0:T(8,128)}, bf16[64,2048]{1,0:T(8,128)(2,1)}) custom-call(s32[1]{0:T(128)} %bitcast.feat_ref, s32[32,256]{1,0:T(8,128)S(1)} %bitcast.29, bf16[32,3,64,128]{3,2,1,0:T(8,128)(2,1)S(1)} %all-to-all-done.1.recv_ref, f32[64,2048]{1,0:T(8,128)S(1)} %get-tuple-element.29.own_ref, ...), custom_call_target="tpu_custom_call" | custom-call | flops 4000000000 | bytes 2097152 | tf_op jit(solution)/shard_map/scatter_rows/pallas_call | solution.py:296
  (37 shorter events, 2.3 us)
Async XLA Ops:
  0.6 1.0 copy-start.2
  1.6 0.8 copy-start.5
  7.9 9.0 %copy-start.9 = (bf16[64,256]{1,0:T(8,128)(2,1)S(1)}, bf16[64,256]{1,0:T(8,128)(2,1)}, u32[]{:S(2)}) copy-start(bf16[64,256]{1,0:T(8,128)(2,1)} %param.15) | copy-start | bytes 98308
  7.9 9.0 %copy-start.10 = (bf16[64,256]{1,0:T(8,128)(2,1)S(1)}, bf16[64,256]{1,0:T(8,128)(2,1)}, u32[]{:S(2)}) copy-start(bf16[64,256]{1,0:T(8,128)(2,1)} %param.16) | copy-start | bytes 98308
  7.9 9.0 %copy-start.3 = (bf16[2048,64]{0,1:T(8,128)(2,1)S(1)}, bf16[2048,64]{0,1:T(8,128)(2,1)}, u32[]{:S(2)}) copy-start(bf16[2048,64]{0,1:T(8,128)(2,1)} %param.9) | copy-start | bytes 786436
  7.9 9.0 %copy-start.8 = (bf16[2048,64]{0,1:T(8,128)(2,1)S(1)}, bf16[2048,64]{0,1:T(8,128)(2,1)}, u32[]{:S(2)}) copy-start(bf16[2048,64]{0,1:T(8,128)(2,1)} %param.17) | copy-start | bytes 786436
  7.9 32.5 %all-to-all-start = ((bf16[32,3,64,128]{3,2,1,0:T(8,128)(2,1)}), bf16[32,3,64,128]{3,2,1,0:T(8,128)(2,1)S(1)}, u32[]{:S(2)}, u32[]{:S(2)}) async-start(bf16[32,3,64,128]{3,2,1,0:T(8,128)(2,1)} %gather_rows.1), calls=%async_computation | async-start | bytes 3145728 | tf_op jit(solution)/shard_map/all_to_all | solution.py:313
  16.8 23.6 %copy-start.4 = (s32[96,2]{0,1:T(2,128)S(1)}, s32[96,2]{0,1:T(2,128)}, u32[]{:S(2)}) copy-start(s32[96,2]{0,1:T(2,128)} %param.13) | copy-start | bytes 2308
  17.1 40.5 %collective-permute-start.5 = (bf16[192,512]{1,0:T(8,128)(2,1)S(1)}, bf16[192,512]{1,0:T(8,128)(2,1)S(1)}, u32[]{:S(2)}, u32[]{:S(2)}) collective-permute-start(bf16[192,512]{1,0:T(8,128)(2,1)S(1)} %get-tuple-element.45), channel_id=1, source_target_pairs={{0,3},{1,2},{2,1},{3,0},{4,7},{5,6},{6,5},{7,4},{8,11},{9,10},{10,... | collective-permute-start | bytes 589832 | tf_op jit(solution)/shard_map/ppermute | solution.py:318
  19.9 37.7 %collective-permute-start.3 = (bf16[192,512]{1,0:T(8,128)(2,1)S(1)}, bf16[192,512]{1,0:T(8,128)(2,1)S(1)}, u32[]{:S(2)}, u32[]{:S(2)}) collective-permute-start(bf16[192,512]{1,0:T(8,128)(2,1)S(1)} %get-tuple-element.46), channel_id=1, source_target_pairs={{0,1},{1,0},{2,3},{3,2},{4,5},{5,4},{6,7},{7,6},{8,9},{9,8},{10,11... | collective-permute-start | bytes 589832 | tf_op jit(solution)/shard_map/ppermute | solution.py:318
  20.8 36.8 %collective-permute-start.4 = (bf16[192,512]{1,0:T(8,128)(2,1)S(1)}, bf16[192,512]{1,0:T(8,128)(2,1)S(1)}, u32[]{:S(2)}, u32[]{:S(2)}) collective-permute-start(bf16[192,512]{1,0:T(8,128)(2,1)S(1)} %get-tuple-element.47), channel_id=1, source_target_pairs={{0,2},{1,3},{2,0},{3,1},{4,6},{5,7},{6,4},{7,5},{8,10},{9,11},{10,... | collective-permute-start | bytes 589832 | tf_op jit(solution)/shard_map/ppermute | solution.py:318
  40.4 1.9 %copy-start = (bf16[96,128,128]{2,1,0:T(8,128)(2,1)S(1)}, bf16[96,128,128]{2,1,0:T(8,128)(2,1)}, u32[]{:S(2)}) copy-start(bf16[96,128,128]{2,1,0:T(8,128)(2,1)} %rest_4_.2) | copy-start | bytes 9437188
  53.8 3.8 %collective-permute-start = (bf16[64,512]{1,0:T(8,128)(2,1)S(1)}, bf16[64,512]{1,0:T(8,128)(2,1)S(1)}, u32[]{:S(2)}, u32[]{:S(2)}) collective-permute-start(bf16[64,512]{1,0:T(8,128)(2,1)S(1)} %get-tuple-element.21), channel_id=1, source_target_pairs={{0,1},{1,0},{2,3},{3,2},{4,5},{5,4},{6,7},{7,6},{8,9},{9,8},{10,11... | collective-permute-start | bytes 196616 | tf_op jit(solution)/shard_map/ppermute | solution.py:318
  53.9 6.3 %collective-permute-start.1 = (bf16[64,512]{1,0:T(8,128)(2,1)S(1)}, bf16[64,512]{1,0:T(8,128)(2,1)S(1)}, u32[]{:S(2)}, u32[]{:S(2)}) collective-permute-start(bf16[64,512]{1,0:T(8,128)(2,1)S(1)} %get-tuple-element.22), channel_id=1, source_target_pairs={{0,2},{1,3},{2,0},{3,1},{4,6},{5,7},{6,4},{7,5},{8,10},{9,11},{10,... | collective-permute-start | bytes 196616 | tf_op jit(solution)/shard_map/ppermute | solution.py:318
  57.5 5.6 %collective-permute-start.2 = (bf16[64,512]{1,0:T(8,128)(2,1)S(1)}, bf16[64,512]{1,0:T(8,128)(2,1)S(1)}, u32[]{:S(2)}, u32[]{:S(2)}) collective-permute-start(bf16[64,512]{1,0:T(8,128)(2,1)S(1)} %get-tuple-element.23), channel_id=1, source_target_pairs={{0,3},{1,2},{2,1},{3,0},{4,7},{5,6},{6,5},{7,4},{8,11},{9,10},{10,... | collective-permute-start | bytes 196616 | tf_op jit(solution)/shard_map/ppermute | solution.py:318
  63.1 8.2 %copy-start.1 = (bf16[96,128,128]{2,1,0:T(8,128)(2,1)S(1)}, bf16[96,128,128]{2,1,0:T(8,128)(2,1)}, u32[]{:S(2)}) copy-start(bf16[96,128,128]{2,1,0:T(8,128)(2,1)} %rest_4_.2) | copy-start | bytes 9437188
  63.9 3.4 %collective-permute-start.6 = (bf16[64,512]{1,0:T(8,128)(2,1)S(1)}, bf16[64,512]{1,0:T(8,128)(2,1)S(1)}, u32[]{:S(2)}, u32[]{:S(2)}) collective-permute-start(bf16[64,512]{1,0:T(8,128)(2,1)S(1)} %get-tuple-element.25), channel_id=1, source_target_pairs={{0,1},{1,0},{2,3},{3,2},{4,5},{5,4},{6,7},{7,6},{8,9},{9,8},{10,11... | collective-permute-start | bytes 196616 | tf_op jit(solution)/shard_map/ppermute | solution.py:318
  64.1 5.9 %collective-permute-start.7 = (bf16[64,512]{1,0:T(8,128)(2,1)S(1)}, bf16[64,512]{1,0:T(8,128)(2,1)S(1)}, u32[]{:S(2)}, u32[]{:S(2)}) collective-permute-start(bf16[64,512]{1,0:T(8,128)(2,1)S(1)} %get-tuple-element.26), channel_id=1, source_target_pairs={{0,2},{1,3},{2,0},{3,1},{4,6},{5,7},{6,4},{7,5},{8,10},{9,11},{10,... | collective-permute-start | bytes 196616 | tf_op jit(solution)/shard_map/ppermute | solution.py:318
  65.6 5.8 %collective-permute-start.8 = (bf16[64,512]{1,0:T(8,128)(2,1)S(1)}, bf16[64,512]{1,0:T(8,128)(2,1)S(1)}, u32[]{:S(2)}, u32[]{:S(2)}) collective-permute-start(bf16[64,512]{1,0:T(8,128)(2,1)S(1)} %get-tuple-element.27), channel_id=1, source_target_pairs={{0,3},{1,2},{2,1},{3,0},{4,7},{5,6},{6,5},{7,4},{8,11},{9,10},{10,... | collective-permute-start | bytes 196616 | tf_op jit(solution)/shard_map/ppermute | solution.py:318
  85.2 29.9 %copy-start.6 = (s32[1,32,256]{2,1,0:T(8,128)S(1)}, s32[1,32,256]{2,1,0:T(8,128)}, u32[]{:S(2)}) copy-start(s32[1,32,256]{2,1,0:T(8,128)} %param.14) | copy-start | bytes 98308
  85.2 29.9 %all-to-all-start.1 = ((bf16[32,3,64,128]{3,2,1,0:T(8,128)(2,1)}), bf16[32,3,64,128]{3,2,1,0:T(8,128)(2,1)S(1)}, u32[]{:S(2)}, u32[]{:S(2)}) async-start(bf16[32,3,64,128]{3,2,1,0:T(8,128)(2,1)} %hub_backward.1), calls=%async_computation.1 | async-start | bytes 3145728 | tf_op jit(solution)/shard_map/all_to_all | solution.py:313
  89.3 3.5 %collective-permute-start.9 = (bf16[128,512]{1,0:T(8,128)(2,1)S(1)}, bf16[128,512]{1,0:T(8,128)(2,1)S(1)}, u32[]{:S(2)}, u32[]{:S(2)}) collective-permute-start(bf16[128,512]{1,0:T(8,128)(2,1)S(1)} %get-tuple-element.31), channel_id=1, source_target_pairs={{0,1},{1,0},{2,3},{3,2},{4,5},{5,4},{6,7},{7,6},{8,9},{9,8},{10,11... | collective-permute-start | bytes 393224 | tf_op jit(solution)/shard_map/ppermute | solution.py:318
  89.5 21.6 %collective-permute-start.10 = (bf16[128,512]{1,0:T(8,128)(2,1)S(1)}, bf16[128,512]{1,0:T(8,128)(2,1)S(1)}, u32[]{:S(2)}, u32[]{:S(2)}) collective-permute-start(bf16[128,512]{1,0:T(8,128)(2,1)S(1)} %get-tuple-element.32), channel_id=1, source_target_pairs={{0,2},{1,3},{2,0},{3,1},{4,6},{5,7},{6,4},{7,5},{8,10},{9,11},{10,... | collective-permute-start | bytes 393224 | tf_op jit(solution)/shard_map/ppermute | solution.py:318
  91.6 23.5 %collective-permute-start.11 = (bf16[128,512]{1,0:T(8,128)(2,1)S(1)}, bf16[128,512]{1,0:T(8,128)(2,1)S(1)}, u32[]{:S(2)}, u32[]{:S(2)}) collective-permute-start(bf16[128,512]{1,0:T(8,128)(2,1)S(1)} %get-tuple-element.33), channel_id=1, source_target_pairs={{0,3},{1,2},{2,1},{3,0},{4,7},{5,6},{6,5},{7,4},{8,11},{9,10},{10,... | collective-permute-start | bytes 393224 | tf_op jit(solution)/shard_map/ppermute | solution.py:318
  (1 other events, 0.7 us)

commit v3 on v0

v3 whole, which is shorter than its diff:
```python
import jax
import jax.numpy as jnp
from jax import lax
from jax.experimental import pallas as pl
from jax.experimental.pallas import tpu as pltpu
from jax.sharding import PartitionSpec as P

BF = jnp.bfloat16
F32 = jnp.float32
I32 = jnp.int32
NT = (((1,), (1,)), ((), ()))
NN = (((1,), (0,)), ((), ()))
TN = (((0,), (0,)), ((), ()))

COLS = 64
NODES = 2048
DOM = 32
FEAT = 4
SLOTS = 256
TILE = 128
TILES = 96
LOCAL_TILES = 32
OWN_TILES = NODES // TILE
RECV_TILES = DOM * SLOTS // TILE
HALF = NODES // 2
HALF_TILES = OWN_TILES // 2
LOW = 256
HIGH = NODES // LOW
HUBS = 4096
HID = FEAT * COLS
EARLY = 2 * COLS + COLS // 2

SPARE_TILES = 576
SPARE_SUMS = 288
SPARE_ROWS = 2304
LIST = 1024
LISTS = 4608

SMEM = pl.BlockSpec(memory_space=pltpu.SMEM)
ANY = pl.BlockSpec(memory_space=pl.ANY)


def dot(a, b, dims):
    return lax.dot_general(a, b, dims, preferred_element_type=F32)


def shape(*dims, dtype=BF):
    return jax.ShapeDtypeStruct(dims, dtype)


VMEM = pl.BlockSpec(memory_space=pltpu.VMEM)


def local_call(kernel, outs, args, name, places=(), scratch=(), flops=10**9, size=2**21, mib=14):
    places = dict(places)
    return pl.pallas_call(
        kernel,
        out_shape=outs,
        in_specs=[places.get(i, VMEM) for i in range(len(args))],
        out_specs=[places.get(100 + i, SMEM if o.dtype == I32 else VMEM) for i, o in enumerate(outs)],
        scratch_shapes=list(scratch),
        compiler_params=pltpu.CompilerParams(vmem_limit_bytes=mib * 1024 * 1024),
        cost_estimate=pl.CostEstimate(flops=flops, bytes_accessed=size, transcendentals=0),
        name=name,
    )(*args)


def one_hot(low):
    rows = lax.broadcasted_iota(I32, (LOW, low.shape[1]), 0)
    return jnp.where(rows == low, 1.0, 0.0).astype(BF)


def pack_kernel(feat_ref, x_ref, up_ref, self_ref, neigh_ref, keep_ref, send_ref):
    for k, out in enumerate((keep_ref, send_ref)):
        lanes = pl.ds(pl.multiple_of((feat_ref[0] ^ k) * HALF, HALF), HALF)
        out[:COLS] = x_ref[:, lanes]
        out[COLS : 2 * COLS] = up_ref[:, lanes]
        for part in range(2):
            half = slice(part * COLS // 2, (part + 1) * COLS // 2)
            out[2 * COLS :, 2 * part * HID : (2 * part + 1) * HID] = self_ref[half]
            out[2 * COLS :, (2 * part + 1) * HID : (2 * part + 2) * HID] = neigh_ref[half]


def pack(feat, x, up, self_weight, neigh_weight):
    return local_call(
        pack_kernel,
        [shape(EARLY, HALF)] * 2,
        [feat, x, up, self_weight, neigh_weight],
        "pack",
        places={0: SMEM},
        flops=0,
        mib=60,
    )


def gather_kernel(x_ref, slot_ref, hub_ref, out_ref, stacked):
    for b in range(HIGH):
        stacked[b * COLS : (b + 1) * COLS, :] = x_ref[:, b * LOW : (b + 1) * LOW]

    @pl.loop(0, DOM, unroll=16)
    def _(r):
        index = slot_ref[pl.ds(r, 1), :]
        high = index >> 8
        found = dot(stacked[...], one_hot(index & (LOW - 1)), NN)
        out = jnp.zeros((COLS, SLOTS), F32)
        for b in range(HIGH):
            out = jnp.where(high == b, found[b * COLS : (b + 1) * COLS], out)
        out = out.astype(BF)
        out_ref[r, 0] = out[:, :TILE]
        out_ref[r, 1] = out[:, TILE:]
        out_ref[r, 2] = hub_ref[...]


def gather_rows(x, slots, hubs):
    return local_call(
        gather_kernel,
        [shape(DOM, 3, COLS, TILE)],
        [x, slots, hubs],
        "gather_rows",
        scratch=[pltpu.VMEM((HIGH * COLS, LOW), BF)],
        flops=4 * 10**9,
        mib=60,
    )[0]


def prepare_kernel(index_ref, x_ref, tile_hbm, list_hbm, sorted_hbm, total_hbm, list_ref, total_ref, tile_ref, sems):
    copy = pltpu.make_async_copy(tile_hbm, tile_ref, sems.at[0])
    copy.start()
    copy.wait()

    def sort(c, count):
        source = index_ref[1, c]
        own = source < OWN_TILES
        to = jnp.where(own, RECV_TILES + jnp.minimum(count, LOCAL_TILES - 1), source - OWN_TILES)
        list_ref[to] = index_ref[0, c]
        list_ref[TILES + to] = c
        pltpu.make_async_copy(tile_ref.at[c], sorted_hbm.at[to], sems.at[1]).start()
        return count + own.astype(I32)

    lax.fori_loop(0, TILES, sort, jnp.int32(0))
    total_ref[...] = jnp.zeros_like(total_ref)
    group = 8

    @pl.loop(0, LOCAL_TILES // group)
    def _(g):
        products = []
        for k in range(group):
            place = RECV_TILES + g * group + k
            c = list_ref[TILES + place]
            s = jnp.minimum(index_ref[1, c], OWN_TILES - 1)
            list_ref[TILES + place] = s
            lanes = pl.ds(pl.multiple_of(s * TILE, TILE), TILE)
            products.append(dot(tile_ref[c], x_ref[:, lanes], NT))
        for k in range(group):
            d = list_ref[RECV_TILES + g * group + k]
            total_ref[d] = total_ref[d] + products[k]

    outs = [
        pltpu.make_async_copy(total_ref, total_hbm.at[pl.ds(0, OWN_TILES)], sems.at[2]),
        pltpu.make_async_copy(list_ref, list_hbm.at[0], sems.at[3]),
    ]
    for copy in outs:
        copy.start()
    for copy in outs:
        copy.wait()
    pltpu.make_async_copy(tile_ref, sorted_hbm.at[pl.ds(0, TILES)], sems.at[1]).wait()


def prepare(index, x, tiles):
    return local_call(
        prepare_kernel,
        [
            shape(LISTS, LIST, dtype=I32),
            shape(SPARE_TILES, TILE, TILE),
            shape(SPARE_SUMS, TILE, COLS, dtype=F32),
        ],
        [index, x, tiles],
        "prepare",
        places={0: SMEM, 2: ANY, 100: ANY, 101: ANY, 102: ANY},
        scratch=[
            pltpu.SMEM((LIST,), I32),
            pltpu.VMEM((OWN_TILES, TILE, COLS), F32),
            pltpu.VMEM((TILES, TILE, TILE), BF),
            pltpu.SemaphoreType.DMA((4,)),
        ],
        mib=60,
    )


HUB_STEPS = 4
HALF_ROWS = HALF // HUB_STEPS


def hub_row_copies(half, hub_hbm, hub_ref, sems):
    copies = []
    for i in range(HUB_STEPS):
        rows = pl.ds(pl.multiple_of(half * HALF + i * HALF_ROWS, HALF_ROWS), HALF_ROWS)
        part = pl.ds(i * HALF_ROWS, HALF_ROWS)
        copies.append(pltpu.make_async_copy(hub_hbm.at[rows], hub_ref.at[part], sems.at[i]))
    return copies


def add_hub_rows(copies, hub_ref, hubs, total, first_tile):
    tiles = HALF_ROWS // TILE
    for step in range(HUB_STEPS):
        copies[step].wait()
        part = dot(hub_ref[step * HALF_ROWS : (step + 1) * HALF_ROWS], hubs[...], NT)
        for k in range(tiles):
            t = first_tile + step * tiles + k
            total[t] = total[t] + part[k * TILE : (k + 1) * TILE]


def forward_send_kernel(feat_ref, list_hbm, recv_ref, tile_hbm, local_hbm, hub_hbm, *rest):
    send_ref, keep_ref, hubs, target_ref, tile_ref, total, hub_ref, sems = rest
    away = 1 - feat_ref[0]
    tile_copy = pltpu.make_async_copy(tile_hbm.at[pl.ds(0, RECV_TILES)], tile_ref, sems.at[HUB_STEPS])
    local_copy = pltpu.make_async_copy(local_hbm.at[pl.ds(0, OWN_TILES)], total, sems.at[HUB_STEPS + 1])
    list_copy = pltpu.make_async_copy(list_hbm.at[0], target_ref, sems.at[HUB_STEPS + 2])
    copies = hub_row_copies(away, hub_hbm, hub_ref, sems)
    for copy in (list_copy, tile_copy, local_copy):
        copy.start()
    for q in range(DOM):
        hubs[:, q * TILE : (q + 1) * TILE] = recv_ref[q, 2]
    for copy in copies:
        copy.start()
    list_copy.wait()
    tile_copy.wait()
    local_copy.wait()
    group = 16

    @pl.loop(0, RECV_TILES // group)
    def _(step):
        first = step * group
        products = [dot(tile_ref[first + k], recv_ref[first // 2 + k // 2, k % 2], NT) for k in range(group)]
        for k, product in enumerate(products):
            d = target_ref[first + k]
            total[d] = total[d] + product

    add_hub_rows(copies, hub_ref, hubs, total, away * HALF_TILES)
    for j in range(HALF_TILES):
        send_ref[:, j * TILE : (j + 1) * TILE] = total[away * HALF_TILES + j].T.astype(BF)
        keep_ref[j] = total[feat_ref[0] * HALF_TILES + j]


def forward_send(feat, target, recv, tiles, local, hub_coef):
    return local_call(
        forward_send_kernel,
        [shape(COLS, HALF), shape(HALF_TILES, TILE, COLS, dtype=F32), shape(COLS, HUBS)],
        [feat, target, recv, tiles, local, hub_coef],
        "forward_send",
        places={0: SMEM, 1: ANY, 3: ANY, 4: ANY, 5: ANY},
        scratch=[
            pltpu.SMEM((LIST,), I32),
            pltpu.VMEM((RECV_TILES, TILE, TILE), BF),
            pltpu.VMEM((OWN_TILES, TILE, COLS), F32),
            pltpu.VMEM((HALF, HUBS), BF),
            pltpu.SemaphoreType.DMA((HUB_STEPS + 3,)),
        ],
        flops=2 * 10**9,
        size=2**23,
        mib=47,
    )


def forward_keep_kernel(feat_ref, sum_ref, hubs, hub_hbm, keep_ref, total, hub_ref, sems):
    copies = hub_row_copies(feat_ref[0], hub_hbm, hub_ref, sems)
    for copy in copies:
        copy.start()
    total[...] = sum_ref[...]
    add_hub_rows(copies, hub_ref, hubs, total, 0)
    for j in range(HALF_TILES):
        keep_ref[:, j * TILE : (j + 1) * TILE] = total[j].T.astype(BF)


def forward_keep(feat, sums, hubs, hub_coef):
    return local_call(
        forward_keep_kernel,
        [shape(COLS, HALF)],
        [feat, sums, hubs, hub_coef],
        "forward_keep",
        places={0: SMEM, 3: ANY},
        scratch=[
            pltpu.VMEM(sums.shape, F32),
            pltpu.VMEM((HALF, HUBS), BF),
            pltpu.SemaphoreType.DMA((HUB_STEPS,)),
        ],
        size=2**23,
        mib=47,
    )[0]


def rows_of(feat_ref, k):
    return pl.ds(pl.multiple_of((feat_ref[0] * 2 + feat_ref[1] ^ k) * COLS, COLS), COLS)


def dense_kernel(feat_ref, *rest):
    aggs, earlies, outs, scratch = rest[:4], rest[4:8], rest[8:14], rest[14:]
    keep_grad, send_grad, grad_ref, self_ref, keep_out, send_out = outs
    agg, x, up, neigh_ref, output = scratch
    for k in range(FEAT):
        rows = rows_of(feat_ref, k)
        agg[rows] = aggs[k][...]
        x[rows] = earlies[k][:COLS]
        up[rows] = earlies[k][COLS : 2 * COLS]
        for part in range(2):
            packed = earlies[k][2 * COLS :, part * 2 * HID : (part + 1) * 2 * HID]
            first = (feat_ref[0] * 2 + feat_ref[1] ^ k) * COLS + part * COLS // 2
            half = pl.ds(pl.multiple_of(first, COLS // 2), COLS // 2)
            self_ref[half] = packed[:, :HID]
            neigh_ref[half] = packed[:, HID:]
    pre_act = dot(self_ref[...], x[...], TN) + dot(neigh_ref[...], agg[...], TN)
    fall = jnp.exp(jnp.minimum(pre_act, 0.0))
    output[...] = jnp.where(pre_act > 0, pre_act, fall - 1.0).astype(BF)
    slope = jnp.where(pre_act > 0, 1.0, fall)
    grad_pre = (up[...].astype(F32) * slope).astype(BF)
    grad_ref[...] = grad_pre
    weight = jnp.concatenate([neigh_ref[rows_of(feat_ref, 0)], neigh_ref[rows_of(feat_ref, 2)]], 0)
    grad_agg = dot(weight, grad_pre, NN).astype(BF)
    keep_grad[...] = grad_agg[:COLS]
    send_grad[...] = grad_agg[COLS:]
    keep_out[...] = output[rows_of(feat_ref, 0)]
    send_out[...] = output[rows_of(feat_ref, 2)]


def dense(feat, aggs, earlies):
    block = pltpu.VMEM((HID, HALF), BF)
    return local_call(
        dense_kernel,
        [shape(COLS, HALF)] * 2 + [shape(HID, HALF), shape(HID, HID)] + [shape(COLS, HALF)] * 2,
        [feat, *aggs, *earlies],
        "dense",
        places={0: SMEM},
        scratch=[block] * 3 + [pltpu.VMEM((HID, HID), BF), block],
    )


HUB_LANES = HUBS // HUB_STEPS


def hub_lane_copies(half, hub_hbm, hub_ref, sems):
    rows = pl.ds(pl.multiple_of(half * HALF, HALF), HALF)
    copies = []
    for i in range(HUB_STEPS):
        lanes = pl.ds(i * HUB_LANES, HUB_LANES)
        copies.append(pltpu.make_async_copy(hub_hbm.at[rows, lanes], hub_ref.at[:, lanes], sems.at[i]))
    return copies


def hub_backward_kernel(feat_ref, grad_ref, self_ref, pre_ref, hub_hbm, *rest):
    out_ref, keep_back, send_back, hub_ref, sems = rest
    copies = hub_lane_copies(feat_ref[0], hub_hbm, hub_ref, sems)
    for copy in copies:
        copy.start()
    weight = jnp.concatenate([self_ref[rows_of(feat_ref, 0)], self_ref[rows_of(feat_ref, 2)]], 0)
    back = dot(weight, pre_ref[...], NN).astype(BF)
    keep_back[...] = back[:COLS]
    send_back[...] = back[COLS:]
    for i, copy in enumerate(copies):
        copy.wait()
        lanes = slice(i * HUB_LANES, (i + 1) * HUB_LANES)
        out_ref[:, lanes] = dot(grad_ref[...], hub_ref[:, lanes], NN)


def hub_backward(feat, grad, self_weight, grad_pre, hub_coef):
    return local_call(
        hub_backward_kernel,
        [shape(COLS, HUBS, dtype=F32), shape(COLS, HALF), shape(COLS, HALF)],
        [feat, grad, self_weight, grad_pre, hub_coef],
        "hub_backward",
        places={0: SMEM, 4: ANY},
        scratch=[pltpu.VMEM((HALF, HUBS), BF), pltpu.SemaphoreType.DMA((HUB_STEPS,))],
        size=2**23,
        mib=47,
    )


def split_tiles(feat_ref, keep_ref, come_ref, grads):
    for k, part in enumerate((keep_ref, come_ref)):
        first = (feat_ref[0] ^ k) * HALF_TILES
        for j in range(HALF_TILES):
            grads[first + j] = part[:, j * TILE : (j + 1) * TILE]


def backward_kernel(feat_ref, list_hbm, keep_ref, come_ref, terms_hbm, tile_hbm, hub_hbm, *rest):
    out_ref, target_ref, grads, terms_ref, tile_ref, hub_ref, sems = rest
    group = RECV_TILES // HUB_STEPS
    doms = DOM // HUB_STEPS
    hub_parts = hub_lane_copies(1 - feat_ref[0], hub_hbm, hub_ref, sems)
    tile_parts, term_parts = [], []
    for i in range(HUB_STEPS):
        part = pl.ds(i * group, group)
        tile_parts.append(pltpu.make_async_copy(tile_hbm.at[part], tile_ref.at[part], sems.at[HUB_STEPS + i]))
        lanes = pl.ds(i * HUB_LANES, HUB_LANES)
        term_parts.append(
            pltpu.make_async_copy(terms_hbm.at[:, lanes], terms_ref.at[:, lanes], sems.at[2 * HUB_STEPS + i])
        )
    list_copy = pltpu.make_async_copy(list_hbm.at[0], target_ref, sems.at[3 * HUB_STEPS])
    list_copy.start()
    for copies in zip(tile_parts, hub_parts, term_parts):
        for copy in copies:
            copy.start()
    split_tiles(feat_ref, keep_ref, come_ref, grads)
    list_copy.wait()
    for step in range(HUB_STEPS):
        tile_parts[step].wait()
        for s in range(step * group, (step + 1) * group):
            out_ref[s // 2, s % 2] = dot(grads[target_ref[s]], tile_ref[s], NN).astype(BF)
        hub_parts[step].wait()
        term_parts[step].wait()
        lanes = slice(step * HUB_LANES, (step + 1) * HUB_LANES)
        terms = (terms_ref[:, lanes] + dot(come_ref[...], hub_ref[:, lanes], NN)).astype(BF)
        for k in range(doms):
            out_ref[step * doms + k, 2] = terms[:, k * TILE : (k + 1) * TILE]


def backward(feat, target, keep, come, terms, tiles, hub_coef):
    return local_call(
        backward_kernel,
        [shape(DOM, 3, COLS, TILE)],
        [feat, target, keep, come, terms, tiles, hub_coef],
        "backward",
        places={0: SMEM, 1: ANY, 4: ANY, 5: ANY, 6: ANY},
        scratch=[
            pltpu.SMEM((LIST,), I32),
            pltpu.VMEM((OWN_TILES, COLS, TILE), BF),
            pltpu.VMEM((COLS, HUBS), F32),
            pltpu.VMEM((RECV_TILES, TILE, TILE), BF),
            pltpu.VMEM((HALF, HUBS), BF),
            pltpu.SemaphoreType.DMA((3 * HUB_STEPS + 1,)),
        ],
        flops=2 * 10**9,
        size=2**23,
        mib=47,
    )[0]


def own_backward_kernel(feat_ref, list_hbm, keep_ref, come_ref, tile_hbm, own_hbm, *rest):
    list_ref, own_ref, grads, total, tile_ref, sems = rest
    copies = [
        pltpu.make_async_copy(list_hbm.at[0], list_ref, sems.at[0]),
        pltpu.make_async_copy(tile_hbm.at[pl.ds(RECV_TILES, LOCAL_TILES)], tile_ref, sems.at[1]),
    ]
    for copy in copies:
        copy.start()
    split_tiles(feat_ref, keep_ref, come_ref, grads)
    total[...] = jnp.zeros_like(total)
    for copy in copies:
        copy.wait()
    group = 8

    @pl.loop(0, LOCAL_TILES // group)
    def _(g):
        places = [RECV_TILES + g * group + k for k in range(group)]
        products = [dot(grads[list_ref[c]], tile_ref[c - RECV_TILES], NN) for c in places]
        for c, product in zip(places, products):
            s = list_ref[TILES + c]
            total[s] = total[s] + product

    for t in range(OWN_TILES):
        own_ref[:, t * TILE : (t + 1) * TILE] = total[t]
    out_copy = pltpu.make_async_copy(own_ref, own_hbm.at[pl.ds(0, COLS)], sems.at[2])
    out_copy.start()
    out_copy.wait()


def own_backward(feat, lists, keep, come, tiles):
    return local_call(
        own_backward_kernel,
        [shape(SPARE_ROWS, NODES, dtype=F32)],
        [feat, lists, keep, come, tiles],
        "own_backward",
        places={0: SMEM, 1: ANY, 4: ANY, 100: ANY},
        scratch=[
            pltpu.SMEM((LIST,), I32),
            pltpu.VMEM((COLS, NODES), F32),
            pltpu.VMEM((OWN_TILES, COLS, TILE), BF),
            pltpu.VMEM((OWN_TILES, COLS, TILE), F32),
            pltpu.VMEM((LOCAL_TILES, TILE, TILE), BF),
            pltpu.SemaphoreType.DMA((3,)),
        ],
        mib=60,
    )[0]


def scatter_kernel(feat_ref, slot_ref, recv_ref, own_hbm, keep_ref, come_ref, out_keep, out_come, *rest):
    grad_ref, hub_ref, output_ref, total, own_ref, sems = rest
    own_copy = pltpu.make_async_copy(own_hbm.at[pl.ds(0, COLS)], own_ref, sems.at[0])
    own_copy.start()
    total[...] = jnp.zeros_like(total)
    group = 16

    @pl.loop(0, DOM // group)
    def _(g):
        spread, hots = [], []
        for k in range(group):
            r = g * group + k
            index = slot_ref[pl.ds(r, 1), :]
            high = index >> 8
            rows = jnp.concatenate([recv_ref[r, 0], recv_ref[r, 1]], 1)
            spread.append(
                jnp.concatenate([jnp.where(high == b, rows, jnp.zeros_like(rows)) for b in range(HIGH)], 0)
            )
            hots.append(one_hot(index & (LOW - 1)))
        total[...] += dot(jnp.concatenate(spread, 1), jnp.concatenate(hots, 1), NT)

    hub = jnp.zeros((COLS, TILE), F32)
    for r in range(DOM):
        hub = hub + recv_ref[r, 2].astype(F32)
    hub_ref[...] = hub
    own_copy.wait()
    for b in range(HIGH):
        lanes = slice(b * LOW, (b + 1) * LOW)
        grad_ref[:, lanes] = total[b * COLS : (b + 1) * COLS] + own_ref[:, lanes]
    keep = pl.ds(pl.multiple_of(feat_ref[0] * HALF, HALF), HALF)
    come = pl.ds(pl.multiple_of((1 - feat_ref[0]) * HALF, HALF), HALF)
    grad_ref[:, keep] = grad_ref[:, keep] + keep_ref[...].astype(F32)
    grad_ref[:, come] = grad_ref[:, come] + come_ref[...].astype(F32)
    output_ref[:, keep] = out_keep[...]
    output_ref[:, come] = out_come[...]


def scatter_rows(feat, slots, recv, own, keep, come, out_keep, out_come):
    return local_call(
        scatter_kernel,
        [shape(COLS, NODES, dtype=F32), shape(COLS, TILE, dtype=F32), shape(COLS, NODES)],
        [feat, slots, recv, own, keep, come, out_keep, out_come],
        "scatter_rows",
        places={0: SMEM, 3: ANY},
        scratch=[
            pltpu.VMEM((HIGH * COLS, LOW), F32),
            pltpu.VMEM((COLS, NODES), F32),
            pltpu.SemaphoreType.DMA((1,)),
        ],
        mib=47,
    )


def to_dom(x):
    return lax.all_to_all(x, "dom", split_axis=0, concat_axis=0, tiled=True)


def swap(x, k):
    return lax.ppermute(x, "feat", [(f, f ^ k) for f in range(FEAT)])


def after(x, *others):
    return lax.optimization_barrier((x, *others))[0]


def body(
    features,
    hub_feats,
    hub_coef,
    tile_coef,
    tile_index,
    boundary_rows,
    self_weight,
    neigh_weight,
    out_grad,
):
    x = features.T
    up = out_grad.T
    slots = boundary_rows[0]
    index = tile_index.T
    place = lax.axis_index("feat")
    high = place // 2
    feat = jnp.stack([high, place % 2])

    outgoing = gather_rows(x, slots, hub_feats.T)
    incoming = to_dom(outgoing)
    x_in, up_in = lax.optimization_barrier((x, up, outgoing))[:2]
    early, early_send = pack(feat, x_in, up_in, self_weight, neigh_weight)
    early_2 = swap(early_send, 2)
    early_1 = swap(early, 1)
    lists, tiles, local_sum = prepare(index, x_in, tile_coef)
    agg_send, sums, hubs = forward_send(feat, lists, incoming, tiles, local_sum, hub_coef)
    agg_2 = swap(agg_send, 2)
    early_2 = after(early_2, agg_send)
    early = [early, early_1, early_2, swap(early_2, 1)]
    agg = forward_keep(feat, sums, hubs, hub_coef)
    grad, grad_send, grad_pre, self_weight, out_keep, out_send = dense(
        feat, [agg, swap(agg, 1), agg_2, swap(agg_2, 1)], early
    )
    grad_2 = swap(grad_send, 2)
    terms, back, back_send = hub_backward(feat, grad, self_weight, grad_pre, hub_coef)
    grad_2, back_send, out_send = lax.optimization_barrier((grad_2, back_send, out_send))
    back_2 = swap(back_send, 2)
    sums = backward(feat, lists, grad, grad_2, terms, tiles, hub_coef)
    sums, back_2, out_send = lax.optimization_barrier((sums, back_2, out_send))
    returned = to_dom(sums)
    out_2 = swap(out_send, 2)
    own_grad = own_backward(feat, lists, after(grad, sums), grad_2, tiles)
    grad_feats, grad_hubs, output_rows = scatter_rows(
        feat, slots, returned, own_grad, back, back_2, out_keep, out_2
    )
    return (output_rows.T, grad_feats.T, grad_hubs.T)


def solution(mesh):
    return jax.shard_map(
        body,
        mesh=mesh,
        in_specs=(
            P("dom", "feat"),
            P("dom", "feat"),
            P("dom", None),
            P("dom", None, None),
            P("dom", None),
            P("dom", None, None),
            P("feat", None),
            P("feat", None),
            P("dom", "feat"),
        ),
        out_specs=(P("dom", "feat"), P("dom", "feat"), P("dom", "feat")),
        check_vma=False,
    )
```

time: 376 us -> 105 us (0.28)
  blocking collectives: 91.5 us -> 0 us
  local copies, waits for them, and re-layouts: 63.1 us -> 0.7 us
  other arithmetic: 57.7 us -> 0.65 us
  waiting for transfers between devices: 81.3 us -> 30.1 us
  Pallas kernels: 0 us -> 45.2 us
  matrix products: 41.6 us -> 0 us
  between operations: 14.2 us -> 0.96 us
    all_gather x1 -> x0, blocking collectives: 91.5 us -> none  [body(): lax.all_gather(hub_feats, 'dom', axis=0, tiled=True)]
    scatter-add x1 -> x0, other arithmetic: 48 us -> none  [body(): returned = jnp.zeros((node_count + 1, feat_width), jnp.float32).at[flat_i...]
    pallas_call x0 -> x10, Pallas kernels: none -> 45.2 us  [local_call(): pl.pallas_call(kernel, out_shape=outs, in_specs=[places.get(i, VMEM) for...]
    dot_general x9 -> x0, matrix products: 41.6 us -> none  [the longest x1 13.6 us: body(): jnp.dot(aggregate, neigh_weight, preferred_element_type=jnp.float32)]
    gather x4 -> x0, local copies, waits for them, and re-layouts: 37.2 us -> none  [the longest x2 32 us: body(): jnp.take(features, jnp.maximum(slot_table, 0), axis=0)]
    reduce_scatter x1 -> x0, waiting for transfers between devices: 36.2 us -> none  [body(): lax.psum_scatter(partial_sum, 'feat', scatter_dimension=1, tiled=True)]
    all_gather x1 -> x0, waiting for transfers between devices: 20.3 us -> none  [body(): grad_full = lax.all_gather(grad_pre, 'feat', axis=1, tiled=True)]
    ppermute x0 -> x9, waiting for transfers between devices: none -> 16.7 us  [swap(): return lax.ppermute(x, 'feat', [(f, f ^ k) for f in range(FEAT)])]
  transfers between devices with their start and end apart: 5 -> 11, of which waited for: 3 -> 6; matrix products, arithmetic and copies ran while one was open for 6% -> 1% of each run, Pallas kernels for 0% -> 33%
where the time goes in v3:
time: 105 us; the launch traced here: 104 us
  Pallas kernels  45.2 us (43%)
  waiting for transfers between devices  30.1 us (29%)
  starting transfers between devices  26.5 us (25%)
    pallas_call x10, Pallas kernels, local_call(): pl.pallas_call(kernel, out_shape=outs, in_specs=[places.get(i, VMEM) for...  45.2 us
    ppermute x9, waiting for transfers between devices, swap(): return lax.ppermute(x, 'feat', [(f, f ^ k) for f in range(FEAT)])  16.7 us
    ppermute x9, starting transfers between devices, swap(): return lax.ppermute(x, 'feat', [(f, f ^ k) for f in range(FEAT)])  13.8 us
    all_to_all x2, waiting for transfers between devices, to_dom(): return lax.all_to_all(x, 'dom', split_axis=0, concat_axis=0, tiled=True)  13.5 us
    all_to_all x2, starting transfers between devices, to_dom(): return lax.all_to_all(x, 'dom', split_axis=0, concat_axis=0, tiled=True)  12.7 us
  transfers between devices with their start and end apart: 11, of which 6 were waited for; matrix products, arithmetic and copies ran while one was open for 1% of the time, Pallas kernels for 33%

profile of v3, /device:TPU:0, one launch (start us, length us, event | category | flops | bytes accessed | tf_op | source)
XLA Modules:
  0.0 104.2 jit_solution(1318601719516479841)
XLA Ops:
  0.6 4.9 %gather_rows.1 = bf16[32,3,64,128]{3,2,1,0:T(8,128)(2,1)} custom-call(bf16[64,2048]{1,0:T(8,128)(2,1)} %bitcast.13, s32[32,256]{1,0:T(8,128)} %bitcast.10, bf16[64,128]{1,0:T(8,128)(2,1)} %bitcast.19), custom_call_target="tpu_custom_call" | custom-call | flops 4000000000 | bytes 2097152 | tf_op jit(solution)/shard_map/gather_rows/pallas_call | solution.py:56
  5.6 8.8 %all-to-all-start = ((bf16[32,3,64,128]{3,2,1,0:T(8,128)(2,1)}), bf16[32,3,64,128]{3,2,1,0:T(8,128)(2,1)S(1)}, u32[]{:S(2)}, u32[]{:S(2)}) async-start(bf16[32,3,64,128]{3,2,1,0:T(8,128)(2,1)} %gather_rows.1), calls=%async_computation | async-start | bytes 3145728 | tf_op jit(solution)/shard_map/all_to_all | solution.py:539
  14.3 0.7 pad_add_fusion.feat_ref
  15.0 1.9 %pack.1 = (bf16[160,1024]{1,0:T(8,128)(2,1)}, bf16[160,1024]{1,0:T(8,128)(2,1)}) custom-call(s32[2]{0:T(128)} %pad_add_fusion.feat_ref, bf16[64,2048]{1,0:T(8,128)(2,1)} %bitcast.14, bf16[64,2048]{1,0:T(8,128)(2,1)} %bitcast.12, bf16[64,256]{1,0:T(8,128)(2,1)} %self_ref.1, bf16[64,256]{1,0:T(8,128)(2,1)} %neigh_ref.1), custom_call_target="tpu_custom_call" | custom-call | bytes 2097152 | tf_op jit(solution)/shard_map/pack/pallas_call | solution.py:56
  16.9 3.6 %collective-permute-start.4 = (bf16[160,1024]{1,0:T(8,128)(2,1)}, bf16[160,1024]{1,0:T(8,128)(2,1)S(1)}, u32[]{:S(2)}, u32[]{:S(2)}) collective-permute-start(bf16[160,1024]{1,0:T(8,128)(2,1)} %get-tuple-element.42), channel_id=1, source_target_pairs={{0,2},{1,3},{2,0},{3,1},{4,6},{5,7},{6,4},{7,5},{8,10},{9,11},{10,... | collective-permute-start | bytes 983048 | tf_op jit(solution)/shard_map/ppermute | solution.py:543
  20.5 6.1 %prepare.1 = (s32[4608,1024]{1,0:T(8,128)}, bf16[576,128,128]{2,1,0:T(8,128)(2,1)}, f32[288,128,64]{2,1,0:T(8,128)}) custom-call(s32[2,96]{1,0:T(2,128)} %bitcast.20, bf16[64,2048]{1,0:T(8,128)(2,1)} %bitcast.15, bf16[96,128,128]{2,1,0:T(8,128)(2,1)} %tile_hbm.1), custom_call_target="tpu_custom_call" | custom-call | flops 1000000000 | bytes 2097152 | tf_op jit(solution)/shard_map/prepare/pallas_call | solution.py:56
  26.7 11.3 %all-to-all-done.recv_ref = bf16[32,3,64,128]{3,2,1,0:T(8,128)(2,1)S(1)} async-done(((bf16[32,3,64,128]{3,2,1,0:T(8,128)(2,1)}), bf16[32,3,64,128]{3,2,1,0:T(8,128)(2,1)S(1)}, u32[]{:S(2)}, u32[]{:S(2)}) %all-to-all-start) | async-done | bytes 1572896 | tf_op jit(solution)/shard_map/all_to_all | solution.py:539
  37.9 0.7 copy-done.3
  38.6 6.6 %forward_send.1 = (bf16[64,1024]{1,0:T(8,128)(2,1)S(1)}, f32[8,128,64]{2,1,0:T(8,128)S(1)}, bf16[64,4096]{1,0:T(8,128)(2,1)S(1)}) custom-call(s32[2]{0:T(128)S(1)} %copy-done.3, s32[4608,1024]{1,0:T(8,128)} %get-tuple-element.34.list_hbm, bf16[32,3,64,128]{3,2,1,0:T(8,128)(2,1)S(1)} %all-to-all-done.recv_ref, ...), custom_call_target="tpu_custom_call" | custom-call | flops 2000000000 | bytes 8388608 | tf_op jit(solution)/shard_map/forward_send/pallas_call | solution.py:56
  45.3 3.7 %collective-permute-start.1 = (bf16[64,1024]{1,0:T(8,128)(2,1)S(1)}, bf16[64,1024]{1,0:T(8,128)(2,1)S(1)}, u32[]{:S(2)}, u32[]{:S(2)}) collective-permute-start(bf16[64,1024]{1,0:T(8,128)(2,1)S(1)} %get-tuple-element.39), channel_id=1, source_target_pairs={{0,2},{1,3},{2,0},{3,1},{4,6},{5,7},{6,4},{7,5},{8,10},{9,11},{10,... | collective-permute-start | bytes 393224 | tf_op jit(solution)/shard_map/ppermute | solution.py:543
  49.0 5.0 %forward_keep.1.rest_0_ = bf16[64,1024]{1,0:T(8,128)(2,1)S(1)} custom-call(s32[2]{0:T(128)S(1)} %copy-done.3, f32[8,128,64]{2,1,0:T(8,128)S(1)} %get-tuple-element.37.sum_ref, bf16[64,4096]{1,0:T(8,128)(2,1)S(1)} %get-tuple-element.38.hubs, bf16[2048,4096]{1,0:T(8,128)(2,1)} %hub_hbm.7), custom_call_target="tpu_custom_call" | custom-call | flops 1000000000 | bytes 8388608 | tf_op jit(solution)/shard_map/forward_keep/pallas_call | solution.py:56
  54.6 0.8 collective-permute-done.rest_1_
  55.6 1.4 %dense.1 = (bf16[64,1024]{1,0:T(8,128)(2,1)S(1)}, bf16[64,1024]{1,0:T(8,128)(2,1)S(1)}, bf16[256,1024]{1,0:T(8,128)(2,1)S(1)}, bf16[256,256]{1,0:T(8,128)(2,1)S(...) custom-call(s32[2]{0:T(128)S(1)} %copy-done.3, bf16[64,1024]{1,0:T(8,128)(2,1)S(1)} %forward_keep.1.rest_0_, ...), custom_call_target="tpu_custom_call" | custom-call | flops 1000000000 | bytes 2097152 | tf_op jit(solution)/shard_map/dense/pallas_call | solution.py:56
  57.1 2.1 %collective-permute-start.6 = (bf16[64,1024]{1,0:T(8,128)(2,1)S(1)}, bf16[64,1024]{1,0:T(8,128)(2,1)S(1)}, u32[]{:S(2)}, u32[]{:S(2)}) collective-permute-start(bf16[64,1024]{1,0:T(8,128)(2,1)S(1)} %get-tuple-element.45), channel_id=1, source_target_pairs={{0,2},{1,3},{2,0},{3,1},{4,6},{5,7},{6,4},{7,5},{8,10},{9,11},{10,... | collective-permute-start | bytes 393224 | tf_op jit(solution)/shard_map/ppermute | solution.py:543
  59.2 4.6 %hub_backward.1 = (f32[64,4096]{1,0:T(8,128)S(1)}, bf16[64,1024]{1,0:T(8,128)(2,1)S(1)}, bf16[64,1024]{1,0:T(8,128)(2,1)S(1)}) custom-call(s32[2]{0:T(128)S(1)} %copy-done.3, bf16[64,1024]{1,0:T(8,128)(2,1)S(1)} %get-tuple-element.55.grad_ref.keep_ref, bf16[256,256]{1,0:T(8,128)(2,1)S(1)} %get-tuple-element.46.self_ref, ...), custom_call_target="tpu_custom_call" | custom-call | flops 1000000000 | bytes 8388608 | tf_op jit(solution)/shard_map/hub_backward/pallas_call | solution.py:56
  63.8 0.6 collective-permute-done.6.come_ref
  64.4 1.8 %collective-permute-start.7 = (bf16[64,1024]{1,0:T(8,128)(2,1)S(1)}, bf16[64,1024]{1,0:T(8,128)(2,1)S(1)}, u32[]{:S(2)}, u32[]{:S(2)}) collective-permute-start(bf16[64,1024]{1,0:T(8,128)(2,1)S(1)} %get-tuple-element.52), channel_id=1, source_target_pairs={{0,2},{1,3},{2,0},{3,1},{4,6},{5,7},{6,4},{7,5},{8,10},{9,11},{10,... | collective-permute-start | bytes 393224 | tf_op jit(solution)/shard_map/ppermute | solution.py:543
  66.2 6.4 %backward.1 = bf16[32,3,64,128]{3,2,1,0:T(8,128)(2,1)} custom-call(s32[2]{0:T(128)S(1)} %copy-done.3, s32[4608,1024]{1,0:T(8,128)} %get-tuple-element.34.list_hbm, bf16[64,1024]{1,0:T(8,128)(2,1)S(1)} %get-tuple-element.55.grad_ref.keep_ref, bf16[64,1024]{1,0:T(8,128)(2,1)S(1)} %collective-permute-done.6.come_ref, ...), custom_call_target="tpu_custom_call" | custom-call | flops 2000000000 | bytes 8388608 | tf_op jit(solution)/shard_map/backward/pallas_call | solution.py:56
  72.7 4.0 %all-to-all-start.1 = ((bf16[32,3,64,128]{3,2,1,0:T(8,128)(2,1)}), bf16[32,3,64,128]{3,2,1,0:T(8,128)(2,1)S(1)}, u32[]{:S(2)}, u32[]{:S(2)}) async-start(bf16[32,3,64,128]{3,2,1,0:T(8,128)(2,1)} %backward.1), calls=%async_computation.1 | async-start | bytes 3145728 | tf_op jit(solution)/shard_map/all_to_all | solution.py:539
  76.7 1.9 %collective-permute-start.8 = (bf16[64,1024]{1,0:T(8,128)(2,1)S(1)}, bf16[64,1024]{1,0:T(8,128)(2,1)S(1)}, u32[]{:S(2)}, u32[]{:S(2)}) collective-permute-start(bf16[64,1024]{1,0:T(8,128)(2,1)S(1)} %get-tuple-element.59), channel_id=1, source_target_pairs={{0,2},{1,3},{2,0},{3,1},{4,6},{5,7},{6,4},{7,5},{8,10},{9,11},{10,... | collective-permute-start | bytes 393224 | tf_op jit(solution)/shard_map/ppermute | solution.py:543
  78.6 3.9 %own_backward.1.own_hbm = f32[2304,2048]{1,0:T(8,128)} custom-call(s32[2]{0:T(128)} %pad_add_fusion.feat_ref, s32[4608,1024]{1,0:T(8,128)} %get-tuple-element.34.list_hbm, bf16[64,1024]{1,0:T(8,128)(2,1)} %copy-done, bf16[64,1024]{1,0:T(8,128)(2,1)} %copy-done.1, bf16[576,128,128]{2,1,0:T(8,128)(2,1)} %get-tuple-element.35.tile_hbm), custom_call_target="tpu_custom_call" | custom-call | flops 1000000000 | bytes 2097152 | tf_op jit(solution)/shard_map/own_backward/pallas_call | solution.py:56
  82.5 15.0 %collective-permute-done.8.out_come = bf16[64,1024]{1,0:T(8,128)(2,1)S(1)} collective-permute-done((bf16[64,1024]{1,0:T(8,128)(2,1)S(1)}, bf16[64,1024]{1,0:T(8,128)(2,1)S(1)}, u32[]{:S(2)}, u32[]{:S(2)}) %collective-permute-start.8) | collective-permute-done | bytes 131104 | tf_op jit(solution)/shard_map/ppermute | solution.py:543
  97.6 2.2 %all-to-all-done.1.recv_ref = bf16[32,3,64,128]{3,2,1,0:T(8,128)(2,1)S(1)} async-done(((bf16[32,3,64,128]{3,2,1,0:T(8,128)(2,1)}), bf16[32,3,64,128]{3,2,1,0:T(8,128)(2,1)S(1)}, u32[]{:S(2)}, u32[]{:S(2)}) %all-to-all-start.1) | async-done | bytes 1572896 | tf_op jit(solution)/shard_map/all_to_all | solution.py:539
  99.8 4.2 %scatter_rows.1 = (f32[64,2048]{1,0:T(8,128)}, f32[64,128]{1,0:T(8,128)}, bf16[64,2048]{1,0:T(8,128)(2,1)}) custom-call(s32[2]{0:T(128)S(1)} %copy-done.4, s32[32,256]{1,0:T(8,128)S(1)} %bitcast.11, bf16[32,3,64,128]{3,2,1,0:T(8,128)(2,1)S(1)} %all-to-all-done.1.recv_ref, f32[2304,2048]{1,0:T(8,128)} %own_backward.1.own_hbm, ...), custom_call_target="tpu_custom_call" | custom-call | flops 1000000000 | bytes 2097152 | tf_op jit(solution)/shard_map/scatter_rows/pallas_call | solution.py:56
  (21 shorter events, 0.9 us)
Async XLA Ops:
  5.6 32.4 %all-to-all-start = ((bf16[32,3,64,128]{3,2,1,0:T(8,128)(2,1)}), bf16[32,3,64,128]{3,2,1,0:T(8,128)(2,1)S(1)}, u32[]{:S(2)}, u32[]{:S(2)}) async-start(bf16[32,3,64,128]{3,2,1,0:T(8,128)(2,1)} %gather_rows.1), calls=%async_computation | async-start | bytes 3145728 | tf_op jit(solution)/shard_map/all_to_all | solution.py:539
  16.9 28.3 %collective-permute-start.4 = (bf16[160,1024]{1,0:T(8,128)(2,1)}, bf16[160,1024]{1,0:T(8,128)(2,1)S(1)}, u32[]{:S(2)}, u32[]{:S(2)}) collective-permute-start(bf16[160,1024]{1,0:T(8,128)(2,1)} %get-tuple-element.42), channel_id=1, source_target_pairs={{0,2},{1,3},{2,0},{3,1},{4,6},{5,7},{6,4},{7,5},{8,10},{9,11},{10,... | collective-permute-start | bytes 983048 | tf_op jit(solution)/shard_map/ppermute | solution.py:543
  20.5 34.1 %collective-permute-start.3 = (bf16[160,1024]{1,0:T(8,128)(2,1)}, bf16[160,1024]{1,0:T(8,128)(2,1)S(1)}, u32[]{:S(2)}, u32[]{:S(2)}) collective-permute-start(bf16[160,1024]{1,0:T(8,128)(2,1)} %get-tuple-element.41.rest_4_), channel_id=1, source_target_pairs={{0,1},{1,0},{2,3},{3,2},{4,5},{5,4},{6,7},{7,6},{8,9},{9,8},{10,11... | collective-permute-start | bytes 983048 | tf_op jit(solution)/shard_map/ppermute | solution.py:543
  37.9 0.7 copy-start.3
  45.2 10.4 %copy-start.5 = (bf16[160,1024]{1,0:T(8,128)(2,1)S(1)}, bf16[160,1024]{1,0:T(8,128)(2,1)}, u32[]{:S(2)}) copy-start(bf16[160,1024]{1,0:T(8,128)(2,1)} %get-tuple-element.41.rest_4_) | copy-start | bytes 983044
  45.2 10.4 %collective-permute-start.5 = (bf16[160,1024]{1,0:T(8,128)(2,1)S(1)}, bf16[160,1024]{1,0:T(8,128)(2,1)S(1)}, u32[]{:S(2)}, u32[]{:S(2)}) collective-permute-start(bf16[160,1024]{1,0:T(8,128)(2,1)S(1)} %collective-permute-done.4.rest_6_), channel_id=1, source_target_pairs={{0,1},{1,0},{2,3},{3,2},{4,5},{5,4},{6,7},{7,6},{8,9},{9,8},{10,11... | collective-permute-start | bytes 983048 | tf_op jit(solution)/shard_map/ppermute | solution.py:543
  45.3 8.9 %collective-permute-start.1 = (bf16[64,1024]{1,0:T(8,128)(2,1)S(1)}, bf16[64,1024]{1,0:T(8,128)(2,1)S(1)}, u32[]{:S(2)}, u32[]{:S(2)}) collective-permute-start(bf16[64,1024]{1,0:T(8,128)(2,1)S(1)} %get-tuple-element.39), channel_id=1, source_target_pairs={{0,2},{1,3},{2,0},{3,1},{4,6},{5,7},{6,4},{7,5},{8,10},{9,11},{10,... | collective-permute-start | bytes 393224 | tf_op jit(solution)/shard_map/ppermute | solution.py:543
  54.0 1.4 %collective-permute-start = (bf16[64,1024]{1,0:T(8,128)(2,1)S(1)}, bf16[64,1024]{1,0:T(8,128)(2,1)S(1)}, u32[]{:S(2)}, u32[]{:S(2)}) collective-permute-start(bf16[64,1024]{1,0:T(8,128)(2,1)S(1)} %forward_keep.1.rest_0_), channel_id=1, source_target_pairs={{0,1},{1,0},{2,3},{3,2},{4,5},{5,4},{6,7},{7,6},{8,9},{9,8},{10,11... | collective-permute-start | bytes 393224 | tf_op jit(solution)/shard_map/ppermute | solution.py:543
  54.3 1.4 %collective-permute-start.2 = (bf16[64,1024]{1,0:T(8,128)(2,1)S(1)}, bf16[64,1024]{1,0:T(8,128)(2,1)S(1)}, u32[]{:S(2)}, u32[]{:S(2)}) collective-permute-start(bf16[64,1024]{1,0:T(8,128)(2,1)S(1)} %collective-permute-done.1.rest_2_), channel_id=1, source_target_pairs={{0,1},{1,0},{2,3},{3,2},{4,5},{5,4},{6,7},{7,6},{8,9},{9,8},{10,11... | collective-permute-start | bytes 393224 | tf_op jit(solution)/shard_map/ppermute | solution.py:543
  57.1 15.6 %copy-start = (bf16[64,1024]{1,0:T(8,128)(2,1)}, bf16[64,1024]{1,0:T(8,128)(2,1)S(1)}, u32[]{:S(2)}) copy-start(bf16[64,1024]{1,0:T(8,128)(2,1)S(1)} %get-tuple-element.55.grad_ref.keep_ref) | copy-start | bytes 393220
  57.1 7.3 %collective-permute-start.6 = (bf16[64,1024]{1,0:T(8,128)(2,1)S(1)}, bf16[64,1024]{1,0:T(8,128)(2,1)S(1)}, u32[]{:S(2)}, u32[]{:S(2)}) collective-permute-start(bf16[64,1024]{1,0:T(8,128)(2,1)S(1)} %get-tuple-element.45), channel_id=1, source_target_pairs={{0,2},{1,3},{2,0},{3,1},{4,6},{5,7},{6,4},{7,5},{8,10},{9,11},{10,... | collective-permute-start | bytes 393224 | tf_op jit(solution)/shard_map/ppermute | solution.py:543
  64.4 8.3 %copy-start.1 = (bf16[64,1024]{1,0:T(8,128)(2,1)}, bf16[64,1024]{1,0:T(8,128)(2,1)S(1)}, u32[]{:S(2)}) copy-start(bf16[64,1024]{1,0:T(8,128)(2,1)S(1)} %collective-permute-done.6.come_ref) | copy-start | bytes 393220
  64.4 8.3 %collective-permute-start.7 = (bf16[64,1024]{1,0:T(8,128)(2,1)S(1)}, bf16[64,1024]{1,0:T(8,128)(2,1)S(1)}, u32[]{:S(2)}, u32[]{:S(2)}) collective-permute-start(bf16[64,1024]{1,0:T(8,128)(2,1)S(1)} %get-tuple-element.52), channel_id=1, source_target_pairs={{0,2},{1,3},{2,0},{3,1},{4,6},{5,7},{6,4},{7,5},{8,10},{9,11},{10,... | collective-permute-start | bytes 393224 | tf_op jit(solution)/shard_map/ppermute | solution.py:543
  72.7 27.1 %all-to-all-start.1 = ((bf16[32,3,64,128]{3,2,1,0:T(8,128)(2,1)}), bf16[32,3,64,128]{3,2,1,0:T(8,128)(2,1)S(1)}, u32[]{:S(2)}, u32[]{:S(2)}) async-start(bf16[32,3,64,128]{3,2,1,0:T(8,128)(2,1)} %backward.1), calls=%async_computation.1 | async-start | bytes 3145728 | tf_op jit(solution)/shard_map/all_to_all | solution.py:539
  76.7 23.1 %copy-start.2 = (s32[1,32,256]{2,1,0:T(8,128)S(1)}, s32[1,32,256]{2,1,0:T(8,128)}, u32[]{:S(2)}) copy-start(s32[1,32,256]{2,1,0:T(8,128)} %param.14) | copy-start | bytes 98308
  76.7 23.1 %copy-start.4 = (s32[2]{0:T(128)S(1)}, s32[2]{0:T(128)}, u32[]{:S(2)}) copy-start(s32[2]{0:T(128)} %pad_add_fusion.feat_ref) | copy-start | bytes 28
  76.7 20.9 %collective-permute-start.8 = (bf16[64,1024]{1,0:T(8,128)(2,1)S(1)}, bf16[64,1024]{1,0:T(8,128)(2,1)S(1)}, u32[]{:S(2)}, u32[]{:S(2)}) collective-permute-start(bf16[64,1024]{1,0:T(8,128)(2,1)S(1)} %get-tuple-element.59), channel_id=1, source_target_pairs={{0,2},{1,3},{2,0},{3,1},{4,6},{5,7},{6,4},{7,5},{8,10},{9,11},{10,... | collective-permute-start | bytes 393224 | tf_op jit(solution)/shard_map/ppermute | solution.py:543

commit v4 on v3

v4 whole, which is shorter than its diff:
```python
import jax
import jax.numpy as jnp
from jax import lax
from jax.experimental import pallas as pl
from jax.experimental.pallas import tpu as pltpu
from jax.sharding import PartitionSpec as P

BF = jnp.bfloat16
F32 = jnp.float32
I32 = jnp.int32
NT = (((1,), (1,)), ((), ()))
NN = (((1,), (0,)), ((), ()))
TN = (((0,), (0,)), ((), ()))

COLS = 64
NODES = 2048
DOM = 32
FEAT = 4
SLOTS = 256
TILE = 128
TILES = 96
LOCAL_TILES = 32
OWN_TILES = NODES // TILE
RECV_TILES = DOM * SLOTS // TILE
HALF = NODES // 2
HALF_TILES = OWN_TILES // 2
LOW = 256
HIGH = NODES // LOW
HUBS = 4096
HID = FEAT * COLS
EARLY = 2 * COLS + COLS // 2

SPARE_TILES = 576
SPARE_SUMS = 288
SPARE_ROWS = 2304
LIST = 1024
LISTS = 4608

SMEM = pl.BlockSpec(memory_space=pltpu.SMEM)
ANY = pl.BlockSpec(memory_space=pl.ANY)


def dot(a, b, dims):
    return lax.dot_general(a, b, dims, preferred_element_type=F32)


def shape(*dims, dtype=BF):
    return jax.ShapeDtypeStruct(dims, dtype)


VMEM = pl.BlockSpec(memory_space=pltpu.VMEM)


def local_call(kernel, outs, args, name, places=(), scratch=(), flops=10**9, size=2**21, mib=14):
    places = dict(places)
    return pl.pallas_call(
        kernel,
        out_shape=outs,
        in_specs=[places.get(i, VMEM) for i in range(len(args))],
        out_specs=[places.get(100 + i, SMEM if o.dtype == I32 else VMEM) for i, o in enumerate(outs)],
        scratch_shapes=list(scratch),
        compiler_params=pltpu.CompilerParams(vmem_limit_bytes=mib * 1024 * 1024),
        cost_estimate=pl.CostEstimate(flops=flops, bytes_accessed=size, transcendentals=0),
        name=name,
    )(*args)


def one_hot(low):
    rows = lax.broadcasted_iota(I32, (LOW, low.shape[1]), 0)
    return jnp.where(rows == low, 1.0, 0.0).astype(BF)


def pack_kernel(x_ref, up_ref, self_ref, neigh_ref, keep_ref, send_ref):
    for k, out in enumerate((keep_ref, send_ref)):
        lanes = pl.ds(pl.multiple_of((chip() ^ k) * HALF, HALF), HALF)
        out[:COLS] = x_ref[:, lanes]
        out[COLS : 2 * COLS] = up_ref[:, lanes]
        for part in range(2):
            half = slice(part * COLS // 2, (part + 1) * COLS // 2)
            out[2 * COLS :, 2 * part * HID : (2 * part + 1) * HID] = self_ref[half]
            out[2 * COLS :, (2 * part + 1) * HID : (2 * part + 2) * HID] = neigh_ref[half]


def pack(x, up, self_weight, neigh_weight):
    return local_call(
        pack_kernel,
        [shape(EARLY, HALF)] * 2,
        [x, up, self_weight, neigh_weight],
        "pack",
        places={},
        flops=0,
        mib=60,
    )


def gather_kernel(x_ref, slot_ref, hub_ref, out_ref, stacked):
    for b in range(HIGH):
        stacked[b * COLS : (b + 1) * COLS, :] = x_ref[:, b * LOW : (b + 1) * LOW]

    @pl.loop(0, DOM, unroll=16)
    def _(r):
        index = slot_ref[pl.ds(r, 1), :]
        high = index >> 8
        found = dot(stacked[...], one_hot(index & (LOW - 1)), NN)
        out = jnp.zeros((COLS, SLOTS), F32)
        for b in range(HIGH):
            out = jnp.where(high == b, found[b * COLS : (b + 1) * COLS], out)
        out = out.astype(BF)
        out_ref[r, 0] = out[:, :TILE]
        out_ref[r, 1] = out[:, TILE:]
        out_ref[r, 2] = hub_ref[...]


def gather_rows(x, slots, hubs):
    return local_call(
        gather_kernel,
        [shape(DOM, 3, COLS, TILE)],
        [x, slots, hubs],
        "gather_rows",
        scratch=[pltpu.VMEM((HIGH * COLS, LOW), BF)],
        flops=4 * 10**9,
        mib=60,
    )[0]


def prepare_kernel(index_ref, x_ref, tile_hbm, list_hbm, sorted_hbm, total_hbm, list_ref, total_ref, tile_ref, sems):
    copy = pltpu.make_async_copy(tile_hbm, tile_ref, sems.at[0])
    copy.start()
    copy.wait()

    def sort(c, count):
        source = index_ref[1, c]
        own = source < OWN_TILES
        to = jnp.where(own, RECV_TILES + jnp.minimum(count, LOCAL_TILES - 1), source - OWN_TILES)
        list_ref[to] = index_ref[0, c]
        list_ref[TILES + to] = c
        pltpu.make_async_copy(tile_ref.at[c], sorted_hbm.at[to], sems.at[1]).start()
        return count + own.astype(I32)

    lax.fori_loop(0, TILES, sort, jnp.int32(0))
    total_ref[...] = jnp.zeros_like(total_ref)
    group = 8

    @pl.loop(0, LOCAL_TILES // group)
    def _(g):
        products = []
        for k in range(group):
            place = RECV_TILES + g * group + k
            c = list_ref[TILES + place]
            s = jnp.minimum(index_ref[1, c], OWN_TILES - 1)
            list_ref[TILES + place] = s
            lanes = pl.ds(pl.multiple_of(s * TILE, TILE), TILE)
            products.append(dot(tile_ref[c], x_ref[:, lanes], NT))
        for k in range(group):
            d = list_ref[RECV_TILES + g * group + k]
            total_ref[d] = total_ref[d] + products[k]

    outs = [
        pltpu.make_async_copy(total_ref, total_hbm.at[pl.ds(0, OWN_TILES)], sems.at[2]),
        pltpu.make_async_copy(list_ref, list_hbm.at[0], sems.at[3]),
    ]
    for copy in outs:
        copy.start()
    for copy in outs:
        copy.wait()
    pltpu.make_async_copy(tile_ref, sorted_hbm.at[pl.ds(0, TILES)], sems.at[1]).wait()


def prepare(index, x, tiles):
    return local_call(
        prepare_kernel,
        [
            shape(LISTS, LIST, dtype=I32),
            shape(SPARE_TILES, TILE, TILE),
            shape(SPARE_SUMS, TILE, COLS, dtype=F32),
        ],
        [index, x, tiles],
        "prepare",
        places={0: SMEM, 2: ANY, 100: ANY, 101: ANY, 102: ANY},
        scratch=[
            pltpu.SMEM((LIST,), I32),
            pltpu.VMEM((OWN_TILES, TILE, COLS), F32),
            pltpu.VMEM((TILES, TILE, TILE), BF),
            pltpu.SemaphoreType.DMA((4,)),
        ],
        mib=60,
    )


HUB_STEPS = 4
HALF_ROWS = HALF // HUB_STEPS


def half_rows(half, step):
    return pl.ds(pl.multiple_of(half * HALF + step * HALF_ROWS, HALF_ROWS), HALF_ROWS)


def add_hub_rows(hub_ref, half, step, hubs, total, first_tile):
    tiles = HALF_ROWS // TILE
    part = dot(hub_ref[half_rows(half, step)], hubs[...], NT)
    for k in range(tiles):
        t = first_tile + step * tiles + k
        total[t] = total[t] + part[k * TILE : (k + 1) * TILE]


def forward_send_kernel(list_hbm, recv_ref, tile_hbm, local_hbm, hub_hbm, *rest):
    send_ref, keep_ref, hubs, hub_ref, target_ref, tile_ref, total, sems = rest
    away = 1 - chip()
    firsts = [
        pltpu.make_async_copy(src, dst, sems.at[2 * HUB_STEPS + i])
        for i, (src, dst) in enumerate(
            (
                (list_hbm.at[0], target_ref),
                (tile_hbm.at[pl.ds(0, RECV_TILES)], tile_ref),
                (local_hbm.at[pl.ds(0, OWN_TILES)], total),
            )
        )
    ]
    copies = []
    for h, half in enumerate((away, chip())):
        for i in range(HUB_STEPS):
            rows = half_rows(half, i)
            copies.append(pltpu.make_async_copy(hub_hbm.at[rows], hub_ref.at[rows], sems.at[h * HUB_STEPS + i]))
    for copy in firsts + copies:
        copy.start()
    for q in range(DOM):
        hubs[:, q * TILE : (q + 1) * TILE] = recv_ref[q, 2]
    for copy in firsts:
        copy.wait()
    group = 16

    @pl.loop(0, RECV_TILES // group)
    def _(step):
        first = step * group
        products = [dot(tile_ref[first + k], recv_ref[first // 2 + k // 2, k % 2], NT) for k in range(group)]
        for k, product in enumerate(products):
            d = target_ref[first + k]
            total[d] = total[d] + product

    for step in range(HUB_STEPS):
        copies[step].wait()
        add_hub_rows(hub_ref, away, step, hubs, total, away * HALF_TILES)
    for j in range(HALF_TILES):
        send_ref[:, j * TILE : (j + 1) * TILE] = total[away * HALF_TILES + j].T.astype(BF)
        keep_ref[j] = total[chip() * HALF_TILES + j]
    for copy in copies[HUB_STEPS:]:
        copy.wait()


def forward_send(lists, recv, tiles, local, hub_coef):
    return local_call(
        forward_send_kernel,
        [
            shape(COLS, HALF),
            shape(HALF_TILES, TILE, COLS, dtype=F32),
            shape(COLS, HUBS),
            shape(NODES, HUBS),
        ],
        [lists, recv, tiles, local, hub_coef],
        "forward_send",
        places={0: ANY, 2: ANY, 3: ANY, 4: ANY},
        scratch=[
            pltpu.SMEM((LIST,), I32),
            pltpu.VMEM((RECV_TILES, TILE, TILE), BF),
            pltpu.VMEM((OWN_TILES, TILE, COLS), F32),
            pltpu.SemaphoreType.DMA((2 * HUB_STEPS + 3,)),
        ],
        flops=2 * 10**9,
        size=2**24,
        mib=34,
    )


def forward_keep_kernel(sum_ref, hubs, hub_ref, keep_ref, total):
    total[...] = sum_ref[...]
    for step in range(HUB_STEPS):
        add_hub_rows(hub_ref, chip(), step, hubs, total, 0)
    for j in range(HALF_TILES):
        keep_ref[:, j * TILE : (j + 1) * TILE] = total[j].T.astype(BF)


def forward_keep(sums, hubs, hub):
    return local_call(
        forward_keep_kernel,
        [shape(COLS, HALF)],
        [sums, hubs, hub],
        "forward_keep",
        places={},
        scratch=[pltpu.VMEM(sums.shape, F32)],
        size=2**23,
        mib=20,
    )[0]


def chip():
    return lax.axis_index("feat") // 2


def rows_of(k):
    return pl.ds(pl.multiple_of((lax.axis_index("feat") ^ k) * COLS, COLS), COLS)


def dense_kernel(*rest):
    aggs, earlies, outs, scratch = rest[:4], rest[4:8], rest[8:14], rest[14:]
    keep_grad, send_grad, grad_ref, self_ref, keep_out, send_out = outs
    agg, x, up, neigh_ref, output = scratch
    for k in range(FEAT):
        rows = rows_of(k)
        agg[rows] = aggs[k][...]
        x[rows] = earlies[k][:COLS]
        up[rows] = earlies[k][COLS : 2 * COLS]
        for part in range(2):
            packed = earlies[k][2 * COLS :, part * 2 * HID : (part + 1) * 2 * HID]
            first = (lax.axis_index("feat") ^ k) * COLS + part * COLS // 2
            half = pl.ds(pl.multiple_of(first, COLS // 2), COLS // 2)
            self_ref[half] = packed[:, :HID]
            neigh_ref[half] = packed[:, HID:]
    pre_act = dot(self_ref[...], x[...], TN) + dot(neigh_ref[...], agg[...], TN)
    fall = jnp.exp(jnp.minimum(pre_act, 0.0))
    output[...] = jnp.where(pre_act > 0, pre_act, fall - 1.0).astype(BF)
    slope = jnp.where(pre_act > 0, 1.0, fall)
    grad_pre = (up[...].astype(F32) * slope).astype(BF)
    grad_ref[...] = grad_pre
    weight = jnp.concatenate([neigh_ref[rows_of(0)], neigh_ref[rows_of(2)]], 0)
    grad_agg = dot(weight, grad_pre, NN).astype(BF)
    keep_grad[...] = grad_agg[:COLS]
    send_grad[...] = grad_agg[COLS:]
    keep_out[...] = output[rows_of(0)]
    send_out[...] = output[rows_of(2)]


def dense(aggs, earlies):
    block = pltpu.VMEM((HID, HALF), BF)
    return local_call(
        dense_kernel,
        [shape(COLS, HALF)] * 2 + [shape(HID, HALF), shape(HID, HID)] + [shape(COLS, HALF)] * 2,
        [*aggs, *earlies],
        "dense",
        places={},
        scratch=[block] * 3 + [pltpu.VMEM((HID, HID), BF), block],
    )


HUB_LANES = HUBS // HUB_STEPS


def hub_part(half, step):
    return pl.ds(pl.multiple_of(half * HALF, HALF), HALF), slice(step * HUB_LANES, (step + 1) * HUB_LANES)


def hub_backward_kernel(grad_ref, self_ref, pre_ref, hub_ref, out_ref, keep_back, send_back):
    weight = jnp.concatenate([self_ref[rows_of(0)], self_ref[rows_of(2)]], 0)
    back = dot(weight, pre_ref[...], NN).astype(BF)
    keep_back[...] = back[:COLS]
    send_back[...] = back[COLS:]
    for step in range(HUB_STEPS):
        rows, lanes = hub_part(chip(), step)
        out_ref[:, lanes] = dot(grad_ref[...], hub_ref[rows, lanes], NN)


def hub_backward(grad, self_weight, grad_pre, hub):
    return local_call(
        hub_backward_kernel,
        [shape(COLS, HUBS, dtype=F32), shape(COLS, HALF), shape(COLS, HALF)],
        [grad, self_weight, grad_pre, hub],
        "hub_backward",
        places={},
        size=2**23,
        mib=20,
    )


def split_tiles(keep_ref, come_ref, grads):
    for k, part in enumerate((keep_ref, come_ref)):
        first = (chip() ^ k) * HALF_TILES
        for j in range(HALF_TILES):
            grads[first + j] = part[:, j * TILE : (j + 1) * TILE]


def backward_kernel(list_hbm, keep_ref, come_ref, terms_ref, tile_hbm, hub_ref, *rest):
    out_ref, target_ref, grads, tile_ref, sems = rest
    group = RECV_TILES // HUB_STEPS
    doms = DOM // HUB_STEPS
    list_copy = pltpu.make_async_copy(list_hbm.at[0], target_ref, sems.at[HUB_STEPS])
    list_copy.start()
    copies = []
    for i in range(HUB_STEPS):
        part = pl.ds(i * group, group)
        copies.append(pltpu.make_async_copy(tile_hbm.at[part], tile_ref.at[part], sems.at[i]))
        copies[i].start()
    split_tiles(keep_ref, come_ref, grads)
    list_copy.wait()
    for step in range(HUB_STEPS):
        rows, lanes = hub_part(1 - chip(), step)
        terms = (terms_ref[:, lanes] + dot(come_ref[...], hub_ref[rows, lanes], NN)).astype(BF)
        for k in range(doms):
            out_ref[step * doms + k, 2] = terms[:, k * TILE : (k + 1) * TILE]
        copies[step].wait()
        for s in range(step * group, (step + 1) * group):
            out_ref[s // 2, s % 2] = dot(grads[target_ref[s]], tile_ref[s], NN).astype(BF)


def backward(lists, keep, come, terms, tiles, hub):
    return local_call(
        backward_kernel,
        [shape(DOM, 3, COLS, TILE)],
        [lists, keep, come, terms, tiles, hub],
        "backward",
        places={0: ANY, 4: ANY},
        scratch=[
            pltpu.SMEM((LIST,), I32),
            pltpu.VMEM((OWN_TILES, COLS, TILE), BF),
            pltpu.VMEM((RECV_TILES, TILE, TILE), BF),
            pltpu.SemaphoreType.DMA((HUB_STEPS + 1,)),
        ],
        flops=2 * 10**9,
        size=2**23,
        mib=20,
    )[0]


def own_backward_kernel(list_hbm, keep_ref, come_ref, tile_hbm, own_hbm, *rest):
    list_ref, own_ref, grads, total, tile_ref, sems = rest
    copies = [
        pltpu.make_async_copy(list_hbm.at[0], list_ref, sems.at[0]),
        pltpu.make_async_copy(tile_hbm.at[pl.ds(RECV_TILES, LOCAL_TILES)], tile_ref, sems.at[1]),
    ]
    for copy in copies:
        copy.start()
    split_tiles(keep_ref, come_ref, grads)
    total[...] = jnp.zeros_like(total)
    for copy in copies:
        copy.wait()
    group = 8

    @pl.loop(0, LOCAL_TILES // group)
    def _(g):
        places = [RECV_TILES + g * group + k for k in range(group)]
        products = [dot(grads[list_ref[c]], tile_ref[c - RECV_TILES], NN) for c in places]
        for c, product in zip(places, products):
            s = list_ref[TILES + c]
            total[s] = total[s] + product

    for t in range(OWN_TILES):
        own_ref[:, t * TILE : (t + 1) * TILE] = total[t]
    out_copy = pltpu.make_async_copy(own_ref, own_hbm.at[pl.ds(0, COLS)], sems.at[2])
    out_copy.start()
    out_copy.wait()


def own_backward(lists, keep, come, tiles):
    return local_call(
        own_backward_kernel,
        [shape(SPARE_ROWS, NODES, dtype=F32)],
        [lists, keep, come, tiles],
        "own_backward",
        places={0: ANY, 3: ANY, 100: ANY},
        scratch=[
            pltpu.SMEM((LIST,), I32),
            pltpu.VMEM((COLS, NODES), F32),
            pltpu.VMEM((OWN_TILES, COLS, TILE), BF),
            pltpu.VMEM((OWN_TILES, COLS, TILE), F32),
            pltpu.VMEM((LOCAL_TILES, TILE, TILE), BF),
            pltpu.SemaphoreType.DMA((3,)),
        ],
        mib=60,
    )[0]


def scatter_kernel(slot_ref, recv_ref, own_hbm, keep_ref, come_ref, out_keep, out_come, *rest):
    grad_ref, hub_ref, output_ref, total, own_ref, sems = rest
    own_copy = pltpu.make_async_copy(own_hbm.at[pl.ds(0, COLS)], own_ref, sems.at[0])
    own_copy.start()
    total[...] = jnp.zeros_like(total)
    group = 16

    @pl.loop(0, DOM // group)
    def _(g):
        spread, hots = [], []
        for k in range(group):
            r = g * group + k
            index = slot_ref[pl.ds(r, 1), :]
            high = index >> 8
            rows = jnp.concatenate([recv_ref[r, 0], recv_ref[r, 1]], 1)
            spread.append(
                jnp.concatenate([jnp.where(high == b, rows, jnp.zeros_like(rows)) for b in range(HIGH)], 0)
            )
            hots.append(one_hot(index & (LOW - 1)))
        total[...] += dot(jnp.concatenate(spread, 1), jnp.concatenate(hots, 1), NT)

    hub = jnp.zeros((COLS, TILE), F32)
    for r in range(DOM):
        hub = hub + recv_ref[r, 2].astype(F32)
    hub_ref[...] = hub
    own_copy.wait()
    for b in range(HIGH):
        lanes = slice(b * LOW, (b + 1) * LOW)
        grad_ref[:, lanes] = total[b * COLS : (b + 1) * COLS] + own_ref[:, lanes]
    keep = pl.ds(pl.multiple_of(chip() * HALF, HALF), HALF)
    come = pl.ds(pl.multiple_of((1 - chip()) * HALF, HALF), HALF)
    grad_ref[:, keep] = grad_ref[:, keep] + keep_ref[...].astype(F32)
    grad_ref[:, come] = grad_ref[:, come] + come_ref[...].astype(F32)
    output_ref[:, keep] = out_keep[...]
    output_ref[:, come] = out_come[...]


def scatter_rows(slots, recv, own, keep, come, out_keep, out_come):
    return local_call(
        scatter_kernel,
        [shape(COLS, NODES, dtype=F32), shape(COLS, TILE, dtype=F32), shape(COLS, NODES)],
        [slots, recv, own, keep, come, out_keep, out_come],
        "scatter_rows",
        places={2: ANY},
        scratch=[
            pltpu.VMEM((HIGH * COLS, LOW), F32),
            pltpu.VMEM((COLS, NODES), F32),
            pltpu.SemaphoreType.DMA((1,)),
        ],
        mib=47,
    )


def to_dom(x):
    return lax.all_to_all(x, "dom", split_axis=0, concat_axis=0, tiled=True)


def swap(x, k):
    return lax.ppermute(x, "feat", [(f, f ^ k) for f in range(FEAT)])


def after(x, *others):
    return lax.optimization_barrier((x, *others))[0]


def body(
    features,
    hub_feats,
    hub_coef,
    tile_coef,
    tile_index,
    boundary_rows,
    self_weight,
    neigh_weight,
    out_grad,
):
    x = features.T
    up = out_grad.T
    slots = boundary_rows[0]
    index = tile_index.T

    outgoing = gather_rows(x, slots, hub_feats.T)
    incoming = to_dom(outgoing)
    x_in, up_in = lax.optimization_barrier((x, up, outgoing))[:2]
    early, early_send = pack(x_in, up_in, self_weight, neigh_weight)
    early_2 = swap(early_send, 2)
    early_1 = swap(early, 1)
    lists, tiles, local_sum = prepare(index, x_in, tile_coef)
    agg_send, sums, hubs, hub = forward_send(lists, incoming, tiles, local_sum, hub_coef)
    agg_2 = swap(agg_send, 2)
    early_2 = after(early_2, agg_send)
    early = [early, early_1, early_2, swap(early_2, 1)]
    agg = forward_keep(sums, hubs, hub)
    grad, grad_send, grad_pre, self_weight, out_keep, out_send = dense(
        [agg, swap(agg, 1), agg_2, swap(agg_2, 1)], early
    )
    grad_2 = swap(grad_send, 2)
    terms, back, back_send = hub_backward(grad, self_weight, grad_pre, hub)
    back_2 = swap(back_send, 2)
    sums = backward(lists, grad, grad_2, terms, tiles, hub)
    sums, back_2, out_send = lax.optimization_barrier((sums, back_2, out_send))
    returned = to_dom(sums)
    out_2 = swap(out_send, 2)
    own_grad = own_backward(lists, after(grad, sums), grad_2, tiles)
    grad_feats, grad_hubs, output_rows = scatter_rows(
        slots, returned, own_grad, back, back_2, out_keep, out_2
    )
    return (output_rows.T, grad_feats.T, grad_hubs.T)


def solution(mesh):
    return jax.shard_map(
        body,
        mesh=mesh,
        in_specs=(
            P("dom", "feat"),
            P("dom", "feat"),
            P("dom", None),
            P("dom", None, None),
            P("dom", None),
            P("dom", None, None),
            P("feat", None),
            P("feat", None),
            P("dom", "feat"),
        ),
        out_specs=(P("dom", "feat"), P("dom", "feat"), P("dom", "feat")),
        check_vma=False,
    )
```

time: 105 us -> 98.4 us (0.937)
  Pallas kernels: 45.2 us -> 37 us
  waiting for transfers between devices: 30.1 us -> 32 us
  starting transfers between devices: 26.5 us -> 28 us
    pallas_call x10, Pallas kernels: 45.2 us -> 37 us  [local_call(): pl.pallas_call(kernel, out_shape=outs, in_specs=[places.get(i, VMEM) for...]
    all_to_all x2, waiting for transfers between devices: 13.5 us -> 16.3 us  [to_dom(): return lax.all_to_all(x, 'dom', split_axis=0, concat_axis=0, tiled=True)]
    ppermute x9, starting transfers between devices: 13.8 us -> 15.1 us  [swap(): return lax.ppermute(x, 'feat', [(f, f ^ k) for f in range(FEAT)])]
  transfers between devices with their start and end apart: 11 -> 11, of which waited for: 6 -> 7; matrix products, arithmetic and copies ran while one was open for 1% -> 0% of each run, Pallas kernels for 33% -> 28%
where the time goes in v4:
time: 98.4 us; the launch traced here: 98 us
  Pallas kernels  37 us (38%)
  waiting for transfers between devices  32 us (33%)
  starting transfers between devices  28 us (28%)
    pallas_call x10, Pallas kernels, local_call(): pl.pallas_call(kernel, out_shape=outs, in_specs=[places.get(i, VMEM) for...  37 us
    all_to_all x2, waiting for transfers between devices, to_dom(): return lax.all_to_all(x, 'dom', split_axis=0, concat_axis=0, tiled=True)  16.3 us
    ppermute x9, waiting for transfers between devices, swap(): return lax.ppermute(x, 'feat', [(f, f ^ k) for f in range(FEAT)])  15.8 us
    ppermute x9, starting transfers between devices, swap(): return lax.ppermute(x, 'feat', [(f, f ^ k) for f in range(FEAT)])  15.1 us
    all_to_all x2, starting transfers between devices, to_dom(): return lax.all_to_all(x, 'dom', split_axis=0, concat_axis=0, tiled=True)  12.9 us
  transfers between devices with their start and end apart: 11, of which 7 were waited for; matrix products, arithmetic and copies ran while one was open for 0% of the time, Pallas kernels for 28%

profile of v4, /device:TPU:0, one launch (start us, length us, event | category | flops | bytes accessed | tf_op | source)
XLA Modules:
  0.0 98.0 jit_solution(7419262970290495963)
XLA Ops:
  0.6 4.9 %gather_rows.1 = bf16[32,3,64,128]{3,2,1,0:T(8,128)(2,1)} custom-call(bf16[64,2048]{1,0:T(8,128)(2,1)} %bitcast.11, s32[32,256]{1,0:T(8,128)} %bitcast.8, bf16[64,128]{1,0:T(8,128)(2,1)} %bitcast.17), custom_call_target="tpu_custom_call" | custom-call | flops 4000000000 | bytes 2097152 | tf_op jit(solution)/shard_map/gather_rows/pallas_call | solution.py:56
  5.6 8.8 %all-to-all-start = ((bf16[32,3,64,128]{3,2,1,0:T(8,128)(2,1)}), bf16[32,3,64,128]{3,2,1,0:T(8,128)(2,1)S(1)}, u32[]{:S(2)}, u32[]{:S(2)}) async-start(bf16[32,3,64,128]{3,2,1,0:T(8,128)(2,1)} %gather_rows.1), calls=%async_computation | async-start | bytes 3145728 | tf_op jit(solution)/shard_map/all_to_all | solution.py:524
  14.3 1.9 %pack.1 = (bf16[160,1024]{1,0:T(8,128)(2,1)}, bf16[160,1024]{1,0:T(8,128)(2,1)}) custom-call(bf16[64,2048]{1,0:T(8,128)(2,1)} %bitcast.12, bf16[64,2048]{1,0:T(8,128)(2,1)} %bitcast.10, bf16[64,256]{1,0:T(8,128)(2,1)} %self_ref.1, bf16[64,256]{1,0:T(8,128)(2,1)} %neigh_ref.1), custom_call_target="tpu_custom_call" | custom-call | bytes 2097152 | tf_op jit(solution)/shard_map/pack/pallas_call | solution.py:56
  16.2 3.6 %collective-permute-start.4 = (bf16[160,1024]{1,0:T(8,128)(2,1)}, bf16[160,1024]{1,0:T(8,128)(2,1)S(1)}, u32[]{:S(2)}, u32[]{:S(2)}) collective-permute-start(bf16[160,1024]{1,0:T(8,128)(2,1)} %get-tuple-element.41), channel_id=1, source_target_pairs={{0,2},{1,3},{2,0},{3,1},{4,6},{5,7},{6,4},{7,5},{8,10},{9,11},{10,... | collective-permute-start | bytes 983048 | tf_op jit(solution)/shard_map/ppermute | solution.py:528
  19.8 6.1 %prepare.1 = (s32[4608,1024]{1,0:T(8,128)}, bf16[576,128,128]{2,1,0:T(8,128)(2,1)}, f32[288,128,64]{2,1,0:T(8,128)}) custom-call(s32[2,96]{1,0:T(2,128)} %bitcast.18, bf16[64,2048]{1,0:T(8,128)(2,1)} %bitcast.13, bf16[96,128,128]{2,1,0:T(8,128)(2,1)} %tile_hbm.1), custom_call_target="tpu_custom_call" | custom-call | flops 1000000000 | bytes 2097152 | tf_op jit(solution)/shard_map/prepare/pallas_call | solution.py:56
  26.0 12.0 %all-to-all-done.recv_ref = bf16[32,3,64,128]{3,2,1,0:T(8,128)(2,1)S(1)} async-done(((bf16[32,3,64,128]{3,2,1,0:T(8,128)(2,1)}), bf16[32,3,64,128]{3,2,1,0:T(8,128)(2,1)S(1)}, u32[]{:S(2)}, u32[]{:S(2)}) %all-to-all-start) | async-done | bytes 1572896 | tf_op jit(solution)/shard_map/all_to_all | solution.py:524
  37.9 6.9 %forward_send.1 = (bf16[64,1024]{1,0:T(8,128)(2,1)S(1)}, f32[8,128,64]{2,1,0:T(8,128)S(1)}, bf16[64,4096]{1,0:T(8,128)(2,1)S(1)}, bf16[2048,4096]{1,0:T(8,128)(2,1)S(1)}) custom-call(s32[4608,1024]{1,0:T(8,128)} %get-tuple-element.32.list_hbm, bf16[32,3,64,128]{3,2,1,0:T(8,128)(2,1)S(1)} %all-to-all-done.recv_ref, ...), custom_call_target="tpu_custom_call" | custom-call | flops 2000000000 | bytes 16777216 | tf_op jit(solution)/shard_map/forward_send/pallas_call | solution.py:56
  44.9 3.7 %collective-permute-start.1 = (bf16[64,1024]{1,0:T(8,128)(2,1)S(1)}, bf16[64,1024]{1,0:T(8,128)(2,1)S(1)}, u32[]{:S(2)}, u32[]{:S(2)}) collective-permute-start(bf16[64,1024]{1,0:T(8,128)(2,1)S(1)} %get-tuple-element.38), channel_id=1, source_target_pairs={{0,2},{1,3},{2,0},{3,1},{4,6},{5,7},{6,4},{7,5},{8,10},{9,11},{10,... | collective-permute-start | bytes 393224 | tf_op jit(solution)/shard_map/ppermute | solution.py:528
  48.6 2.4 %forward_keep.1.rest_0_ = bf16[64,1024]{1,0:T(8,128)(2,1)S(1)} custom-call(f32[8,128,64]{2,1,0:T(8,128)S(1)} %get-tuple-element.35.sum_ref, bf16[64,4096]{1,0:T(8,128)(2,1)S(1)} %get-tuple-element.36.hubs, bf16[2048,4096]{1,0:T(8,128)(2,1)S(1)} %get-tuple-element.37.hub_ref), custom_call_target="tpu_custom_call" | custom-call | flops 1000000000 | bytes 8388608 | tf_op jit(solution)/shard_map/forward_keep/pallas_call | solution.py:56
  51.2 1.4 %collective-permute-done.1.rest_2_ = bf16[64,1024]{1,0:T(8,128)(2,1)S(1)} collective-permute-done((bf16[64,1024]{1,0:T(8,128)(2,1)S(1)}, bf16[64,1024]{1,0:T(8,128)(2,1)S(1)}, u32[]{:S(2)}, u32[]{:S(2)}) %collective-permute-start.1) | collective-permute-done | bytes 131104 | tf_op jit(solution)/shard_map/ppermute | solution.py:528
  52.7 1.3 %collective-permute-done.2.rest_3_ = bf16[64,1024]{1,0:T(8,128)(2,1)S(1)} collective-permute-done((bf16[64,1024]{1,0:T(8,128)(2,1)S(1)}, bf16[64,1024]{1,0:T(8,128)(2,1)S(1)}, u32[]{:S(2)}, u32[]{:S(2)}) %collective-permute-start.2) | collective-permute-done | bytes 131104 | tf_op jit(solution)/shard_map/ppermute | solution.py:528
  54.0 0.9 dense.1
  54.9 3.3 %collective-permute-start.6 = (bf16[64,1024]{1,0:T(8,128)(2,1)S(1)}, bf16[64,1024]{1,0:T(8,128)(2,1)S(1)}, u32[]{:S(2)}, u32[]{:S(2)}) collective-permute-start(bf16[64,1024]{1,0:T(8,128)(2,1)S(1)} %get-tuple-element.44), channel_id=1, source_target_pairs={{0,2},{1,3},{2,0},{3,1},{4,6},{5,7},{6,4},{7,5},{8,10},{9,11},{10,... | collective-permute-start | bytes 393224 | tf_op jit(solution)/shard_map/ppermute | solution.py:528
  58.3 1.7 %hub_backward.1 = (f32[64,4096]{1,0:T(8,128)S(1)}, bf16[64,1024]{1,0:T(8,128)(2,1)S(1)}, bf16[64,1024]{1,0:T(8,128)(2,1)S(1)}) custom-call(bf16[64,1024]{1,0:T(8,128)(2,1)S(1)} %get-tuple-element.51.grad_ref.keep_ref, bf16[256,256]{1,0:T(8,128)(2,1)S(1)} %get-tuple-element.45.self_ref, bf16[256,1024]{1,0:T(8,128)(2,1)S(1)} %get-tuple-element.46.pre_ref, ...), custom_call_target="tpu_custom_call" | custom-call | flops 1000000000 | bytes 8388608 | tf_op jit(solution)/shard_map/hub_backward/pallas_call | solution.py:56
  59.9 0.5 collective-permute-start.7
  60.5 1.7 %collective-permute-done.6.come_ref = bf16[64,1024]{1,0:T(8,128)(2,1)S(1)} collective-permute-done((bf16[64,1024]{1,0:T(8,128)(2,1)S(1)}, bf16[64,1024]{1,0:T(8,128)(2,1)S(1)}, u32[]{:S(2)}, u32[]{:S(2)}) %collective-permute-start.6) | collective-permute-done | bytes 131104 | tf_op jit(solution)/shard_map/ppermute | solution.py:528
  62.1 4.6 %backward.1 = bf16[32,3,64,128]{3,2,1,0:T(8,128)(2,1)} custom-call(s32[4608,1024]{1,0:T(8,128)} %get-tuple-element.32.list_hbm, bf16[64,1024]{1,0:T(8,128)(2,1)S(1)} %get-tuple-element.51.grad_ref.keep_ref, bf16[64,1024]{1,0:T(8,128)(2,1)S(1)} %collective-permute-done.6.come_ref, f32[64,4096]{1,0:T(8,128)S(1)} %get-tuple-element.47.terms_ref, ...), custom_call_target="tpu_custom_call" | custom-call | flops 2000000000 | bytes 8388608 | tf_op jit(solution)/shard_map/backward/pallas_call | solution.py:56
  66.7 0.3 collective-permute-done.7.come_ref
  67.0 4.1 %all-to-all-start.1 = ((bf16[32,3,64,128]{3,2,1,0:T(8,128)(2,1)}), bf16[32,3,64,128]{3,2,1,0:T(8,128)(2,1)S(1)}, u32[]{:S(2)}, u32[]{:S(2)}) async-start(bf16[32,3,64,128]{3,2,1,0:T(8,128)(2,1)} %backward.1), calls=%async_computation.1 | async-start | bytes 3145728 | tf_op jit(solution)/shard_map/all_to_all | solution.py:524
  71.1 3.7 %collective-permute-start.8 = (bf16[64,1024]{1,0:T(8,128)(2,1)S(1)}, bf16[64,1024]{1,0:T(8,128)(2,1)S(1)}, u32[]{:S(2)}, u32[]{:S(2)}) collective-permute-start(bf16[64,1024]{1,0:T(8,128)(2,1)S(1)} %get-tuple-element.55), channel_id=1, source_target_pairs={{0,2},{1,3},{2,0},{3,1},{4,6},{5,7},{6,4},{7,5},{8,10},{9,11},{10,... | collective-permute-start | bytes 393224 | tf_op jit(solution)/shard_map/ppermute | solution.py:528
  74.8 3.9 %own_backward.1.own_hbm = f32[2304,2048]{1,0:T(8,128)} custom-call(s32[4608,1024]{1,0:T(8,128)} %get-tuple-element.32.list_hbm, bf16[64,1024]{1,0:T(8,128)(2,1)} %copy-done, bf16[64,1024]{1,0:T(8,128)(2,1)} %copy-done.1, bf16[576,128,128]{2,1,0:T(8,128)(2,1)} %get-tuple-element.33.tile_hbm), custom_call_target="tpu_custom_call" | custom-call | flops 1000000000 | bytes 2097152 | tf_op jit(solution)/shard_map/own_backward/pallas_call | solution.py:56
  78.7 11.1 %collective-permute-done.8.out_come = bf16[64,1024]{1,0:T(8,128)(2,1)S(1)} collective-permute-done((bf16[64,1024]{1,0:T(8,128)(2,1)S(1)}, bf16[64,1024]{1,0:T(8,128)(2,1)S(1)}, u32[]{:S(2)}, u32[]{:S(2)}) %collective-permute-start.8) | collective-permute-done | bytes 131104 | tf_op jit(solution)/shard_map/ppermute | solution.py:528
  89.8 4.3 %all-to-all-done.1.recv_ref = bf16[32,3,64,128]{3,2,1,0:T(8,128)(2,1)S(1)} async-done(((bf16[32,3,64,128]{3,2,1,0:T(8,128)(2,1)}), bf16[32,3,64,128]{3,2,1,0:T(8,128)(2,1)S(1)}, u32[]{:S(2)}, u32[]{:S(2)}) %all-to-all-start.1) | async-done | bytes 1572896 | tf_op jit(solution)/shard_map/all_to_all | solution.py:524
  94.1 3.7 %scatter_rows.1 = (f32[64,2048]{1,0:T(8,128)}, f32[64,128]{1,0:T(8,128)}, bf16[64,2048]{1,0:T(8,128)(2,1)}) custom-call(s32[32,256]{1,0:T(8,128)S(1)} %bitcast.9, bf16[32,3,64,128]{3,2,1,0:T(8,128)(2,1)S(1)} %all-to-all-done.1.recv_ref, f32[2304,2048]{1,0:T(8,128)} %own_backward.1.own_hbm, bf16[64,1024]{1,0:T(8,128)(2,1)S(1)} %get-tuple-element.52.keep_ref, ...), custom_call_target="tpu_custom_call" | custom-call | flops 1000000000 | bytes 2097152 | tf_op jit(solution)/shard_map/scatter_rows/pallas_call | solution.py:56
  (16 shorter events, 0.4 us)
Async XLA Ops:
  5.6 32.4 %all-to-all-start = ((bf16[32,3,64,128]{3,2,1,0:T(8,128)(2,1)}), bf16[32,3,64,128]{3,2,1,0:T(8,128)(2,1)S(1)}, u32[]{:S(2)}, u32[]{:S(2)}) async-start(bf16[32,3,64,128]{3,2,1,0:T(8,128)(2,1)} %gather_rows.1), calls=%async_computation | async-start | bytes 3145728 | tf_op jit(solution)/shard_map/all_to_all | solution.py:524
  16.2 28.6 %collective-permute-start.4 = (bf16[160,1024]{1,0:T(8,128)(2,1)}, bf16[160,1024]{1,0:T(8,128)(2,1)S(1)}, u32[]{:S(2)}, u32[]{:S(2)}) collective-permute-start(bf16[160,1024]{1,0:T(8,128)(2,1)} %get-tuple-element.41), channel_id=1, source_target_pairs={{0,2},{1,3},{2,0},{3,1},{4,6},{5,7},{6,4},{7,5},{8,10},{9,11},{10,... | collective-permute-start | bytes 983048 | tf_op jit(solution)/shard_map/ppermute | solution.py:528
  19.8 32.8 %collective-permute-start.3 = (bf16[160,1024]{1,0:T(8,128)(2,1)}, bf16[160,1024]{1,0:T(8,128)(2,1)S(1)}, u32[]{:S(2)}, u32[]{:S(2)}) collective-permute-start(bf16[160,1024]{1,0:T(8,128)(2,1)} %get-tuple-element.40.rest_4_), channel_id=1, source_target_pairs={{0,1},{1,0},{2,3},{3,2},{4,5},{5,4},{6,7},{7,6},{8,9},{9,8},{10,11... | collective-permute-start | bytes 983048 | tf_op jit(solution)/shard_map/ppermute | solution.py:528
  44.8 9.2 %copy-start.3 = (bf16[160,1024]{1,0:T(8,128)(2,1)S(1)}, bf16[160,1024]{1,0:T(8,128)(2,1)}, u32[]{:S(2)}) copy-start(bf16[160,1024]{1,0:T(8,128)(2,1)} %get-tuple-element.40.rest_4_) | copy-start | bytes 983044
  44.8 9.2 %collective-permute-start.5 = (bf16[160,1024]{1,0:T(8,128)(2,1)S(1)}, bf16[160,1024]{1,0:T(8,128)(2,1)S(1)}, u32[]{:S(2)}, u32[]{:S(2)}) collective-permute-start(bf16[160,1024]{1,0:T(8,128)(2,1)S(1)} %collective-permute-done.4.rest_6_), channel_id=1, source_target_pairs={{0,1},{1,0},{2,3},{3,2},{4,5},{5,4},{6,7},{7,6},{8,9},{9,8},{10,11... | collective-permute-start | bytes 983048 | tf_op jit(solution)/shard_map/ppermute | solution.py:528
  44.9 7.7 %collective-permute-start.1 = (bf16[64,1024]{1,0:T(8,128)(2,1)S(1)}, bf16[64,1024]{1,0:T(8,128)(2,1)S(1)}, u32[]{:S(2)}, u32[]{:S(2)}) collective-permute-start(bf16[64,1024]{1,0:T(8,128)(2,1)S(1)} %get-tuple-element.38), channel_id=1, source_target_pairs={{0,2},{1,3},{2,0},{3,1},{4,6},{5,7},{6,4},{7,5},{8,10},{9,11},{10,... | collective-permute-start | bytes 393224 | tf_op jit(solution)/shard_map/ppermute | solution.py:528
  51.0 1.6 %collective-permute-start = (bf16[64,1024]{1,0:T(8,128)(2,1)S(1)}, bf16[64,1024]{1,0:T(8,128)(2,1)S(1)}, u32[]{:S(2)}, u32[]{:S(2)}) collective-permute-start(bf16[64,1024]{1,0:T(8,128)(2,1)S(1)} %forward_keep.1.rest_0_), channel_id=1, source_target_pairs={{0,1},{1,0},{2,3},{3,2},{4,5},{5,4},{6,7},{7,6},{8,9},{9,8},{10,11... | collective-permute-start | bytes 393224 | tf_op jit(solution)/shard_map/ppermute | solution.py:528
  52.7 1.3 %collective-permute-start.2 = (bf16[64,1024]{1,0:T(8,128)(2,1)S(1)}, bf16[64,1024]{1,0:T(8,128)(2,1)S(1)}, u32[]{:S(2)}, u32[]{:S(2)}) collective-permute-start(bf16[64,1024]{1,0:T(8,128)(2,1)S(1)} %collective-permute-done.1.rest_2_), channel_id=1, source_target_pairs={{0,1},{1,0},{2,3},{3,2},{4,5},{5,4},{6,7},{7,6},{8,9},{9,8},{10,11... | collective-permute-start | bytes 393224 | tf_op jit(solution)/shard_map/ppermute | solution.py:528
  54.9 11.8 %copy-start = (bf16[64,1024]{1,0:T(8,128)(2,1)}, bf16[64,1024]{1,0:T(8,128)(2,1)S(1)}, u32[]{:S(2)}) copy-start(bf16[64,1024]{1,0:T(8,128)(2,1)S(1)} %get-tuple-element.51.grad_ref.keep_ref) | copy-start | bytes 393220
  54.9 7.2 %collective-permute-start.6 = (bf16[64,1024]{1,0:T(8,128)(2,1)S(1)}, bf16[64,1024]{1,0:T(8,128)(2,1)S(1)}, u32[]{:S(2)}, u32[]{:S(2)}) collective-permute-start(bf16[64,1024]{1,0:T(8,128)(2,1)S(1)} %get-tuple-element.44), channel_id=1, source_target_pairs={{0,2},{1,3},{2,0},{3,1},{4,6},{5,7},{6,4},{7,5},{8,10},{9,11},{10,... | collective-permute-start | bytes 393224 | tf_op jit(solution)/shard_map/ppermute | solution.py:528
  59.9 7.1 %collective-permute-start.7 = (bf16[64,1024]{1,0:T(8,128)(2,1)S(1)}, bf16[64,1024]{1,0:T(8,128)(2,1)S(1)}, u32[]{:S(2)}, u32[]{:S(2)}) collective-permute-start(bf16[64,1024]{1,0:T(8,128)(2,1)S(1)} %get-tuple-element.48), channel_id=1, source_target_pairs={{0,2},{1,3},{2,0},{3,1},{4,6},{5,7},{6,4},{7,5},{8,10},{9,11},{10,... | collective-permute-start | bytes 393224 | tf_op jit(solution)/shard_map/ppermute | solution.py:528
  62.1 4.6 %copy-start.1 = (bf16[64,1024]{1,0:T(8,128)(2,1)}, bf16[64,1024]{1,0:T(8,128)(2,1)S(1)}, u32[]{:S(2)}) copy-start(bf16[64,1024]{1,0:T(8,128)(2,1)S(1)} %collective-permute-done.6.come_ref) | copy-start | bytes 393220
  67.0 27.1 %all-to-all-start.1 = ((bf16[32,3,64,128]{3,2,1,0:T(8,128)(2,1)}), bf16[32,3,64,128]{3,2,1,0:T(8,128)(2,1)S(1)}, u32[]{:S(2)}, u32[]{:S(2)}) async-start(bf16[32,3,64,128]{3,2,1,0:T(8,128)(2,1)} %backward.1), calls=%async_computation.1 | async-start | bytes 3145728 | tf_op jit(solution)/shard_map/all_to_all | solution.py:524
  71.1 23.0 %copy-start.2 = (s32[1,32,256]{2,1,0:T(8,128)S(1)}, s32[1,32,256]{2,1,0:T(8,128)}, u32[]{:S(2)}) copy-start(s32[1,32,256]{2,1,0:T(8,128)} %param.14) | copy-start | bytes 98308
  71.1 18.7 %collective-permute-start.8 = (bf16[64,1024]{1,0:T(8,128)(2,1)S(1)}, bf16[64,1024]{1,0:T(8,128)(2,1)S(1)}, u32[]{:S(2)}, u32[]{:S(2)}) collective-permute-start(bf16[64,1024]{1,0:T(8,128)(2,1)S(1)} %get-tuple-element.55), channel_id=1, source_target_pairs={{0,2},{1,3},{2,0},{3,1},{4,6},{5,7},{6,4},{7,5},{8,10},{9,11},{10,... | collective-permute-start | bytes 393224 | tf_op jit(solution)/shard_map/ppermute | solution.py:528

commit v5 on v4

--- a/solution.py
+++ b/solution.py
@@ -51,7 +51,7 @@
 VMEM = pl.BlockSpec(memory_space=pltpu.VMEM)
 
 
-def local_call(kernel, outs, args, name, places=(), scratch=(), flops=10**9, size=2**21, mib=14):
+def local_call(kernel, outs, args, name, places=(), scratch=(), flops=10**9, size=2**21, mib=14, alias=()):
     places = dict(places)
     return pl.pallas_call(
         kernel,
@@ -59,6 +59,7 @@
         in_specs=[places.get(i, VMEM) for i in range(len(args))],
         out_specs=[places.get(100 + i, SMEM if o.dtype == I32 else VMEM) for i, o in enumerate(outs)],
         scratch_shapes=list(scratch),
+        input_output_aliases=dict(alias),
         compiler_params=pltpu.CompilerParams(vmem_limit_bytes=mib * 1024 * 1024),
         cost_estimate=pl.CostEstimate(flops=flops, bytes_accessed=size, transcendentals=0),
         name=name,
@@ -93,22 +94,31 @@
     )
 
 
-def gather_kernel(x_ref, slot_ref, hub_ref, out_ref, stacked):
+GATHER_STEPS = 4
+
+
+def gather_kernel(x_ref, slot_ref, hub_ref, out_hbm, out_ref, stacked, sems):
     for b in range(HIGH):
         stacked[b * COLS : (b + 1) * COLS, :] = x_ref[:, b * LOW : (b + 1) * LOW]
-
-    @pl.loop(0, DOM, unroll=16)
-    def _(r):
-        index = slot_ref[pl.ds(r, 1), :]
-        high = index >> 8
-        found = dot(stacked[...], one_hot(index & (LOW - 1)), NN)
-        out = jnp.zeros((COLS, SLOTS), F32)
-        for b in range(HIGH):
-            out = jnp.where(high == b, found[b * COLS : (b + 1) * COLS], out)
-        out = out.astype(BF)
-        out_ref[r, 0] = out[:, :TILE]
-        out_ref[r, 1] = out[:, TILE:]
-        out_ref[r, 2] = hub_ref[...]
+    group = DOM // GATHER_STEPS
+    copies = []
+    for step in range(GATHER_STEPS):
+        for r in range(step * group, (step + 1) * group):
+            index = slot_ref[r : r + 1, :]
+            high = index >> 8
+            found = dot(stacked[...], one_hot(index & (LOW - 1)), NN)
+            out = jnp.zeros((COLS, SLOTS), F32)
+            for b in range(HIGH):
+                out = jnp.where(high == b, found[b * COLS : (b + 1) * COLS], out)
+            out = out.astype(BF)
+            out_ref[r, 0] = out[:, :TILE]
+            out_ref[r, 1] = out[:, TILE:]
+            out_ref[r, 2] = hub_ref[...]
+        part = pl.ds(step * group, group)
+        copies.append(pltpu.make_async_copy(out_ref.at[part], out_hbm.at[part], sems.at[step]))
+        copies[step].start()
+    for copy in copies:
+        copy.wait()
 
 
 def gather_rows(x, slots, hubs):
@@ -117,7 +127,12 @@
         [shape(DOM, 3, COLS, TILE)],
         [x, slots, hubs],
         "gather_rows",
-        scratch=[pltpu.VMEM((HIGH * COLS, LOW), BF)],
+        places={100: ANY},
+        scratch=[
+            pltpu.VMEM((DOM, 3, COLS, TILE), BF),
+            pltpu.VMEM((HIGH * COLS, LOW), BF),
+            pltpu.SemaphoreType.DMA((GATHER_STEPS,)),
+        ],
         flops=4 * 10**9,
         mib=60,
     )[0]
@@ -188,6 +203,8 @@
 
 
 HUB_STEPS = 4
+KEEP_EARLY = 2
+TILE_STEPS = 4
 HALF_ROWS = HALF // HUB_STEPS
 
 
@@ -211,28 +228,33 @@
         for i, (src, dst) in enumerate(
             (
                 (list_hbm.at[0], target_ref),
-                (tile_hbm.at[pl.ds(0, RECV_TILES)], tile_ref),
                 (local_hbm.at[pl.ds(0, OWN_TILES)], total),
             )
         )
     ]
+    group = RECV_TILES // TILE_STEPS
+    tile_copies = []
+    for i in range(TILE_STEPS):
+        part = pl.ds(i * group, group)
+        tile_copies.append(
+            pltpu.make_async_copy(tile_hbm.at[part], tile_ref.at[part], sems.at[2 * HUB_STEPS + 2 + i])
+        )
     copies = []
     for h, half in enumerate((away, chip())):
-        for i in range(HUB_STEPS):
+        for i in range(KEEP_EARLY if h else HUB_STEPS):
             rows = half_rows(half, i)
             copies.append(pltpu.make_async_copy(hub_hbm.at[rows], hub_ref.at[rows], sems.at[h * HUB_STEPS + i]))
-    for copy in firsts + copies:
+    for copy in tile_copies[:1] + firsts + tile_copies[1:] + copies:
         copy.start()
     for q in range(DOM):
         hubs[:, q * TILE : (q + 1) * TILE] = recv_ref[q, 2]
-    for copy in firsts:
-        copy.wait()
-    group = 16
-
-    @pl.loop(0, RECV_TILES // group)
-    def _(step):
+    for step in range(TILE_STEPS):
         first = step * group
+        tile_copies[step].wait()
         products = [dot(tile_ref[first + k], recv_ref[first // 2 + k // 2, k % 2], NT) for k in range(group)]
+        if step == 0:
+            for copy in firsts:
+                copy.wait()
         for k, product in enumerate(products):
             d = target_ref[first + k]
             total[d] = total[d] + product
@@ -263,7 +285,7 @@
             pltpu.SMEM((LIST,), I32),
             pltpu.VMEM((RECV_TILES, TILE, TILE), BF),
             pltpu.VMEM((OWN_TILES, TILE, COLS), F32),
-            pltpu.SemaphoreType.DMA((2 * HUB_STEPS + 3,)),
+            pltpu.SemaphoreType.DMA((2 * HUB_STEPS + 2 + TILE_STEPS,)),
         ],
         flops=2 * 10**9,
         size=2**24,
@@ -271,25 +293,34 @@
     )
 
 
-def forward_keep_kernel(sum_ref, hubs, hub_ref, keep_ref, total):
+def forward_keep_kernel(sum_ref, hubs, _, hub_hbm, keep_ref, hub_ref, total, sems):
+    copies = []
+    for i in range(KEEP_EARLY, HUB_STEPS):
+        rows = half_rows(chip(), i)
+        copies.append(pltpu.make_async_copy(hub_hbm.at[rows], hub_ref.at[rows], sems.at[i]))
+    for copy in copies:
+        copy.start()
     total[...] = sum_ref[...]
     for step in range(HUB_STEPS):
+        if step >= KEEP_EARLY:
+            copies[step - KEEP_EARLY].wait()
         add_hub_rows(hub_ref, chip(), step, hubs, total, 0)
     for j in range(HALF_TILES):
         keep_ref[:, j * TILE : (j + 1) * TILE] = total[j].T.astype(BF)
 
 
-def forward_keep(sums, hubs, hub):
+def forward_keep(sums, hubs, hub, hub_coef):
     return local_call(
         forward_keep_kernel,
-        [shape(COLS, HALF)],
-        [sums, hubs, hub],
+        [shape(COLS, HALF), shape(NODES, HUBS)],
+        [sums, hubs, hub, hub_coef],
         "forward_keep",
-        places={},
-        scratch=[pltpu.VMEM(sums.shape, F32)],
+        places={3: ANY},
+        scratch=[pltpu.VMEM(sums.shape, F32), pltpu.SemaphoreType.DMA((HUB_STEPS,))],
         size=2**23,
-        mib=20,
-    )[0]
+        mib=28,
+        alias={2: 1},
+    )
 
 
 def chip():
@@ -378,9 +409,10 @@
 
 
 def backward_kernel(list_hbm, keep_ref, come_ref, terms_ref, tile_hbm, hub_ref, *rest):
-    out_ref, target_ref, grads, tile_ref, sems = rest
+    out_hbm, out_ref, target_ref, grads, tile_ref, sems = rest
     group = RECV_TILES // HUB_STEPS
     doms = DOM // HUB_STEPS
+    out_copies = []
     list_copy = pltpu.make_async_copy(list_hbm.at[0], target_ref, sems.at[HUB_STEPS])
     list_copy.start()
     copies = []
@@ -398,6 +430,11 @@
         copies[step].wait()
         for s in range(step * group, (step + 1) * group):
             out_ref[s // 2, s % 2] = dot(grads[target_ref[s]], tile_ref[s], NN).astype(BF)
+        part = pl.ds(step * doms, doms)
+        out_copies.append(pltpu.make_async_copy(out_ref.at[part], out_hbm.at[part], sems.at[HUB_STEPS + 1 + step]))
+        out_copies[step].start()
+    for copy in out_copies:
+        copy.wait()
 
 
 def backward(lists, keep, come, terms, tiles, hub):
@@ -406,12 +443,13 @@
         [shape(DOM, 3, COLS, TILE)],
         [lists, keep, come, terms, tiles, hub],
         "backward",
-        places={0: ANY, 4: ANY},
+        places={0: ANY, 4: ANY, 100: ANY},
         scratch=[
+            pltpu.VMEM((DOM, 3, COLS, TILE), BF),
             pltpu.SMEM((LIST,), I32),
             pltpu.VMEM((OWN_TILES, COLS, TILE), BF),
             pltpu.VMEM((RECV_TILES, TILE, TILE), BF),
-            pltpu.SemaphoreType.DMA((HUB_STEPS + 1,)),
+            pltpu.SemaphoreType.DMA((2 * HUB_STEPS + 1,)),
         ],
         flops=2 * 10**9,
         size=2**23,
@@ -559,7 +597,7 @@
     agg_2 = swap(agg_send, 2)
     early_2 = after(early_2, agg_send)
     early = [early, early_1, early_2, swap(early_2, 1)]
-    agg = forward_keep(sums, hubs, hub)
+    agg, hub = forward_keep(sums, hubs, hub, hub_coef)
     grad, grad_send, grad_pre, self_weight, out_keep, out_send = dense(
         [agg, swap(agg, 1), agg_2, swap(agg_2, 1)], early
     )

time: 98.4 us -> 98.6 us (level)
  waiting for transfers between devices: 32 us -> 33.3 us
    ppermute x9, starting transfers between devices: 15.1 us -> 13.4 us  [swap(): return lax.ppermute(x, 'feat', [(f, f ^ k) for f in range(FEAT)])]
    all_to_all x2, starting transfers between devices: 12.9 us -> 14.5 us  [to_dom(): return lax.all_to_all(x, 'dom', split_axis=0, concat_axis=0, tiled=True)]
  transfers between devices with their start and end apart: 11 -> 11, of which waited for: 7 -> 8; matrix products, arithmetic and copies ran while one was open for 0% -> 0% of each run, Pallas kernels for 28% -> 27%
where the time goes in v5:
time: 98.6 us; the launch traced here: 98.2 us
  Pallas kernels  36.1 us (37%)
  waiting for transfers between devices  33.3 us (34%)
  starting transfers between devices  27.8 us (28%)
    pallas_call x10, Pallas kernels, local_call(): pl.pallas_call(kernel, out_shape=outs, in_specs=[places.get(i, VMEM) for...  36.1 us
    ppermute x9, waiting for transfers between devices, swap(): return lax.ppermute(x, 'feat', [(f, f ^ k) for f in range(FEAT)])  16.7 us
    all_to_all x2, waiting for transfers between devices, to_dom(): return lax.all_to_all(x, 'dom', split_axis=0, concat_axis=0, tiled=True)  16.6 us
    all_to_all x2, starting transfers between devices, to_dom(): return lax.all_to_all(x, 'dom', split_axis=0, concat_axis=0, tiled=True)  14.5 us
    ppermute x9, starting transfers between devices, swap(): return lax.ppermute(x, 'feat', [(f, f ^ k) for f in range(FEAT)])  13.4 us
  transfers between devices with their start and end apart: 11, of which 8 were waited for; matrix products, arithmetic and copies ran while one was open for 0% of the time, Pallas kernels for 27%

profile of v5, /device:TPU:0, one launch (start us, length us, event | category | flops | bytes accessed | tf_op | source)
XLA Modules:
  0.0 98.2 jit_solution(11001103394591873267)
XLA Ops:
  0.6 4.8 %gather_rows.1 = bf16[32,3,64,128]{3,2,1,0:T(8,128)(2,1)} custom-call(bf16[64,2048]{1,0:T(8,128)(2,1)} %bitcast.11, s32[32,256]{1,0:T(8,128)} %bitcast.8, bf16[64,128]{1,0:T(8,128)(2,1)} %bitcast.17), custom_call_target="tpu_custom_call" | custom-call | flops 4000000000 | bytes 2097152 | tf_op jit(solution)/shard_map/gather_rows/pallas_call | solution.py:56
  5.4 8.8 %all-to-all-start = ((bf16[32,3,64,128]{3,2,1,0:T(8,128)(2,1)}), bf16[32,3,64,128]{3,2,1,0:T(8,128)(2,1)S(1)}, u32[]{:S(2)}, u32[]{:S(2)}) async-start(bf16[32,3,64,128]{3,2,1,0:T(8,128)(2,1)} %gather_rows.1), calls=%async_computation | async-start | bytes 3145728 | tf_op jit(solution)/shard_map/all_to_all | solution.py:562
  14.2 1.9 %pack.1 = (bf16[160,1024]{1,0:T(8,128)(2,1)}, bf16[160,1024]{1,0:T(8,128)(2,1)}) custom-call(bf16[64,2048]{1,0:T(8,128)(2,1)} %bitcast.12, bf16[64,2048]{1,0:T(8,128)(2,1)} %bitcast.10, bf16[64,256]{1,0:T(8,128)(2,1)} %self_ref.1, bf16[64,256]{1,0:T(8,128)(2,1)} %neigh_ref.1), custom_call_target="tpu_custom_call" | custom-call | bytes 2097152 | tf_op jit(solution)/shard_map/pack/pallas_call | solution.py:56
  16.1 3.6 %collective-permute-start.4 = (bf16[160,1024]{1,0:T(8,128)(2,1)}, bf16[160,1024]{1,0:T(8,128)(2,1)S(1)}, u32[]{:S(2)}, u32[]{:S(2)}) collective-permute-start(bf16[160,1024]{1,0:T(8,128)(2,1)} %get-tuple-element.44), channel_id=1, source_target_pairs={{0,2},{1,3},{2,0},{3,1},{4,6},{5,7},{6,4},{7,5},{8,10},{9,11},{10,... | collective-permute-start | bytes 983048 | tf_op jit(solution)/shard_map/ppermute | solution.py:566
  19.7 6.1 %prepare.1 = (s32[4608,1024]{1,0:T(8,128)}, bf16[576,128,128]{2,1,0:T(8,128)(2,1)}, f32[288,128,64]{2,1,0:T(8,128)}) custom-call(s32[2,96]{1,0:T(2,128)} %bitcast.18, bf16[64,2048]{1,0:T(8,128)(2,1)} %bitcast.13, bf16[96,128,128]{2,1,0:T(8,128)(2,1)} %tile_hbm.1), custom_call_target="tpu_custom_call" | custom-call | flops 1000000000 | bytes 2097152 | tf_op jit(solution)/shard_map/prepare/pallas_call | solution.py:56
  25.9 11.9 %all-to-all-done.recv_ref = bf16[32,3,64,128]{3,2,1,0:T(8,128)(2,1)S(1)} async-done(((bf16[32,3,64,128]{3,2,1,0:T(8,128)(2,1)}), bf16[32,3,64,128]{3,2,1,0:T(8,128)(2,1)S(1)}, u32[]{:S(2)}, u32[]{:S(2)}) %all-to-all-start) | async-done | bytes 1572896 | tf_op jit(solution)/shard_map/all_to_all | solution.py:562
  37.8 5.7 %forward_send.1 = (bf16[64,1024]{1,0:T(8,128)(2,1)S(1)}, f32[8,128,64]{2,1,0:T(8,128)S(1)}, bf16[64,4096]{1,0:T(8,128)(2,1)S(1)}, bf16[2048,4096]{1,0:T(8,128)(2,1)S(1)}) custom-call(s32[4608,1024]{1,0:T(8,128)} %get-tuple-element.34.list_hbm, bf16[32,3,64,128]{3,2,1,0:T(8,128)(2,1)S(1)} %all-to-all-done.recv_ref, ...), custom_call_target="tpu_custom_call" | custom-call | flops 2000000000 | bytes 16777216 | tf_op jit(solution)/shard_map/forward_send/pallas_call | solution.py:56
  43.6 3.7 %collective-permute-start.1 = (bf16[64,1024]{1,0:T(8,128)(2,1)S(1)}, bf16[64,1024]{1,0:T(8,128)(2,1)S(1)}, u32[]{:S(2)}, u32[]{:S(2)}) collective-permute-start(bf16[64,1024]{1,0:T(8,128)(2,1)S(1)} %get-tuple-element.41), channel_id=1, source_target_pairs={{0,2},{1,3},{2,0},{3,1},{4,6},{5,7},{6,4},{7,5},{8,10},{9,11},{10,... | collective-permute-start | bytes 393224 | tf_op jit(solution)/shard_map/ppermute | solution.py:566
  47.3 3.2 %forward_keep.1 = (bf16[64,1024]{1,0:T(8,128)(2,1)S(1)}, bf16[2048,4096]{1,0:T(8,128)(2,1)S(1)}) custom-call(f32[8,128,64]{2,1,0:T(8,128)S(1)} %get-tuple-element.37.sum_ref, bf16[64,4096]{1,0:T(8,128)(2,1)S(1)} %get-tuple-element.38.hubs, bf16[2048,4096]{1,0:T(8,128)(2,1)S(1)} %get-tuple-element.39._, ...), custom_call_target="tpu_custom_call", output_to_operand_aliasing={{1}: (2, {})} | custom-call | flops 1000000000 | bytes 8388608 | tf_op jit(solution)/shard_map/forward_keep/pallas_call | solution.py:56
  50.7 0.7 collective-permute-done.1.rest_2_
  51.4 0.5 collective-permute-done.rest_1_
  51.9 0.8 collective-permute-done.2.rest_3_
  52.7 0.9 dense.1
  53.6 3.5 %collective-permute-start.6 = (bf16[64,1024]{1,0:T(8,128)(2,1)S(1)}, bf16[64,1024]{1,0:T(8,128)(2,1)S(1)}, u32[]{:S(2)}, u32[]{:S(2)}) collective-permute-start(bf16[64,1024]{1,0:T(8,128)(2,1)S(1)} %get-tuple-element.47), channel_id=1, source_target_pairs={{0,2},{1,3},{2,0},{3,1},{4,6},{5,7},{6,4},{7,5},{8,10},{9,11},{10,... | collective-permute-start | bytes 393224 | tf_op jit(solution)/shard_map/ppermute | solution.py:566
  57.2 1.6 %hub_backward.1 = (f32[64,4096]{1,0:T(8,128)S(1)}, bf16[64,1024]{1,0:T(8,128)(2,1)S(1)}, bf16[64,1024]{1,0:T(8,128)(2,1)S(1)}) custom-call(bf16[64,1024]{1,0:T(8,128)(2,1)S(1)} %get-tuple-element.55.grad_ref.keep_ref, bf16[256,256]{1,0:T(8,128)(2,1)S(1)} %get-tuple-element.48.self_ref, bf16[256,1024]{1,0:T(8,128)(2,1)S(1)} %get-tuple-element.49.pre_ref, ...), custom_call_target="tpu_custom_call" | custom-call | flops 1000000000 | bytes 8388608 | tf_op jit(solution)/shard_map/hub_backward/pallas_call | solution.py:56
  59.2 1.9 %collective-permute-done.6.come_ref = bf16[64,1024]{1,0:T(8,128)(2,1)S(1)} collective-permute-done((bf16[64,1024]{1,0:T(8,128)(2,1)S(1)}, bf16[64,1024]{1,0:T(8,128)(2,1)S(1)}, u32[]{:S(2)}, u32[]{:S(2)}) %collective-permute-start.6) | collective-permute-done | bytes 131104 | tf_op jit(solution)/shard_map/ppermute | solution.py:566
  61.0 4.2 %backward.1 = bf16[32,3,64,128]{3,2,1,0:T(8,128)(2,1)} custom-call(s32[4608,1024]{1,0:T(8,128)} %get-tuple-element.34.list_hbm, bf16[64,1024]{1,0:T(8,128)(2,1)S(1)} %get-tuple-element.55.grad_ref.keep_ref, bf16[64,1024]{1,0:T(8,128)(2,1)S(1)} %collective-permute-done.6.come_ref, f32[64,4096]{1,0:T(8,128)S(1)} %get-tuple-element.51.terms_ref, ...), custom_call_target="tpu_custom_call" | custom-call | flops 2000000000 | bytes 8388608 | tf_op jit(solution)/shard_map/backward/pallas_call | solution.py:56
  65.3 0.4 collective-permute-done.7.come_ref
  65.7 5.7 %all-to-all-start.1 = ((bf16[32,3,64,128]{3,2,1,0:T(8,128)(2,1)}), bf16[32,3,64,128]{3,2,1,0:T(8,128)(2,1)S(1)}, u32[]{:S(2)}, u32[]{:S(2)}) async-start(bf16[32,3,64,128]{3,2,1,0:T(8,128)(2,1)} %backward.1), calls=%async_computation.1 | async-start | bytes 3145728 | tf_op jit(solution)/shard_map/all_to_all | solution.py:562
  71.4 1.9 %collective-permute-start.8 = (bf16[64,1024]{1,0:T(8,128)(2,1)S(1)}, bf16[64,1024]{1,0:T(8,128)(2,1)S(1)}, u32[]{:S(2)}, u32[]{:S(2)}) collective-permute-start(bf16[64,1024]{1,0:T(8,128)(2,1)S(1)} %get-tuple-element.59), channel_id=1, source_target_pairs={{0,2},{1,3},{2,0},{3,1},{4,6},{5,7},{6,4},{7,5},{8,10},{9,11},{10,... | collective-permute-start | bytes 393224 | tf_op jit(solution)/shard_map/ppermute | solution.py:566
  73.4 3.9 %own_backward.1.own_hbm = f32[2304,2048]{1,0:T(8,128)} custom-call(s32[4608,1024]{1,0:T(8,128)} %get-tuple-element.34.list_hbm, bf16[64,1024]{1,0:T(8,128)(2,1)} %copy-done, bf16[64,1024]{1,0:T(8,128)(2,1)} %copy-done.1, bf16[576,128,128]{2,1,0:T(8,128)(2,1)} %get-tuple-element.35.tile_hbm), custom_call_target="tpu_custom_call" | custom-call | flops 1000000000 | bytes 2097152 | tf_op jit(solution)/shard_map/own_backward/pallas_call | solution.py:56
  77.3 12.4 %collective-permute-done.8.out_come = bf16[64,1024]{1,0:T(8,128)(2,1)S(1)} collective-permute-done((bf16[64,1024]{1,0:T(8,128)(2,1)S(1)}, bf16[64,1024]{1,0:T(8,128)(2,1)S(1)}, u32[]{:S(2)}, u32[]{:S(2)}) %collective-permute-start.8) | collective-permute-done | bytes 131104 | tf_op jit(solution)/shard_map/ppermute | solution.py:566
  89.6 4.7 %all-to-all-done.1.recv_ref = bf16[32,3,64,128]{3,2,1,0:T(8,128)(2,1)S(1)} async-done(((bf16[32,3,64,128]{3,2,1,0:T(8,128)(2,1)}), bf16[32,3,64,128]{3,2,1,0:T(8,128)(2,1)S(1)}, u32[]{:S(2)}, u32[]{:S(2)}) %all-to-all-start.1) | async-done | bytes 1572896 | tf_op jit(solution)/shard_map/all_to_all | solution.py:562
  94.3 3.7 %scatter_rows.1 = (f32[64,2048]{1,0:T(8,128)}, f32[64,128]{1,0:T(8,128)}, bf16[64,2048]{1,0:T(8,128)(2,1)}) custom-call(s32[32,256]{1,0:T(8,128)S(1)} %bitcast.9, bf16[32,3,64,128]{3,2,1,0:T(8,128)(2,1)S(1)} %all-to-all-done.1.recv_ref, f32[2304,2048]{1,0:T(8,128)} %own_backward.1.own_hbm, bf16[64,1024]{1,0:T(8,128)(2,1)S(1)} %get-tuple-element.56.keep_ref, ...), custom_call_target="tpu_custom_call" | custom-call | flops 1000000000 | bytes 2097152 | tf_op jit(solution)/shard_map/scatter_rows/pallas_call | solution.py:56
  (16 shorter events, 0.7 us)
Async XLA Ops:
  5.4 32.4 %all-to-all-start = ((bf16[32,3,64,128]{3,2,1,0:T(8,128)(2,1)}), bf16[32,3,64,128]{3,2,1,0:T(8,128)(2,1)S(1)}, u32[]{:S(2)}, u32[]{:S(2)}) async-start(bf16[32,3,64,128]{3,2,1,0:T(8,128)(2,1)} %gather_rows.1), calls=%async_computation | async-start | bytes 3145728 | tf_op jit(solution)/shard_map/all_to_all | solution.py:562
  16.1 27.4 %collective-permute-start.4 = (bf16[160,1024]{1,0:T(8,128)(2,1)}, bf16[160,1024]{1,0:T(8,128)(2,1)S(1)}, u32[]{:S(2)}, u32[]{:S(2)}) collective-permute-start(bf16[160,1024]{1,0:T(8,128)(2,1)} %get-tuple-element.44), channel_id=1, source_target_pairs={{0,2},{1,3},{2,0},{3,1},{4,6},{5,7},{6,4},{7,5},{8,10},{9,11},{10,... | collective-permute-start | bytes 983048 | tf_op jit(solution)/shard_map/ppermute | solution.py:566
  19.7 31.7 %collective-permute-start.3 = (bf16[160,1024]{1,0:T(8,128)(2,1)}, bf16[160,1024]{1,0:T(8,128)(2,1)S(1)}, u32[]{:S(2)}, u32[]{:S(2)}) collective-permute-start(bf16[160,1024]{1,0:T(8,128)(2,1)} %get-tuple-element.43.rest_4_), channel_id=1, source_target_pairs={{0,1},{1,0},{2,3},{3,2},{4,5},{5,4},{6,7},{7,6},{8,9},{9,8},{10,11... | collective-permute-start | bytes 983048 | tf_op jit(solution)/shard_map/ppermute | solution.py:566
  43.5 9.2 %collective-permute-start.5 = (bf16[160,1024]{1,0:T(8,128)(2,1)S(1)}, bf16[160,1024]{1,0:T(8,128)(2,1)S(1)}, u32[]{:S(2)}, u32[]{:S(2)}) collective-permute-start(bf16[160,1024]{1,0:T(8,128)(2,1)S(1)} %collective-permute-done.4.rest_6_), channel_id=1, source_target_pairs={{0,1},{1,0},{2,3},{3,2},{4,5},{5,4},{6,7},{7,6},{8,9},{9,8},{10,11... | collective-permute-start | bytes 983048 | tf_op jit(solution)/shard_map/ppermute | solution.py:566
  43.6 7.7 %collective-permute-start.1 = (bf16[64,1024]{1,0:T(8,128)(2,1)S(1)}, bf16[64,1024]{1,0:T(8,128)(2,1)S(1)}, u32[]{:S(2)}, u32[]{:S(2)}) collective-permute-start(bf16[64,1024]{1,0:T(8,128)(2,1)S(1)} %get-tuple-element.41), channel_id=1, source_target_pairs={{0,2},{1,3},{2,0},{3,1},{4,6},{5,7},{6,4},{7,5},{8,10},{9,11},{10,... | collective-permute-start | bytes 393224 | tf_op jit(solution)/shard_map/ppermute | solution.py:566
  47.3 5.4 %copy-start.3 = (bf16[160,1024]{1,0:T(8,128)(2,1)S(1)}, bf16[160,1024]{1,0:T(8,128)(2,1)}, u32[]{:S(2)}) copy-start(bf16[160,1024]{1,0:T(8,128)(2,1)} %get-tuple-element.43.rest_4_) | copy-start | bytes 983044
  50.4 1.4 %collective-permute-start = (bf16[64,1024]{1,0:T(8,128)(2,1)S(1)}, bf16[64,1024]{1,0:T(8,128)(2,1)S(1)}, u32[]{:S(2)}, u32[]{:S(2)}) collective-permute-start(bf16[64,1024]{1,0:T(8,128)(2,1)S(1)} %get-tuple-element.40.rest_0_), channel_id=1, source_target_pairs={{0,1},{1,0},{2,3},{3,2},{4,5},{5,4},{6,7},{7,6},{8,9},{9,8},{10,11... | collective-permute-start | bytes 393224 | tf_op jit(solution)/shard_map/ppermute | solution.py:566
  51.4 1.3 %collective-permute-start.2 = (bf16[64,1024]{1,0:T(8,128)(2,1)S(1)}, bf16[64,1024]{1,0:T(8,128)(2,1)S(1)}, u32[]{:S(2)}, u32[]{:S(2)}) collective-permute-start(bf16[64,1024]{1,0:T(8,128)(2,1)S(1)} %collective-permute-done.1.rest_2_), channel_id=1, source_target_pairs={{0,1},{1,0},{2,3},{3,2},{4,5},{5,4},{6,7},{7,6},{8,9},{9,8},{10,11... | collective-permute-start | bytes 393224 | tf_op jit(solution)/shard_map/ppermute | solution.py:566
  53.6 11.6 %copy-start = (bf16[64,1024]{1,0:T(8,128)(2,1)}, bf16[64,1024]{1,0:T(8,128)(2,1)S(1)}, u32[]{:S(2)}) copy-start(bf16[64,1024]{1,0:T(8,128)(2,1)S(1)} %get-tuple-element.55.grad_ref.keep_ref) | copy-start | bytes 393220
  53.6 7.4 %collective-permute-start.6 = (bf16[64,1024]{1,0:T(8,128)(2,1)S(1)}, bf16[64,1024]{1,0:T(8,128)(2,1)S(1)}, u32[]{:S(2)}, u32[]{:S(2)}) collective-permute-start(bf16[64,1024]{1,0:T(8,128)(2,1)S(1)} %get-tuple-element.47), channel_id=1, source_target_pairs={{0,2},{1,3},{2,0},{3,1},{4,6},{5,7},{6,4},{7,5},{8,10},{9,11},{10,... | collective-permute-start | bytes 393224 | tf_op jit(solution)/shard_map/ppermute | solution.py:566
  58.8 6.9 %collective-permute-start.7 = (bf16[64,1024]{1,0:T(8,128)(2,1)S(1)}, bf16[64,1024]{1,0:T(8,128)(2,1)S(1)}, u32[]{:S(2)}, u32[]{:S(2)}) collective-permute-start(bf16[64,1024]{1,0:T(8,128)(2,1)S(1)} %get-tuple-element.52), channel_id=1, source_target_pairs={{0,2},{1,3},{2,0},{3,1},{4,6},{5,7},{6,4},{7,5},{8,10},{9,11},{10,... | collective-permute-start | bytes 393224 | tf_op jit(solution)/shard_map/ppermute | solution.py:566
  61.0 4.2 %copy-start.1 = (bf16[64,1024]{1,0:T(8,128)(2,1)}, bf16[64,1024]{1,0:T(8,128)(2,1)S(1)}, u32[]{:S(2)}) copy-start(bf16[64,1024]{1,0:T(8,128)(2,1)S(1)} %collective-permute-done.6.come_ref) | copy-start | bytes 393220
  65.7 28.6 %all-to-all-start.1 = ((bf16[32,3,64,128]{3,2,1,0:T(8,128)(2,1)}), bf16[32,3,64,128]{3,2,1,0:T(8,128)(2,1)S(1)}, u32[]{:S(2)}, u32[]{:S(2)}) async-start(bf16[32,3,64,128]{3,2,1,0:T(8,128)(2,1)} %backward.1), calls=%async_computation.1 | async-start | bytes 3145728 | tf_op jit(solution)/shard_map/all_to_all | solution.py:562
  71.4 22.9 %copy-start.2 = (s32[1,32,256]{2,1,0:T(8,128)S(1)}, s32[1,32,256]{2,1,0:T(8,128)}, u32[]{:S(2)}) copy-start(s32[1,32,256]{2,1,0:T(8,128)} %param.14) | copy-start | bytes 98308
  71.4 18.2 %collective-permute-start.8 = (bf16[64,1024]{1,0:T(8,128)(2,1)S(1)}, bf16[64,1024]{1,0:T(8,128)(2,1)S(1)}, u32[]{:S(2)}, u32[]{:S(2)}) collective-permute-start(bf16[64,1024]{1,0:T(8,128)(2,1)S(1)} %get-tuple-element.59), channel_id=1, source_target_pairs={{0,2},{1,3},{2,0},{3,1},{4,6},{5,7},{6,4},{7,5},{8,10},{9,11},{10,... | collective-permute-start | bytes 393224 | tf_op jit(solution)/shard_map/ppermute | solution.py:566

commit v6 on v5

--- a/solution.py
+++ b/solution.py
@@ -595,9 +595,9 @@
     lists, tiles, local_sum = prepare(index, x_in, tile_coef)
     agg_send, sums, hubs, hub = forward_send(lists, incoming, tiles, local_sum, hub_coef)
     agg_2 = swap(agg_send, 2)
-    early_2 = after(early_2, agg_send)
+    agg, hub = forward_keep(sums, hubs, hub, hub_coef)
+    early_2, agg_2, agg = lax.optimization_barrier((early_2, agg_2, agg))
     early = [early, early_1, early_2, swap(early_2, 1)]
-    agg, hub = forward_keep(sums, hubs, hub, hub_coef)
     grad, grad_send, grad_pre, self_weight, out_keep, out_send = dense(
         [agg, swap(agg, 1), agg_2, swap(agg_2, 1)], early
     )

time: 98.6 us -> 97.1 us (0.985)
  waiting for transfers between devices: 33.3 us -> 31 us
    ppermute x9, starting transfers between devices: 13.4 us -> 15.9 us  [swap(): return lax.ppermute(x, 'feat', [(f, f ^ k) for f in range(FEAT)])]
    ppermute x9, waiting for transfers between devices: 16.7 us -> 14.4 us  [swap(): return lax.ppermute(x, 'feat', [(f, f ^ k) for f in range(FEAT)])]
    all_to_all x2, starting transfers between devices: 14.5 us -> 12.7 us  [to_dom(): return lax.all_to_all(x, 'dom', split_axis=0, concat_axis=0, tiled=True)]
  transfers between devices with their start and end apart: 11 -> 11, of which waited for: 8 -> 7; matrix products, arithmetic and copies ran while one was open for 0% -> 0% of each run, Pallas kernels for 27% -> 28%
where the time goes in v6:
time: 97.1 us; the launch traced here: 96.7 us
  Pallas kernels  36.1 us (37%)
  waiting for transfers between devices  31 us (32%)
  starting transfers between devices  28.7 us (30%)
    pallas_call x10, Pallas kernels, local_call(): pl.pallas_call(kernel, out_shape=outs, in_specs=[places.get(i, VMEM) for...  36.1 us
    all_to_all x2, waiting for transfers between devices, to_dom(): return lax.all_to_all(x, 'dom', split_axis=0, concat_axis=0, tiled=True)  16.6 us
    ppermute x9, starting transfers between devices, swap(): return lax.ppermute(x, 'feat', [(f, f ^ k) for f in range(FEAT)])  15.9 us
    ppermute x9, waiting for transfers between devices, swap(): return lax.ppermute(x, 'feat', [(f, f ^ k) for f in range(FEAT)])  14.4 us
    all_to_all x2, starting transfers between devices, to_dom(): return lax.all_to_all(x, 'dom', split_axis=0, concat_axis=0, tiled=True)  12.7 us
  transfers between devices with their start and end apart: 11, of which 7 were waited for; matrix products, arithmetic and copies ran while one was open for 0% of the time, Pallas kernels for 28%

profile of v6, /device:TPU:0, one launch (start us, length us, event | category | flops | bytes accessed | tf_op | source)
XLA Modules:
  0.0 96.7 jit_solution(2117882884978991892)
XLA Ops:
  0.6 4.8 %gather_rows.1 = bf16[32,3,64,128]{3,2,1,0:T(8,128)(2,1)} custom-call(bf16[64,2048]{1,0:T(8,128)(2,1)} %bitcast.11, s32[32,256]{1,0:T(8,128)} %bitcast.8, bf16[64,128]{1,0:T(8,128)(2,1)} %bitcast.17), custom_call_target="tpu_custom_call" | custom-call | flops 4000000000 | bytes 2097152 | tf_op jit(solution)/shard_map/gather_rows/pallas_call | solution.py:56
  5.4 8.8 %all-to-all-start = ((bf16[32,3,64,128]{3,2,1,0:T(8,128)(2,1)}), bf16[32,3,64,128]{3,2,1,0:T(8,128)(2,1)S(1)}, u32[]{:S(2)}, u32[]{:S(2)}) async-start(bf16[32,3,64,128]{3,2,1,0:T(8,128)(2,1)} %gather_rows.1), calls=%async_computation | async-start | bytes 3145728 | tf_op jit(solution)/shard_map/all_to_all | solution.py:562
  14.2 1.9 %pack.1 = (bf16[160,1024]{1,0:T(8,128)(2,1)}, bf16[160,1024]{1,0:T(8,128)(2,1)}) custom-call(bf16[64,2048]{1,0:T(8,128)(2,1)} %bitcast.12, bf16[64,2048]{1,0:T(8,128)(2,1)} %bitcast.10, bf16[64,256]{1,0:T(8,128)(2,1)} %self_ref.1, bf16[64,256]{1,0:T(8,128)(2,1)} %neigh_ref.1), custom_call_target="tpu_custom_call" | custom-call | bytes 2097152 | tf_op jit(solution)/shard_map/pack/pallas_call | solution.py:56
  16.1 3.6 %collective-permute-start = (bf16[160,1024]{1,0:T(8,128)(2,1)}, bf16[160,1024]{1,0:T(8,128)(2,1)S(1)}, u32[]{:S(2)}, u32[]{:S(2)}) collective-permute-start(bf16[160,1024]{1,0:T(8,128)(2,1)} %get-tuple-element.38), channel_id=1, source_target_pairs={{0,2},{1,3},{2,0},{3,1},{4,6},{5,7},{6,4},{7,5},{8,10},{9,11},{10,... | collective-permute-start | bytes 983048 | tf_op jit(solution)/shard_map/ppermute | solution.py:566
  19.7 6.1 %prepare.1 = (s32[4608,1024]{1,0:T(8,128)}, bf16[576,128,128]{2,1,0:T(8,128)(2,1)}, f32[288,128,64]{2,1,0:T(8,128)}) custom-call(s32[2,96]{1,0:T(2,128)} %bitcast.18, bf16[64,2048]{1,0:T(8,128)(2,1)} %bitcast.13, bf16[96,128,128]{2,1,0:T(8,128)(2,1)} %tile_hbm.1), custom_call_target="tpu_custom_call" | custom-call | flops 1000000000 | bytes 2097152 | tf_op jit(solution)/shard_map/prepare/pallas_call | solution.py:56
  25.9 11.9 %all-to-all-done.recv_ref = bf16[32,3,64,128]{3,2,1,0:T(8,128)(2,1)S(1)} async-done(((bf16[32,3,64,128]{3,2,1,0:T(8,128)(2,1)}), bf16[32,3,64,128]{3,2,1,0:T(8,128)(2,1)S(1)}, u32[]{:S(2)}, u32[]{:S(2)}) %all-to-all-start) | async-done | bytes 1572896 | tf_op jit(solution)/shard_map/all_to_all | solution.py:562
  37.8 5.7 %forward_send.1 = (bf16[64,1024]{1,0:T(8,128)(2,1)S(1)}, f32[8,128,64]{2,1,0:T(8,128)S(1)}, bf16[64,4096]{1,0:T(8,128)(2,1)S(1)}, bf16[2048,4096]{1,0:T(8,128)(2,1)S(1)}) custom-call(s32[4608,1024]{1,0:T(8,128)} %get-tuple-element.36.list_hbm, bf16[32,3,64,128]{3,2,1,0:T(8,128)(2,1)S(1)} %all-to-all-done.recv_ref, ...), custom_call_target="tpu_custom_call" | custom-call | flops 2000000000 | bytes 16777216 | tf_op jit(solution)/shard_map/forward_send/pallas_call | solution.py:56
  43.6 3.7 %collective-permute-start.1 = (bf16[64,1024]{1,0:T(8,128)(2,1)S(1)}, bf16[64,1024]{1,0:T(8,128)(2,1)S(1)}, u32[]{:S(2)}, u32[]{:S(2)}) collective-permute-start(bf16[64,1024]{1,0:T(8,128)(2,1)S(1)} %get-tuple-element.41), channel_id=1, source_target_pairs={{0,2},{1,3},{2,0},{3,1},{4,6},{5,7},{6,4},{7,5},{8,10},{9,11},{10,... | collective-permute-start | bytes 393224 | tf_op jit(solution)/shard_map/ppermute | solution.py:566
  47.2 3.1 %forward_keep.1 = (bf16[64,1024]{1,0:T(8,128)(2,1)S(1)}, bf16[2048,4096]{1,0:T(8,128)(2,1)S(1)}) custom-call(f32[8,128,64]{2,1,0:T(8,128)S(1)} %get-tuple-element.42.sum_ref, bf16[64,4096]{1,0:T(8,128)(2,1)S(1)} %get-tuple-element.43.hubs, bf16[2048,4096]{1,0:T(8,128)(2,1)S(1)} %get-tuple-element.44._, ...), custom_call_target="tpu_custom_call", output_to_operand_aliasing={{1}: (2, {})} | custom-call | flops 1000000000 | bytes 8388608 | tf_op jit(solution)/shard_map/forward_keep/pallas_call | solution.py:56
  50.4 0.6 collective-permute-start.5
  51.0 0.4 collective-permute-start.3
  51.5 0.9 collective-permute-done.2.rest_1_
  52.6 0.9 dense.1
  53.5 3.4 %collective-permute-start.6 = (bf16[64,1024]{1,0:T(8,128)(2,1)S(1)}, bf16[64,1024]{1,0:T(8,128)(2,1)S(1)}, u32[]{:S(2)}, u32[]{:S(2)}) collective-permute-start(bf16[64,1024]{1,0:T(8,128)(2,1)S(1)} %get-tuple-element.51), channel_id=1, source_target_pairs={{0,2},{1,3},{2,0},{3,1},{4,6},{5,7},{6,4},{7,5},{8,10},{9,11},{10,... | collective-permute-start | bytes 393224 | tf_op jit(solution)/shard_map/ppermute | solution.py:566
  56.9 1.7 %hub_backward.1 = (f32[64,4096]{1,0:T(8,128)S(1)}, bf16[64,1024]{1,0:T(8,128)(2,1)S(1)}, bf16[64,1024]{1,0:T(8,128)(2,1)S(1)}) custom-call(bf16[64,1024]{1,0:T(8,128)(2,1)S(1)} %get-tuple-element.59.grad_ref.keep_ref, bf16[256,256]{1,0:T(8,128)(2,1)S(1)} %get-tuple-element.52.self_ref, bf16[256,1024]{1,0:T(8,128)(2,1)S(1)} %get-tuple-element.53.pre_ref, ...), custom_call_target="tpu_custom_call" | custom-call | flops 1000000000 | bytes 8388608 | tf_op jit(solution)/shard_map/hub_backward/pallas_call | solution.py:56
  58.5 0.5 collective-permute-start.7
  59.1 2.0 %collective-permute-done.6.come_ref = bf16[64,1024]{1,0:T(8,128)(2,1)S(1)} collective-permute-done((bf16[64,1024]{1,0:T(8,128)(2,1)S(1)}, bf16[64,1024]{1,0:T(8,128)(2,1)S(1)}, u32[]{:S(2)}, u32[]{:S(2)}) %collective-permute-start.6) | collective-permute-done | bytes 131104 | tf_op jit(solution)/shard_map/ppermute | solution.py:566
  61.1 4.2 %backward.1 = bf16[32,3,64,128]{3,2,1,0:T(8,128)(2,1)} custom-call(s32[4608,1024]{1,0:T(8,128)} %get-tuple-element.36.list_hbm, bf16[64,1024]{1,0:T(8,128)(2,1)S(1)} %get-tuple-element.59.grad_ref.keep_ref, bf16[64,1024]{1,0:T(8,128)(2,1)S(1)} %collective-permute-done.6.come_ref, f32[64,4096]{1,0:T(8,128)S(1)} %get-tuple-element.55.terms_ref, ...), custom_call_target="tpu_custom_call" | custom-call | flops 2000000000 | bytes 8388608 | tf_op jit(solution)/shard_map/backward/pallas_call | solution.py:56
  65.4 4.0 %all-to-all-start.1 = ((bf16[32,3,64,128]{3,2,1,0:T(8,128)(2,1)}), bf16[32,3,64,128]{3,2,1,0:T(8,128)(2,1)S(1)}, u32[]{:S(2)}, u32[]{:S(2)}) async-start(bf16[32,3,64,128]{3,2,1,0:T(8,128)(2,1)} %backward.1), calls=%async_computation.1 | async-start | bytes 3145728 | tf_op jit(solution)/shard_map/all_to_all | solution.py:562
  69.4 3.7 %collective-permute-start.8 = (bf16[64,1024]{1,0:T(8,128)(2,1)S(1)}, bf16[64,1024]{1,0:T(8,128)(2,1)S(1)}, u32[]{:S(2)}, u32[]{:S(2)}) collective-permute-start(bf16[64,1024]{1,0:T(8,128)(2,1)S(1)} %get-tuple-element.63), channel_id=1, source_target_pairs={{0,2},{1,3},{2,0},{3,1},{4,6},{5,7},{6,4},{7,5},{8,10},{9,11},{10,... | collective-permute-start | bytes 393224 | tf_op jit(solution)/shard_map/ppermute | solution.py:566
  73.1 3.9 %own_backward.1.own_hbm = f32[2304,2048]{1,0:T(8,128)} custom-call(s32[4608,1024]{1,0:T(8,128)} %get-tuple-element.36.list_hbm, bf16[64,1024]{1,0:T(8,128)(2,1)} %copy-done, bf16[64,1024]{1,0:T(8,128)(2,1)} %copy-done.1, bf16[576,128,128]{2,1,0:T(8,128)(2,1)} %get-tuple-element.39.tile_hbm), custom_call_target="tpu_custom_call" | custom-call | flops 1000000000 | bytes 2097152 | tf_op jit(solution)/shard_map/own_backward/pallas_call | solution.py:56
  77.0 11.1 %collective-permute-done.8.out_come = bf16[64,1024]{1,0:T(8,128)(2,1)S(1)} collective-permute-done((bf16[64,1024]{1,0:T(8,128)(2,1)S(1)}, bf16[64,1024]{1,0:T(8,128)(2,1)S(1)}, u32[]{:S(2)}, u32[]{:S(2)}) %collective-permute-start.8) | collective-permute-done | bytes 131104 | tf_op jit(solution)/shard_map/ppermute | solution.py:566
  88.1 4.6 %all-to-all-done.1.recv_ref = bf16[32,3,64,128]{3,2,1,0:T(8,128)(2,1)S(1)} async-done(((bf16[32,3,64,128]{3,2,1,0:T(8,128)(2,1)}), bf16[32,3,64,128]{3,2,1,0:T(8,128)(2,1)S(1)}, u32[]{:S(2)}, u32[]{:S(2)}) %all-to-all-start.1) | async-done | bytes 1572896 | tf_op jit(solution)/shard_map/all_to_all | solution.py:562
  92.8 3.7 %scatter_rows.1 = (f32[64,2048]{1,0:T(8,128)}, f32[64,128]{1,0:T(8,128)}, bf16[64,2048]{1,0:T(8,128)(2,1)}) custom-call(s32[32,256]{1,0:T(8,128)S(1)} %bitcast.9, bf16[32,3,64,128]{3,2,1,0:T(8,128)(2,1)S(1)} %all-to-all-done.1.recv_ref, f32[2304,2048]{1,0:T(8,128)} %own_backward.1.own_hbm, bf16[64,1024]{1,0:T(8,128)(2,1)S(1)} %get-tuple-element.60.keep_ref, ...), custom_call_target="tpu_custom_call" | custom-call | flops 1000000000 | bytes 2097152 | tf_op jit(solution)/shard_map/scatter_rows/pallas_call | solution.py:56
  (16 shorter events, 0.4 us)
Async XLA Ops:
  5.4 32.4 %all-to-all-start = ((bf16[32,3,64,128]{3,2,1,0:T(8,128)(2,1)}), bf16[32,3,64,128]{3,2,1,0:T(8,128)(2,1)S(1)}, u32[]{:S(2)}, u32[]{:S(2)}) async-start(bf16[32,3,64,128]{3,2,1,0:T(8,128)(2,1)} %gather_rows.1), calls=%async_computation | async-start | bytes 3145728 | tf_op jit(solution)/shard_map/all_to_all | solution.py:562
  16.1 34.2 %collective-permute-start = (bf16[160,1024]{1,0:T(8,128)(2,1)}, bf16[160,1024]{1,0:T(8,128)(2,1)S(1)}, u32[]{:S(2)}, u32[]{:S(2)}) collective-permute-start(bf16[160,1024]{1,0:T(8,128)(2,1)} %get-tuple-element.38), channel_id=1, source_target_pairs={{0,2},{1,3},{2,0},{3,1},{4,6},{5,7},{6,4},{7,5},{8,10},{9,11},{10,... | collective-permute-start | bytes 983048 | tf_op jit(solution)/shard_map/ppermute | solution.py:566
  37.8 9.4 %copy-start.3 = (bf16[160,1024]{1,0:T(8,128)(2,1)S(1)}, bf16[160,1024]{1,0:T(8,128)(2,1)}, u32[]{:S(2)}) copy-start(bf16[160,1024]{1,0:T(8,128)(2,1)} %get-tuple-element.48.rest_4_) | copy-start | bytes 983044
  43.6 6.8 %collective-permute-start.1 = (bf16[64,1024]{1,0:T(8,128)(2,1)S(1)}, bf16[64,1024]{1,0:T(8,128)(2,1)S(1)}, u32[]{:S(2)}, u32[]{:S(2)}) collective-permute-start(bf16[64,1024]{1,0:T(8,128)(2,1)S(1)} %get-tuple-element.41), channel_id=1, source_target_pairs={{0,2},{1,3},{2,0},{3,1},{4,6},{5,7},{6,4},{7,5},{8,10},{9,11},{10,... | collective-permute-start | bytes 393224 | tf_op jit(solution)/shard_map/ppermute | solution.py:566
  47.2 4.2 %collective-permute-start.4 = (bf16[160,1024]{1,0:T(8,128)(2,1)S(1)}, bf16[160,1024]{1,0:T(8,128)(2,1)S(1)}, u32[]{:S(2)}, u32[]{:S(2)}) collective-permute-start(bf16[160,1024]{1,0:T(8,128)(2,1)S(1)} %copy-done.3), channel_id=1, source_target_pairs={{0,1},{1,0},{2,3},{3,2},{4,5},{5,4},{6,7},{7,6},{8,9},{9,8},{10,11... | collective-permute-start | bytes 983048 | tf_op jit(solution)/shard_map/ppermute | solution.py:566
  50.4 2.2 %collective-permute-start.5 = (bf16[160,1024]{1,0:T(8,128)(2,1)S(1)}, bf16[160,1024]{1,0:T(8,128)(2,1)S(1)}, u32[]{:S(2)}, u32[]{:S(2)}) collective-permute-start(bf16[160,1024]{1,0:T(8,128)(2,1)S(1)} %collective-permute-done.rest_6_), channel_id=1, source_target_pairs={{0,1},{1,0},{2,3},{3,2},{4,5},{5,4},{6,7},{7,6},{8,9},{9,8},{10,11... | collective-permute-start | bytes 983048 | tf_op jit(solution)/shard_map/ppermute | solution.py:566
  51.0 1.4 %collective-permute-start.2 = (bf16[64,1024]{1,0:T(8,128)(2,1)S(1)}, bf16[64,1024]{1,0:T(8,128)(2,1)S(1)}, u32[]{:S(2)}, u32[]{:S(2)}) collective-permute-start(bf16[64,1024]{1,0:T(8,128)(2,1)S(1)} %get-tuple-element.46.rest_0_), channel_id=1, source_target_pairs={{0,1},{1,0},{2,3},{3,2},{4,5},{5,4},{6,7},{7,6},{8,9},{9,8},{10,11... | collective-permute-start | bytes 393224 | tf_op jit(solution)/shard_map/ppermute | solution.py:566
  51.0 1.5 %collective-permute-start.3 = (bf16[64,1024]{1,0:T(8,128)(2,1)S(1)}, bf16[64,1024]{1,0:T(8,128)(2,1)S(1)}, u32[]{:S(2)}, u32[]{:S(2)}) collective-permute-start(bf16[64,1024]{1,0:T(8,128)(2,1)S(1)} %collective-permute-done.1.rest_2_), channel_id=1, source_target_pairs={{0,1},{1,0},{2,3},{3,2},{4,5},{5,4},{6,7},{7,6},{8,9},{9,8},{10,11... | collective-permute-start | bytes 393224 | tf_op jit(solution)/shard_map/ppermute | solution.py:566
  53.5 11.8 %copy-start = (bf16[64,1024]{1,0:T(8,128)(2,1)}, bf16[64,1024]{1,0:T(8,128)(2,1)S(1)}, u32[]{:S(2)}) copy-start(bf16[64,1024]{1,0:T(8,128)(2,1)S(1)} %get-tuple-element.59.grad_ref.keep_ref) | copy-start | bytes 393220
  53.5 7.5 %collective-permute-start.6 = (bf16[64,1024]{1,0:T(8,128)(2,1)S(1)}, bf16[64,1024]{1,0:T(8,128)(2,1)S(1)}, u32[]{:S(2)}, u32[]{:S(2)}) collective-permute-start(bf16[64,1024]{1,0:T(8,128)(2,1)S(1)} %get-tuple-element.51), channel_id=1, source_target_pairs={{0,2},{1,3},{2,0},{3,1},{4,6},{5,7},{6,4},{7,5},{8,10},{9,11},{10,... | collective-permute-start | bytes 393224 | tf_op jit(solution)/shard_map/ppermute | solution.py:566
  58.5 6.9 %collective-permute-start.7 = (bf16[64,1024]{1,0:T(8,128)(2,1)S(1)}, bf16[64,1024]{1,0:T(8,128)(2,1)S(1)}, u32[]{:S(2)}, u32[]{:S(2)}) collective-permute-start(bf16[64,1024]{1,0:T(8,128)(2,1)S(1)} %get-tuple-element.56), channel_id=1, source_target_pairs={{0,2},{1,3},{2,0},{3,1},{4,6},{5,7},{6,4},{7,5},{8,10},{9,11},{10,... | collective-permute-start | bytes 393224 | tf_op jit(solution)/shard_map/ppermute | solution.py:566
  61.0 4.2 %copy-start.1 = (bf16[64,1024]{1,0:T(8,128)(2,1)}, bf16[64,1024]{1,0:T(8,128)(2,1)S(1)}, u32[]{:S(2)}) copy-start(bf16[64,1024]{1,0:T(8,128)(2,1)S(1)} %collective-permute-done.6.come_ref) | copy-start | bytes 393220
  65.4 27.4 %all-to-all-start.1 = ((bf16[32,3,64,128]{3,2,1,0:T(8,128)(2,1)}), bf16[32,3,64,128]{3,2,1,0:T(8,128)(2,1)S(1)}, u32[]{:S(2)}, u32[]{:S(2)}) async-start(bf16[32,3,64,128]{3,2,1,0:T(8,128)(2,1)} %backward.1), calls=%async_computation.1 | async-start | bytes 3145728 | tf_op jit(solution)/shard_map/all_to_all | solution.py:562
  69.4 23.4 %copy-start.2 = (s32[1,32,256]{2,1,0:T(8,128)S(1)}, s32[1,32,256]{2,1,0:T(8,128)}, u32[]{:S(2)}) copy-start(s32[1,32,256]{2,1,0:T(8,128)} %param.14) | copy-start | bytes 98308
  69.4 18.7 %collective-permute-start.8 = (bf16[64,1024]{1,0:T(8,128)(2,1)S(1)}, bf16[64,1024]{1,0:T(8,128)(2,1)S(1)}, u32[]{:S(2)}, u32[]{:S(2)}) collective-permute-start(bf16[64,1024]{1,0:T(8,128)(2,1)S(1)} %get-tuple-element.63), channel_id=1, source_target_pairs={{0,2},{1,3},{2,0},{3,1},{4,6},{5,7},{6,4},{7,5},{8,10},{9,11},{10,... | collective-permute-start | bytes 393224 | tf_op jit(solution)/shard_map/ppermute | solution.py:566

commit v7 on v6

--- a/solution.py
+++ b/solution.py
@@ -203,7 +203,7 @@
 
 
 HUB_STEPS = 4
-KEEP_EARLY = 2
+KEEP_EARLY = 1
 TILE_STEPS = 4
 HALF_ROWS = HALF // HUB_STEPS
 

time: 97.1 us -> 97.7 us (level)
  starting transfers between devices: 28.7 us -> 27.4 us
  waiting for transfers between devices: 31 us -> 32.2 us
    ppermute x9, waiting for transfers between devices: 14.4 us -> 18.1 us  [swap(): return lax.ppermute(x, 'feat', [(f, f ^ k) for f in range(FEAT)])]
    all_to_all x2, waiting for transfers between devices: 16.6 us -> 14.2 us  [to_dom(): return lax.all_to_all(x, 'dom', split_axis=0, concat_axis=0, tiled=True)]
    ppermute x9, starting transfers between devices: 15.9 us -> 14.7 us  [swap(): return lax.ppermute(x, 'feat', [(f, f ^ k) for f in range(FEAT)])]
  transfers between devices with their start and end apart: 11 -> 11, of which waited for: 7 -> 6; matrix products, arithmetic and copies ran while one was open for 0% -> 0% of each run, Pallas kernels for 28% -> 28%
where the time goes in v7:
time: 97.7 us; the launch traced here: 97.2 us
  Pallas kernels  36.6 us (37%)
  waiting for transfers between devices  32.2 us (33%)
  starting transfers between devices  27.4 us (28%)
    pallas_call x10, Pallas kernels, local_call(): pl.pallas_call(kernel, out_shape=outs, in_specs=[places.get(i, VMEM) for...  36.6 us
    ppermute x9, waiting for transfers between devices, swap(): return lax.ppermute(x, 'feat', [(f, f ^ k) for f in range(FEAT)])  18.1 us
    ppermute x9, starting transfers between devices, swap(): return lax.ppermute(x, 'feat', [(f, f ^ k) for f in range(FEAT)])  14.7 us
    all_to_all x2, waiting for transfers between devices, to_dom(): return lax.all_to_all(x, 'dom', split_axis=0, concat_axis=0, tiled=True)  14.2 us
    all_to_all x2, starting transfers between devices, to_dom(): return lax.all_to_all(x, 'dom', split_axis=0, concat_axis=0, tiled=True)  12.8 us
  transfers between devices with their start and end apart: 11, of which 6 were waited for; matrix products, arithmetic and copies ran while one was open for 0% of the time, Pallas kernels for 28%

profile of v7, /device:TPU:0, one launch (start us, length us, event | category | flops | bytes accessed | tf_op | source)
XLA Modules:
  0.0 97.2 jit_solution(7267165213336487016)
XLA Ops:
  0.6 4.8 %gather_rows.1 = bf16[32,3,64,128]{3,2,1,0:T(8,128)(2,1)} custom-call(bf16[64,2048]{1,0:T(8,128)(2,1)} %bitcast.11, s32[32,256]{1,0:T(8,128)} %bitcast.8, bf16[64,128]{1,0:T(8,128)(2,1)} %bitcast.17), custom_call_target="tpu_custom_call" | custom-call | flops 4000000000 | bytes 2097152 | tf_op jit(solution)/shard_map/gather_rows/pallas_call | solution.py:56
  5.4 8.8 %all-to-all-start = ((bf16[32,3,64,128]{3,2,1,0:T(8,128)(2,1)}), bf16[32,3,64,128]{3,2,1,0:T(8,128)(2,1)S(1)}, u32[]{:S(2)}, u32[]{:S(2)}) async-start(bf16[32,3,64,128]{3,2,1,0:T(8,128)(2,1)} %gather_rows.1), calls=%async_computation | async-start | bytes 3145728 | tf_op jit(solution)/shard_map/all_to_all | solution.py:562
  14.2 1.9 %pack.1 = (bf16[160,1024]{1,0:T(8,128)(2,1)}, bf16[160,1024]{1,0:T(8,128)(2,1)}) custom-call(bf16[64,2048]{1,0:T(8,128)(2,1)} %bitcast.12, bf16[64,2048]{1,0:T(8,128)(2,1)} %bitcast.10, bf16[64,256]{1,0:T(8,128)(2,1)} %self_ref.1, bf16[64,256]{1,0:T(8,128)(2,1)} %neigh_ref.1), custom_call_target="tpu_custom_call" | custom-call | bytes 2097152 | tf_op jit(solution)/shard_map/pack/pallas_call | solution.py:56
  16.1 3.6 %collective-permute-start = (bf16[160,1024]{1,0:T(8,128)(2,1)}, bf16[160,1024]{1,0:T(8,128)(2,1)S(1)}, u32[]{:S(2)}, u32[]{:S(2)}) collective-permute-start(bf16[160,1024]{1,0:T(8,128)(2,1)} %get-tuple-element.38), channel_id=1, source_target_pairs={{0,2},{1,3},{2,0},{3,1},{4,6},{5,7},{6,4},{7,5},{8,10},{9,11},{10,... | collective-permute-start | bytes 983048 | tf_op jit(solution)/shard_map/ppermute | solution.py:566
  19.7 6.1 %prepare.1 = (s32[4608,1024]{1,0:T(8,128)}, bf16[576,128,128]{2,1,0:T(8,128)(2,1)}, f32[288,128,64]{2,1,0:T(8,128)}) custom-call(s32[2,96]{1,0:T(2,128)} %bitcast.18, bf16[64,2048]{1,0:T(8,128)(2,1)} %bitcast.13, bf16[96,128,128]{2,1,0:T(8,128)(2,1)} %tile_hbm.1), custom_call_target="tpu_custom_call" | custom-call | flops 1000000000 | bytes 2097152 | tf_op jit(solution)/shard_map/prepare/pallas_call | solution.py:56
  25.9 11.9 %all-to-all-done.recv_ref = bf16[32,3,64,128]{3,2,1,0:T(8,128)(2,1)S(1)} async-done(((bf16[32,3,64,128]{3,2,1,0:T(8,128)(2,1)}), bf16[32,3,64,128]{3,2,1,0:T(8,128)(2,1)S(1)}, u32[]{:S(2)}, u32[]{:S(2)}) %all-to-all-start) | async-done | bytes 1572896 | tf_op jit(solution)/shard_map/all_to_all | solution.py:562
  37.8 5.6 %forward_send.1 = (bf16[64,1024]{1,0:T(8,128)(2,1)S(1)}, f32[8,128,64]{2,1,0:T(8,128)S(1)}, bf16[64,4096]{1,0:T(8,128)(2,1)S(1)}, bf16[2048,4096]{1,0:T(8,128)(2,1)S(1)}) custom-call(s32[4608,1024]{1,0:T(8,128)} %get-tuple-element.36.list_hbm, bf16[32,3,64,128]{3,2,1,0:T(8,128)(2,1)S(1)} %all-to-all-done.recv_ref, ...), custom_call_target="tpu_custom_call" | custom-call | flops 2000000000 | bytes 16777216 | tf_op jit(solution)/shard_map/forward_send/pallas_call | solution.py:56
  43.4 3.7 %collective-permute-start.1 = (bf16[64,1024]{1,0:T(8,128)(2,1)S(1)}, bf16[64,1024]{1,0:T(8,128)(2,1)S(1)}, u32[]{:S(2)}, u32[]{:S(2)}) collective-permute-start(bf16[64,1024]{1,0:T(8,128)(2,1)S(1)} %get-tuple-element.41), channel_id=1, source_target_pairs={{0,2},{1,3},{2,0},{3,1},{4,6},{5,7},{6,4},{7,5},{8,10},{9,11},{10,... | collective-permute-start | bytes 393224 | tf_op jit(solution)/shard_map/ppermute | solution.py:566
  47.1 3.8 %forward_keep.1 = (bf16[64,1024]{1,0:T(8,128)(2,1)S(1)}, bf16[2048,4096]{1,0:T(8,128)(2,1)S(1)}) custom-call(f32[8,128,64]{2,1,0:T(8,128)S(1)} %get-tuple-element.42.sum_ref, bf16[64,4096]{1,0:T(8,128)(2,1)S(1)} %get-tuple-element.43.hubs, bf16[2048,4096]{1,0:T(8,128)(2,1)S(1)} %get-tuple-element.44._, ...), custom_call_target="tpu_custom_call", output_to_operand_aliasing={{1}: (2, {})} | custom-call | flops 1000000000 | bytes 8388608 | tf_op jit(solution)/shard_map/forward_keep/pallas_call | solution.py:56
  50.9 0.6 collective-permute-start.5
  51.6 0.4 collective-permute-start.3
  52.0 0.9 collective-permute-done.2.rest_1_
  53.2 0.9 dense.1
  54.1 2.7 %collective-permute-start.6 = (bf16[64,1024]{1,0:T(8,128)(2,1)S(1)}, bf16[64,1024]{1,0:T(8,128)(2,1)S(1)}, u32[]{:S(2)}, u32[]{:S(2)}) collective-permute-start(bf16[64,1024]{1,0:T(8,128)(2,1)S(1)} %get-tuple-element.51), channel_id=1, source_target_pairs={{0,2},{1,3},{2,0},{3,1},{4,6},{5,7},{6,4},{7,5},{8,10},{9,11},{10,... | collective-permute-start | bytes 393224 | tf_op jit(solution)/shard_map/ppermute | solution.py:566
  56.8 1.6 %hub_backward.1 = (f32[64,4096]{1,0:T(8,128)S(1)}, bf16[64,1024]{1,0:T(8,128)(2,1)S(1)}, bf16[64,1024]{1,0:T(8,128)(2,1)S(1)}) custom-call(bf16[64,1024]{1,0:T(8,128)(2,1)S(1)} %get-tuple-element.59.grad_ref.keep_ref, bf16[256,256]{1,0:T(8,128)(2,1)S(1)} %get-tuple-element.52.self_ref, bf16[256,1024]{1,0:T(8,128)(2,1)S(1)} %get-tuple-element.53.pre_ref, ...), custom_call_target="tpu_custom_call" | custom-call | flops 1000000000 | bytes 8388608 | tf_op jit(solution)/shard_map/hub_backward/pallas_call | solution.py:56
  58.4 1.2 %collective-permute-start.7 = (bf16[64,1024]{1,0:T(8,128)(2,1)S(1)}, bf16[64,1024]{1,0:T(8,128)(2,1)S(1)}, u32[]{:S(2)}, u32[]{:S(2)}) collective-permute-start(bf16[64,1024]{1,0:T(8,128)(2,1)S(1)} %get-tuple-element.56), channel_id=1, source_target_pairs={{0,2},{1,3},{2,0},{3,1},{4,6},{5,7},{6,4},{7,5},{8,10},{9,11},{10,... | collective-permute-start | bytes 393224 | tf_op jit(solution)/shard_map/ppermute | solution.py:566
  59.6 2.0 %collective-permute-done.6.come_ref = bf16[64,1024]{1,0:T(8,128)(2,1)S(1)} collective-permute-done((bf16[64,1024]{1,0:T(8,128)(2,1)S(1)}, bf16[64,1024]{1,0:T(8,128)(2,1)S(1)}, u32[]{:S(2)}, u32[]{:S(2)}) %collective-permute-start.6) | collective-permute-done | bytes 131104 | tf_op jit(solution)/shard_map/ppermute | solution.py:566
  61.6 4.2 %backward.1 = bf16[32,3,64,128]{3,2,1,0:T(8,128)(2,1)} custom-call(s32[4608,1024]{1,0:T(8,128)} %get-tuple-element.36.list_hbm, bf16[64,1024]{1,0:T(8,128)(2,1)S(1)} %get-tuple-element.59.grad_ref.keep_ref, bf16[64,1024]{1,0:T(8,128)(2,1)S(1)} %collective-permute-done.6.come_ref, f32[64,4096]{1,0:T(8,128)S(1)} %get-tuple-element.55.terms_ref, ...), custom_call_target="tpu_custom_call" | custom-call | flops 2000000000 | bytes 8388608 | tf_op jit(solution)/shard_map/backward/pallas_call | solution.py:56
  65.9 4.0 %all-to-all-start.1 = ((bf16[32,3,64,128]{3,2,1,0:T(8,128)(2,1)}), bf16[32,3,64,128]{3,2,1,0:T(8,128)(2,1)S(1)}, u32[]{:S(2)}, u32[]{:S(2)}) async-start(bf16[32,3,64,128]{3,2,1,0:T(8,128)(2,1)} %backward.1), calls=%async_computation.1 | async-start | bytes 3145728 | tf_op jit(solution)/shard_map/all_to_all | solution.py:562
  69.9 2.4 %collective-permute-start.8 = (bf16[64,1024]{1,0:T(8,128)(2,1)S(1)}, bf16[64,1024]{1,0:T(8,128)(2,1)S(1)}, u32[]{:S(2)}, u32[]{:S(2)}) collective-permute-start(bf16[64,1024]{1,0:T(8,128)(2,1)S(1)} %get-tuple-element.63), channel_id=1, source_target_pairs={{0,2},{1,3},{2,0},{3,1},{4,6},{5,7},{6,4},{7,5},{8,10},{9,11},{10,... | collective-permute-start | bytes 393224 | tf_op jit(solution)/shard_map/ppermute | solution.py:566
  72.3 3.9 %own_backward.1.own_hbm = f32[2304,2048]{1,0:T(8,128)} custom-call(s32[4608,1024]{1,0:T(8,128)} %get-tuple-element.36.list_hbm, bf16[64,1024]{1,0:T(8,128)(2,1)} %copy-done, bf16[64,1024]{1,0:T(8,128)(2,1)} %copy-done.1, bf16[576,128,128]{2,1,0:T(8,128)(2,1)} %get-tuple-element.39.tile_hbm), custom_call_target="tpu_custom_call" | custom-call | flops 1000000000 | bytes 2097152 | tf_op jit(solution)/shard_map/own_backward/pallas_call | solution.py:56
  76.2 14.9 %collective-permute-done.8.out_come = bf16[64,1024]{1,0:T(8,128)(2,1)S(1)} collective-permute-done((bf16[64,1024]{1,0:T(8,128)(2,1)S(1)}, bf16[64,1024]{1,0:T(8,128)(2,1)S(1)}, u32[]{:S(2)}, u32[]{:S(2)}) %collective-permute-start.8) | collective-permute-done | bytes 131104 | tf_op jit(solution)/shard_map/ppermute | solution.py:566
  91.2 2.2 %all-to-all-done.1.recv_ref = bf16[32,3,64,128]{3,2,1,0:T(8,128)(2,1)S(1)} async-done(((bf16[32,3,64,128]{3,2,1,0:T(8,128)(2,1)}), bf16[32,3,64,128]{3,2,1,0:T(8,128)(2,1)S(1)}, u32[]{:S(2)}, u32[]{:S(2)}) %all-to-all-start.1) | async-done | bytes 1572896 | tf_op jit(solution)/shard_map/all_to_all | solution.py:562
  93.4 3.7 %scatter_rows.1 = (f32[64,2048]{1,0:T(8,128)}, f32[64,128]{1,0:T(8,128)}, bf16[64,2048]{1,0:T(8,128)(2,1)}) custom-call(s32[32,256]{1,0:T(8,128)S(1)} %bitcast.9, bf16[32,3,64,128]{3,2,1,0:T(8,128)(2,1)S(1)} %all-to-all-done.1.recv_ref, f32[2304,2048]{1,0:T(8,128)} %own_backward.1.own_hbm, bf16[64,1024]{1,0:T(8,128)(2,1)S(1)} %get-tuple-element.60.keep_ref, ...), custom_call_target="tpu_custom_call" | custom-call | flops 1000000000 | bytes 2097152 | tf_op jit(solution)/shard_map/scatter_rows/pallas_call | solution.py:56
  (16 shorter events, 0.3 us)
Async XLA Ops:
  5.4 32.4 %all-to-all-start = ((bf16[32,3,64,128]{3,2,1,0:T(8,128)(2,1)}), bf16[32,3,64,128]{3,2,1,0:T(8,128)(2,1)S(1)}, u32[]{:S(2)}, u32[]{:S(2)}) async-start(bf16[32,3,64,128]{3,2,1,0:T(8,128)(2,1)} %gather_rows.1), calls=%async_computation | async-start | bytes 3145728 | tf_op jit(solution)/shard_map/all_to_all | solution.py:562
  16.1 34.8 %collective-permute-start = (bf16[160,1024]{1,0:T(8,128)(2,1)}, bf16[160,1024]{1,0:T(8,128)(2,1)S(1)}, u32[]{:S(2)}, u32[]{:S(2)}) collective-permute-start(bf16[160,1024]{1,0:T(8,128)(2,1)} %get-tuple-element.38), channel_id=1, source_target_pairs={{0,2},{1,3},{2,0},{3,1},{4,6},{5,7},{6,4},{7,5},{8,10},{9,11},{10,... | collective-permute-start | bytes 983048 | tf_op jit(solution)/shard_map/ppermute | solution.py:566
  37.8 9.3 %copy-start.3 = (bf16[160,1024]{1,0:T(8,128)(2,1)S(1)}, bf16[160,1024]{1,0:T(8,128)(2,1)}, u32[]{:S(2)}) copy-start(bf16[160,1024]{1,0:T(8,128)(2,1)} %get-tuple-element.48.rest_4_) | copy-start | bytes 983044
  43.4 7.5 %collective-permute-start.1 = (bf16[64,1024]{1,0:T(8,128)(2,1)S(1)}, bf16[64,1024]{1,0:T(8,128)(2,1)S(1)}, u32[]{:S(2)}, u32[]{:S(2)}) collective-permute-start(bf16[64,1024]{1,0:T(8,128)(2,1)S(1)} %get-tuple-element.41), channel_id=1, source_target_pairs={{0,2},{1,3},{2,0},{3,1},{4,6},{5,7},{6,4},{7,5},{8,10},{9,11},{10,... | collective-permute-start | bytes 393224 | tf_op jit(solution)/shard_map/ppermute | solution.py:566
  47.1 4.9 %collective-permute-start.4 = (bf16[160,1024]{1,0:T(8,128)(2,1)S(1)}, bf16[160,1024]{1,0:T(8,128)(2,1)S(1)}, u32[]{:S(2)}, u32[]{:S(2)}) collective-permute-start(bf16[160,1024]{1,0:T(8,128)(2,1)S(1)} %copy-done.3), channel_id=1, source_target_pairs={{0,1},{1,0},{2,3},{3,2},{4,5},{5,4},{6,7},{7,6},{8,9},{9,8},{10,11... | collective-permute-start | bytes 983048 | tf_op jit(solution)/shard_map/ppermute | solution.py:566
  50.9 2.2 %collective-permute-start.5 = (bf16[160,1024]{1,0:T(8,128)(2,1)S(1)}, bf16[160,1024]{1,0:T(8,128)(2,1)S(1)}, u32[]{:S(2)}, u32[]{:S(2)}) collective-permute-start(bf16[160,1024]{1,0:T(8,128)(2,1)S(1)} %collective-permute-done.rest_6_), channel_id=1, source_target_pairs={{0,1},{1,0},{2,3},{3,2},{4,5},{5,4},{6,7},{7,6},{8,9},{9,8},{10,11... | collective-permute-start | bytes 983048 | tf_op jit(solution)/shard_map/ppermute | solution.py:566
  51.5 1.4 %collective-permute-start.2 = (bf16[64,1024]{1,0:T(8,128)(2,1)S(1)}, bf16[64,1024]{1,0:T(8,128)(2,1)S(1)}, u32[]{:S(2)}, u32[]{:S(2)}) collective-permute-start(bf16[64,1024]{1,0:T(8,128)(2,1)S(1)} %get-tuple-element.46.rest_0_), channel_id=1, source_target_pairs={{0,1},{1,0},{2,3},{3,2},{4,5},{5,4},{6,7},{7,6},{8,9},{9,8},{10,11... | collective-permute-start | bytes 393224 | tf_op jit(solution)/shard_map/ppermute | solution.py:566
  51.6 1.5 %collective-permute-start.3 = (bf16[64,1024]{1,0:T(8,128)(2,1)S(1)}, bf16[64,1024]{1,0:T(8,128)(2,1)S(1)}, u32[]{:S(2)}, u32[]{:S(2)}) collective-permute-start(bf16[64,1024]{1,0:T(8,128)(2,1)S(1)} %collective-permute-done.1.rest_2_), channel_id=1, source_target_pairs={{0,1},{1,0},{2,3},{3,2},{4,5},{5,4},{6,7},{7,6},{8,9},{9,8},{10,11... | collective-permute-start | bytes 393224 | tf_op jit(solution)/shard_map/ppermute | solution.py:566
  54.1 11.8 %copy-start = (bf16[64,1024]{1,0:T(8,128)(2,1)}, bf16[64,1024]{1,0:T(8,128)(2,1)S(1)}, u32[]{:S(2)}) copy-start(bf16[64,1024]{1,0:T(8,128)(2,1)S(1)} %get-tuple-element.59.grad_ref.keep_ref) | copy-start | bytes 393220
  54.1 7.5 %collective-permute-start.6 = (bf16[64,1024]{1,0:T(8,128)(2,1)S(1)}, bf16[64,1024]{1,0:T(8,128)(2,1)S(1)}, u32[]{:S(2)}, u32[]{:S(2)}) collective-permute-start(bf16[64,1024]{1,0:T(8,128)(2,1)S(1)} %get-tuple-element.51), channel_id=1, source_target_pairs={{0,2},{1,3},{2,0},{3,1},{4,6},{5,7},{6,4},{7,5},{8,10},{9,11},{10,... | collective-permute-start | bytes 393224 | tf_op jit(solution)/shard_map/ppermute | solution.py:566
  58.4 7.5 %collective-permute-start.7 = (bf16[64,1024]{1,0:T(8,128)(2,1)S(1)}, bf16[64,1024]{1,0:T(8,128)(2,1)S(1)}, u32[]{:S(2)}, u32[]{:S(2)}) collective-permute-start(bf16[64,1024]{1,0:T(8,128)(2,1)S(1)} %get-tuple-element.56), channel_id=1, source_target_pairs={{0,2},{1,3},{2,0},{3,1},{4,6},{5,7},{6,4},{7,5},{8,10},{9,11},{10,... | collective-permute-start | bytes 393224 | tf_op jit(solution)/shard_map/ppermute | solution.py:566
  61.6 4.2 %copy-start.1 = (bf16[64,1024]{1,0:T(8,128)(2,1)}, bf16[64,1024]{1,0:T(8,128)(2,1)S(1)}, u32[]{:S(2)}) copy-start(bf16[64,1024]{1,0:T(8,128)(2,1)S(1)} %collective-permute-done.6.come_ref) | copy-start | bytes 393220
  65.9 27.5 %all-to-all-start.1 = ((bf16[32,3,64,128]{3,2,1,0:T(8,128)(2,1)}), bf16[32,3,64,128]{3,2,1,0:T(8,128)(2,1)S(1)}, u32[]{:S(2)}, u32[]{:S(2)}) async-start(bf16[32,3,64,128]{3,2,1,0:T(8,128)(2,1)} %backward.1), calls=%async_computation.1 | async-start | bytes 3145728 | tf_op jit(solution)/shard_map/all_to_all | solution.py:562
  69.9 23.5 %copy-start.2 = (s32[1,32,256]{2,1,0:T(8,128)S(1)}, s32[1,32,256]{2,1,0:T(8,128)}, u32[]{:S(2)}) copy-start(s32[1,32,256]{2,1,0:T(8,128)} %param.14) | copy-start | bytes 98308
  69.9 21.3 %collective-permute-start.8 = (bf16[64,1024]{1,0:T(8,128)(2,1)S(1)}, bf16[64,1024]{1,0:T(8,128)(2,1)S(1)}, u32[]{:S(2)}, u32[]{:S(2)}) collective-permute-start(bf16[64,1024]{1,0:T(8,128)(2,1)S(1)} %get-tuple-element.63), channel_id=1, source_target_pairs={{0,2},{1,3},{2,0},{3,1},{4,6},{5,7},{6,4},{7,5},{8,10},{9,11},{10,... | collective-permute-start | bytes 393224 | tf_op jit(solution)/shard_map/ppermute | solution.py:566
